TPU v7x, 32 devices: a whole 2x2x4 slice. The times are simulated.
32 devices in a mesh: section: 2 (over core), row: 4 (over y, x), col: 4 (over z).
Axes of the slice: x: 2, y: 2, z: 4, core: 2. Of those that a mesh axis runs over, the one named last changes fastest.
Arguments:
- tokens: bfloat16 [3, 1536, 1024], P(None, 'col', 'row'), may hold values from -6 to 6
- cotangent: bfloat16 [3, 1536, 1024], P(None, 'col', 'row'), may hold values from -6 to 6
- block_order: int32 [3, 24], replicated, may hold values from 0 to 23, each once within a row
- lengths: int32 [3, 4], replicated, may hold values from 1 to 12, 24 in all within a row
- decay: float32 [2, 3, 24, 8], P('section', None, 'col', 'row'), may hold values from 0 to 1
- write_gate: float32 [2, 3, 1536, 8], P('section', None, 'col', 'row'), may hold values from 0.1 to 1
- gain_attn: bfloat16 [2, 1024], P('section', ('row', 'col')), may hold values from 0.5 to 1.5
- w_query: bfloat16 [2, 1024, 1024], P('section', 'col', 'row'), may hold values from -0.1875 to 0.1875
- w_key: bfloat16 [2, 1024, 1024], P('section', 'col', 'row'), may hold values from -0.1875 to 0.1875
- w_value: bfloat16 [2, 1024, 1024], P('section', 'col', 'row'), may hold values from -0.1875 to 0.1875
- persist_key: bfloat16 [2, 16, 1024], P('section', 'col', 'row'), may hold values from -6 to 6
- persist_value: bfloat16 [2, 16, 1024], P('section', 'col', 'row'), may hold values from -6 to 6
- w_output: bfloat16 [2, 1024, 1024], P('section', 'row', 'col'), may hold values from -0.75 to 0.75
- gain_ffn: bfloat16 [2, 1024], P('section', ('row', 'col')), may hold values from 0.5 to 1.5
- w_gate: bfloat16 [2, 1024, 2816], P('section', 'col', 'row'), may hold values from -0.1875 to 0.1875
- w_up: bfloat16 [2, 1024, 2816], P('section', 'col', 'row'), may hold values from -0.1875 to 0.1875
- w_down: bfloat16 [2, 2816, 1024], P('section', 'row', 'col'), may hold values from -0.21875 to 0.21875
Outputs:
- activations: bfloat16 [2, 3, 1536, 1024], P('section', None, 'col', 'row')
- input_grads: bfloat16 [2, 3, 1536, 1024], P('section', None, 'col', 'row')
- grad_gain_attn: float32 [2, 1024], P('section', ('row', 'col'))
- grad_query: float32 [2, 1024, 1024], P('section', 'col', 'row')
- grad_key: float32 [2, 1024, 1024], P('section', 'col', 'row')
- grad_value: float32 [2, 1024, 1024], P('section', 'col', 'row')
- grad_pkey: float32 [2, 16, 1024], P('section', 'col', 'row')
- grad_pvalue: float32 [2, 16, 1024], P('section', 'col', 'row')
- grad_output: float32 [2, 1024, 1024], P('section', 'row', 'col')
- grad_gain_ffn: float32 [2, 1024], P('section', ('row', 'col'))
- grad_gate: float32 [2, 1024, 2816], P('section', 'col', 'row')
- grad_up: float32 [2, 1024, 2816], P('section', 'col', 'row')
- grad_down: float32 [2, 2816, 1024], P('section', 'row', 'col')
Inputs may be any that keep to these rules, and one draw needn't show every extreme that they name: Each row block_order[m] is a permutation of the 24 block numbers. lengths[m] lists, in blocks of 64 tokens, the lengths of the 4 sequences of micro-batch m laid end to end in dealt order; for each micro-batch they sum to 24, and the longest has exactly 12 blocks.
All inputs are finite; a program needn't handle non-finite values.
Results may differ from a plain program's by a relative error of at most 0.033.
Values may be sent and summed in bfloat16 or wider, within the bound.
A program may use at most 192 MiB of HBM per device.

v0:
```python
import jax
import jax.numpy as jnp
from jax import lax
from jax.sharding import PartitionSpec as P

BLOCK = 64


epsilon = 1e-06
highest = lax.Precision.HIGHEST


def prefix(value, axis, join, neutral, backward):
    count = lax.axis_size(axis)
    place = lax.axis_index(axis)
    ahead = count - 1 - place if backward else place
    gathered = jax.tree.map(
        lambda a, kind: lax.all_gather(a.astype(kind), axis), value, (jnp.bfloat16, jnp.bfloat16)
    )
    state = jax.tree.map(lambda a, e: jnp.zeros_like(a) + jnp.asarray(e, a.dtype), value, neutral)

    def one(lap, state):
        source = count - 1 - lap if backward else lap
        return join(
            state,
            jax.tree.map(
                lambda a, own: lax.dynamic_index_in_dim(a, source, 0, False).astype(own.dtype),
                gathered,
                value,
            ),
        )

    return lax.fori_loop(0, ahead, one, state)


def from_behind(value, axis, by):
    peers = lax.axis_size(axis)
    pairs = [(i, i + by) for i in range(peers) if 0 <= i + by < peers]
    return lax.ppermute(value, axis, pairs)


def fetch_weights(shards):
    gathered = (
        lax.all_gather(shards[0], "col", axis=1, tiled=True),
        lax.all_gather(shards[1], "col", axis=1, tiled=True),
        lax.all_gather(shards[2], "col", axis=1, tiled=True),
        lax.all_gather(shards[3], "col", axis=1, tiled=True),
        lax.all_gather(shards[4], "col", axis=1, tiled=True),
        lax.all_gather(shards[5], "col", axis=1, tiled=True),
        lax.all_gather(shards[6], "col", axis=2, tiled=True),
        lax.all_gather(shards[7], "col", axis=1, tiled=True),
        lax.all_gather(shards[8], "col", axis=1, tiled=True),
        lax.all_gather(shards[9], "col", axis=1, tiled=True),
        lax.all_gather(shards[10], "col", axis=2, tiled=True),
    )
    weights = tuple((member[0] for member in gathered))
    columns = None
    return (weights, columns)


def regroup(pair, picks):
    whole = (
        lax.all_gather(pair[0], "col", axis=1, tiled=True),
        lax.all_gather(pair[1], "col", axis=1, tiled=True),
    )

    def select(full):
        micro_count, row_count, feat_count = full.shape
        blocks = full.reshape(micro_count, row_count // BLOCK, BLOCK, feat_count)
        chosen = jnp.take_along_axis(blocks, picks[:, :, None, None], axis=1)
        return chosen.reshape(micro_count, -1, feat_count)

    return tuple((select(member) for member in whole))


def norm_forward(residual, gain):
    sq_total = lax.psum(jnp.sum(residual * residual, axis=1), "row")
    full_width = residual.shape[1] * lax.axis_size("row")
    inv_rms = lax.rsqrt(sq_total / full_width + epsilon)
    return (residual * inv_rms[:, None] * gain, inv_rms)


def norm_reverse(residual, inv_rms, gain, grad_normed):
    weighted = grad_normed * gain
    cross_sum = lax.psum(jnp.sum(weighted * residual, axis=1), "row")
    full_width = residual.shape[1] * lax.axis_size("row")
    grad_resid = (
        inv_rms[:, None] * weighted - residual * (inv_rms**3 * cross_sum / full_width)[:, None]
    )
    grad_gain = jnp.sum(grad_normed * residual * inv_rms[:, None], axis=0)
    return (grad_resid, grad_gain)


def spread_features(local_rows):
    return lax.all_gather(local_rows, "row", axis=1, tiled=True)


def collect_partial(partial_rows):
    return lax.psum_scatter(
        partial_rows.astype(jnp.bfloat16), "row", scatter_dimension=1, tiled=True
    ).astype(jnp.float32)


def spread_grads(local_rows):
    return lax.all_gather(local_rows, "row", axis=1, tiled=True)


def collect_grads(partial_rows):
    return lax.psum_scatter(
        partial_rows.astype(jnp.bfloat16), "row", scatter_dimension=1, tiled=True
    ).astype(jnp.float32)


def chain_combine(earlier, later_pair):
    return (earlier[0] * later_pair[0], later_pair[0][:, None, None] * earlier[1] + later_pair[1])


def split_blocks(values, head_count):
    row_count, feat_count = values.shape
    return values.reshape(row_count // BLOCK, BLOCK, head_count, feat_count // head_count)


def mixer_forward(queries, keys_loc, values_loc, gate_rows, keep_rows, persist_key, persist_value):
    head_count = gate_rows.shape[1]
    head_size = queries.shape[1] // head_count
    score_scale = head_size ** (-0.5)
    query_blk = split_blocks(queries, head_count)
    key_blk = split_blocks(keys_loc, head_count)
    value_blk = split_blocks(values_loc, head_count)
    block_count = query_blk.shape[0]
    persist_keys = persist_key.reshape(-1, head_count, head_size)
    persist_values = persist_value.reshape(-1, head_count, head_size)
    persist_count = persist_keys.shape[0]
    inner_scores = (
        jnp.einsum("cihd,cjhd->chij", query_blk, key_blk, preferred_element_type=jnp.float32)
        * score_scale
    )
    outer_scores = (
        jnp.einsum("cihd,phd->chip", query_blk, persist_keys, preferred_element_type=jnp.float32)
        * score_scale
    )
    causal = jnp.arange(BLOCK)[:, None] >= jnp.arange(BLOCK)[None, :]
    inner_scores = jnp.where(causal, inner_scores, -1e30)
    scores = jnp.concatenate([outer_scores, inner_scores], axis=-1)
    row_max = jnp.max(scores, axis=-1, keepdims=True)
    expo_terms = jnp.exp(scores - row_max)
    softmax_p = expo_terms / jnp.sum(expo_terms, axis=-1, keepdims=True)
    weights = softmax_p.astype(jnp.bfloat16)
    attended = jnp.einsum(
        "chip,phd->cihd",
        weights[..., :persist_count],
        persist_values,
        preferred_element_type=jnp.float32,
    )
    attended = attended + jnp.einsum(
        "chij,cjhd->cihd",
        weights[..., persist_count:],
        value_blk,
        preferred_element_type=jnp.float32,
    )
    gate_blk = gate_rows.reshape(block_count, BLOCK, head_count)
    scaled_keys = key_blk.astype(jnp.float32) * (gate_blk / BLOCK)[..., None]
    update = jnp.einsum(
        "cthd,cthe->chde", scaled_keys, value_blk.astype(jnp.float32), precision=highest
    )
    zero_state = jnp.zeros((head_count, head_size, head_size), jnp.float32)

    def chain_step(state_acc, step_item):
        update_c, keep_c = step_item
        state_acc = keep_c[:, None, None] * state_acc + update_c
        return (state_acc, state_acc)

    _, local_after = lax.scan(chain_step, zero_state, (update, keep_rows))
    through = jnp.prod(keep_rows, axis=0)
    _, before_state = prefix(
        (through, local_after[-1]),
        "col",
        chain_combine,
        (jnp.ones_like(through), zero_state),
        False,
    )
    after_state = local_after + jnp.cumprod(keep_rows, axis=0)[..., None, None] * before_state[None]
    prior_state = jnp.concatenate([before_state[None], after_state[:-1]], axis=0)
    states = keep_rows[..., None, None] * prior_state
    mem_read = (
        jnp.einsum("cihd,chde->cihe", query_blk.astype(jnp.float32), states, precision=highest)
        * score_scale
    )
    mixed_out = (attended + mem_read).reshape(queries.shape)
    return (mixed_out, softmax_p, states)


def mixer_back(
    queries,
    keys_loc,
    values_loc,
    gate_rows,
    keep_rows,
    persist_key,
    persist_value,
    softmax_p,
    states,
    grad_mixed,
):
    head_count = gate_rows.shape[1]
    head_size = queries.shape[1] // head_count
    score_scale = head_size ** (-0.5)
    query_blk = split_blocks(queries, head_count)
    key_blk = split_blocks(keys_loc, head_count)
    value_blk = split_blocks(values_loc, head_count)
    grad_blk = split_blocks(grad_mixed, head_count)
    block_count = query_blk.shape[0]
    persist_keys = persist_key.reshape(-1, head_count, head_size)
    persist_values = persist_value.reshape(-1, head_count, head_size)
    persist_count = persist_keys.shape[0]
    weights = softmax_p.astype(jnp.bfloat16)
    grad_weights = jnp.concatenate(
        [
            jnp.einsum(
                "cihd,phd->chip", grad_blk, persist_values, preferred_element_type=jnp.float32
            ),
            jnp.einsum("cihd,cjhd->chij", grad_blk, value_blk, preferred_element_type=jnp.float32),
        ],
        axis=-1,
    )
    centre = jnp.sum(softmax_p * grad_weights, axis=-1, keepdims=True)
    grad_scores = (softmax_p * (grad_weights - centre)).astype(jnp.bfloat16)
    grad_outer = grad_scores[..., :persist_count]
    grad_inner = grad_scores[..., persist_count:]
    grad_pvalue = jnp.einsum(
        "chip,cihd->phd", weights[..., :persist_count], grad_blk, preferred_element_type=jnp.float32
    )
    grad_value = jnp.einsum(
        "chij,cihd->cjhd",
        weights[..., persist_count:],
        grad_blk,
        preferred_element_type=jnp.float32,
    )
    grad_query = jnp.einsum(
        "chip,phd->cihd", grad_outer, persist_keys, preferred_element_type=jnp.float32
    )
    grad_query = (
        grad_query
        + jnp.einsum("chij,cjhd->cihd", grad_inner, key_blk, preferred_element_type=jnp.float32)
    ) * score_scale
    grad_key = (
        jnp.einsum("chij,cihd->cjhd", grad_inner, query_blk, preferred_element_type=jnp.float32)
        * score_scale
    )
    grad_pkey = (
        jnp.einsum("chip,cihd->phd", grad_outer, query_blk, preferred_element_type=jnp.float32)
        * score_scale
    )
    grad_float = grad_blk.astype(jnp.float32)
    query_float = query_blk.astype(jnp.float32)
    grad_query = (
        grad_query
        + jnp.einsum("cihe,chde->cihd", grad_float, states, precision=highest) * score_scale
    )
    grad_states = (
        jnp.einsum("cihd,cihe->chde", query_float, grad_float, precision=highest) * score_scale
    )
    zero_state = jnp.zeros((head_count, head_size, head_size), jnp.float32)

    def back_step(state_acc, step_item):
        grad_c, keep_c = step_item
        return (keep_c[:, None, None] * (grad_c + state_acc), state_acc)

    leaving, local_grads = lax.scan(back_step, zero_state, (grad_states, keep_rows), reverse=True)
    through = jnp.prod(keep_rows, axis=0)
    _, from_above = prefix(
        (through, leaving), "col", chain_combine, (jnp.ones_like(through), zero_state), True
    )
    suffix_prod = jnp.cumprod(keep_rows[::-1], axis=0)[::-1]
    later_prod = jnp.concatenate([suffix_prod[1:], jnp.ones_like(suffix_prod[:1])], axis=0)
    carried = local_grads + later_prod[..., None, None] * from_above[None]
    gate_blk = gate_rows.reshape(block_count, BLOCK, head_count)
    scaled_keys = key_blk.astype(jnp.float32) * (gate_blk / BLOCK)[..., None]
    grad_key = grad_key + (gate_blk / BLOCK)[..., None] * jnp.einsum(
        "cthe,chde->cthd", value_blk.astype(jnp.float32), carried, precision=highest
    )
    grad_value = grad_value + jnp.einsum("cthd,chde->cthe", scaled_keys, carried, precision=highest)
    flat_shape = queries.shape
    return (
        grad_query.reshape(flat_shape).astype(jnp.bfloat16),
        grad_key.reshape(flat_shape).astype(jnp.bfloat16),
        grad_value.reshape(flat_shape).astype(jnp.bfloat16),
        grad_pkey.reshape(persist_count, -1),
        grad_pvalue.reshape(persist_count, -1),
    )


def layer_forward(layer_in, weights, gate_rows, keep_rows, with_output):
    (
        gain_attn,
        w_query,
        w_key,
        w_value,
        persist_key,
        persist_value,
        w_output,
        gain_ffn,
        w_gate,
        w_up,
        w_down,
    ) = weights
    residual = layer_in.astype(jnp.float32)
    normed, inv_attn = norm_forward(residual, gain_attn.astype(jnp.float32))
    attn_in = spread_features(normed.astype(jnp.bfloat16))
    queries = jnp.dot(attn_in, w_query, preferred_element_type=jnp.float32).astype(jnp.bfloat16)
    keys_loc = jnp.dot(attn_in, w_key, preferred_element_type=jnp.float32).astype(jnp.bfloat16)
    values_loc = jnp.dot(attn_in, w_value, preferred_element_type=jnp.float32).astype(jnp.bfloat16)
    mixed_out, softmax_p, states = mixer_forward(
        queries, keys_loc, values_loc, gate_rows, keep_rows, persist_key, persist_value
    )
    mixed_low = mixed_out.astype(jnp.bfloat16)
    middle = residual + collect_partial(
        jnp.dot(mixed_low, w_output, preferred_element_type=jnp.float32)
    )
    normed_ffn, inv_ffn = norm_forward(middle, gain_ffn.astype(jnp.float32))
    ffn_in = spread_features(normed_ffn.astype(jnp.bfloat16))
    gate_pre = jnp.dot(ffn_in, w_gate, preferred_element_type=jnp.float32)
    up_pre = jnp.dot(ffn_in, w_up, preferred_element_type=jnp.float32)
    ffn_act = (jax.nn.silu(gate_pre) * up_pre).astype(jnp.bfloat16)
    kept_vals = (
        residual,
        inv_attn,
        attn_in,
        queries,
        keys_loc,
        values_loc,
        softmax_p,
        states,
        mixed_low,
        middle,
        inv_ffn,
        ffn_in,
        gate_pre,
        up_pre,
        ffn_act,
    )
    layer_out = None
    if with_output:
        down_sum = collect_partial(jnp.dot(ffn_act, w_down, preferred_element_type=jnp.float32))
        layer_out = (middle + down_sum).astype(jnp.bfloat16)
    return (layer_out, kept_vals)


def layer_backward(upstream, weights, gate_rows, keep_rows, kept_vals):
    (
        gain_attn,
        w_query,
        w_key,
        w_value,
        persist_key,
        persist_value,
        w_output,
        gain_ffn,
        w_gate,
        w_up,
        w_down,
    ) = weights
    (
        residual,
        inv_attn,
        attn_in,
        queries,
        keys_loc,
        values_loc,
        softmax_p,
        states,
        mixed_low,
        middle,
        inv_ffn,
        ffn_in,
        gate_pre,
        up_pre,
        ffn_act,
    ) = kept_vals
    grad_final = upstream.astype(jnp.float32)
    full_down = spread_grads(upstream)
    grad_down = jnp.dot(ffn_act.T, full_down, preferred_element_type=jnp.float32)
    grad_act = jnp.dot(full_down, w_down.T, preferred_element_type=jnp.float32)
    sigmoid_g = jax.nn.sigmoid(gate_pre)
    silu_g = gate_pre * sigmoid_g
    grad_gatepre = (grad_act * up_pre * (sigmoid_g + silu_g * (1.0 - sigmoid_g))).astype(
        jnp.bfloat16
    )
    grad_uppre = (grad_act * silu_g).astype(jnp.bfloat16)
    grad_gate = jnp.dot(ffn_in.T, grad_gatepre, preferred_element_type=jnp.float32)
    grad_up = jnp.dot(ffn_in.T, grad_uppre, preferred_element_type=jnp.float32)
    ffn_partial = jnp.dot(grad_gatepre, w_gate.T, preferred_element_type=jnp.float32)
    ffn_partial = ffn_partial + jnp.dot(grad_uppre, w_up.T, preferred_element_type=jnp.float32)
    grad_ffn_in = collect_grads(ffn_partial)
    back_mid, grad_gain_ffn = norm_reverse(
        middle, inv_ffn, gain_ffn.astype(jnp.float32), grad_ffn_in
    )
    grad_middle = grad_final + back_mid
    full_mid = spread_grads(grad_middle.astype(jnp.bfloat16))
    grad_output = jnp.dot(mixed_low.T, full_mid, preferred_element_type=jnp.float32)
    grad_mixed = jnp.dot(full_mid, w_output.T, preferred_element_type=jnp.float32).astype(
        jnp.bfloat16
    )
    grad_q, grad_k, grad_v, grad_pkey, grad_pvalue = mixer_back(
        queries,
        keys_loc,
        values_loc,
        gate_rows,
        keep_rows,
        persist_key,
        persist_value,
        softmax_p,
        states,
        grad_mixed,
    )
    grad_query = jnp.dot(attn_in.T, grad_q, preferred_element_type=jnp.float32)
    grad_key = jnp.dot(attn_in.T, grad_k, preferred_element_type=jnp.float32)
    grad_value = jnp.dot(attn_in.T, grad_v, preferred_element_type=jnp.float32)
    attn_partial = jnp.dot(grad_q, w_query.T, preferred_element_type=jnp.float32)
    attn_partial = attn_partial + jnp.dot(grad_k, w_key.T, preferred_element_type=jnp.float32)
    attn_partial = attn_partial + jnp.dot(grad_v, w_value.T, preferred_element_type=jnp.float32)
    grad_attn_in = collect_grads(attn_partial)
    back_in, grad_gain_attn = norm_reverse(
        residual, inv_attn, gain_attn.astype(jnp.float32), grad_attn_in
    )
    grad_input = (grad_middle + back_in).astype(jnp.bfloat16)
    return (
        grad_input,
        (
            grad_gain_attn,
            grad_query,
            grad_key,
            grad_value,
            grad_pkey,
            grad_pvalue,
            grad_output,
            grad_gain_ffn,
            grad_gate,
            grad_up,
            grad_down,
        ),
    )


def local(
    tokens,
    cotangent,
    block_order,
    lengths,
    decay,
    write_gate,
    gain_attn,
    w_query,
    w_key,
    w_value,
    persist_key,
    persist_value,
    w_output,
    gain_ffn,
    w_gate,
    w_up,
    w_down,
):
    micro_count = tokens.shape[0]
    section_id = lax.axis_index("section")
    col_id = lax.axis_index("col")
    block_count = tokens.shape[1] // BLOCK
    total_blocks = block_order.shape[1]
    shards = (
        gain_attn,
        w_query,
        w_key,
        w_value,
        persist_key,
        persist_value,
        w_output,
        gain_ffn,
        w_gate,
        w_up,
        w_down,
    )
    my_blocks = col_id * block_count + jnp.arange(block_count, dtype=jnp.int32)
    deal_picks = jnp.take(block_order, my_blocks, axis=1)
    position_ids = jnp.arange(total_blocks, dtype=jnp.int32)
    matches = (block_order[:, :, None] == my_blocks[None, None, :]).astype(jnp.int32)
    back_picks = jnp.sum(matches * position_ids[None, :, None], axis=1)
    dealt_tokens, dealt_cot = regroup((tokens, cotangent), deal_picks)

    def micro_inputs(micro_idx):
        length_row = lax.dynamic_index_in_dim(lengths, micro_idx, 0, keepdims=False)
        seq_ends = jnp.cumsum(length_row)
        starts = seq_ends - length_row
        is_start = jnp.any(my_blocks[:, None] == starts[None, :], axis=1)
        decay_rows = lax.dynamic_index_in_dim(decay[0], micro_idx, 0, keepdims=False)
        keep_rows = jnp.where(is_start[:, None], jnp.zeros_like(decay_rows), decay_rows)
        gate_rows = lax.dynamic_index_in_dim(write_gate[0], micro_idx, 0, keepdims=False)
        return (gate_rows, keep_rows)

    received = jnp.zeros(tokens.shape[1:], jnp.bfloat16)
    outputs = jnp.zeros(tokens.shape, jnp.bfloat16)
    section_inputs = jnp.zeros(tokens.shape, jnp.bfloat16)
    for tick_num in range(micro_count + 1):
        micro_pos = tick_num - section_id
        is_valid = (micro_pos >= 0) & (micro_pos < micro_count)
        micro_idx = jnp.clip(micro_pos, 0, micro_count - 1)
        layer_in = jnp.where(
            section_id == 0, dealt_tokens[min(tick_num, micro_count - 1)], received
        )
        weights, columns = fetch_weights(shards)
        gate_rows, keep_rows = micro_inputs(micro_idx)
        layer_out, _ = layer_forward(layer_in, weights, gate_rows, keep_rows, True)
        outputs = jnp.where(
            is_valid, lax.dynamic_update_index_in_dim(outputs, layer_out, micro_idx, 0), outputs
        )
        section_inputs = jnp.where(
            is_valid,
            lax.dynamic_update_index_in_dim(section_inputs, layer_in, micro_idx, 0),
            section_inputs,
        )
        if tick_num < micro_count:
            received = from_behind(layer_out, "section", 1)
    received = jnp.zeros(tokens.shape[1:], jnp.bfloat16)
    input_grads = jnp.zeros(tokens.shape, jnp.bfloat16)
    grad_acc = None
    for tick_num in range(micro_count + 1):
        micro_pos = micro_count - tick_num - section_id
        is_valid = (micro_pos >= 0) & (micro_pos < micro_count)
        micro_idx = jnp.clip(micro_pos, 0, micro_count - 1)
        upstream = jnp.where(
            section_id == 1,
            lax.dynamic_index_in_dim(dealt_cot, micro_idx, 0, keepdims=False),
            received,
        )
        layer_in = lax.dynamic_index_in_dim(section_inputs, micro_idx, 0, keepdims=False)
        weights, columns = fetch_weights(shards)
        gate_rows, keep_rows = micro_inputs(micro_idx)
        _, kept_vals = layer_forward(layer_in, weights, gate_rows, keep_rows, False)
        grad_input, weight_grads = layer_backward(
            upstream, weights, gate_rows, keep_rows, kept_vals
        )
        valid_f = is_valid.astype(jnp.float32)
        if grad_acc is None:
            grad_acc = tuple((valid_f * member for member in weight_grads))
        else:
            grad_acc = tuple(
                (running + valid_f * member for running, member in zip(grad_acc, weight_grads))
            )
        input_grads = jnp.where(
            is_valid,
            lax.dynamic_update_index_in_dim(input_grads, grad_input, micro_idx, 0),
            input_grads,
        )
        if tick_num < micro_count:
            received = from_behind(grad_input, "section", -1)
    summed = (
        lax.psum_scatter(
            grad_acc[0][None].astype(jnp.bfloat16), "col", scatter_dimension=1, tiled=True
        ).astype(jnp.float32),
        lax.psum_scatter(
            grad_acc[1][None].astype(jnp.bfloat16), "col", scatter_dimension=1, tiled=True
        ).astype(jnp.float32),
        lax.psum_scatter(
            grad_acc[2][None].astype(jnp.bfloat16), "col", scatter_dimension=1, tiled=True
        ).astype(jnp.float32),
        lax.psum_scatter(
            grad_acc[3][None].astype(jnp.bfloat16), "col", scatter_dimension=1, tiled=True
        ).astype(jnp.float32),
        lax.psum_scatter(
            grad_acc[4][None].astype(jnp.bfloat16), "col", scatter_dimension=1, tiled=True
        ).astype(jnp.float32),
        lax.psum_scatter(
            grad_acc[5][None].astype(jnp.bfloat16), "col", scatter_dimension=1, tiled=True
        ).astype(jnp.float32),
        lax.psum_scatter(
            grad_acc[6][None].astype(jnp.bfloat16), "col", scatter_dimension=2, tiled=True
        ).astype(jnp.float32),
        lax.psum_scatter(
            grad_acc[7][None].astype(jnp.bfloat16), "col", scatter_dimension=1, tiled=True
        ).astype(jnp.float32),
        lax.psum_scatter(
            grad_acc[8][None].astype(jnp.bfloat16), "col", scatter_dimension=1, tiled=True
        ).astype(jnp.float32),
        lax.psum_scatter(
            grad_acc[9][None].astype(jnp.bfloat16), "col", scatter_dimension=1, tiled=True
        ).astype(jnp.float32),
        lax.psum_scatter(
            grad_acc[10][None].astype(jnp.bfloat16), "col", scatter_dimension=2, tiled=True
        ).astype(jnp.float32),
    )
    restored_out, restored_grads = regroup((outputs, input_grads), back_picks)
    return (restored_out[None], restored_grads[None]) + tuple(summed)


def solution(mesh):
    return jax.shard_map(
        local,
        mesh=mesh,
        in_specs=(
            P(None, "col", "row"),
            P(None, "col", "row"),
            P(),
            P(),
            P("section", None, "col", "row"),
            P("section", None, "col", "row"),
            P("section", ("row", "col")),
            P("section", "col", "row"),
            P("section", "col", "row"),
            P("section", "col", "row"),
            P("section", "col", "row"),
            P("section", "col", "row"),
            P("section", "row", "col"),
            P("section", ("row", "col")),
            P("section", "col", "row"),
            P("section", "col", "row"),
            P("section", "row", "col"),
        ),
        out_specs=(
            P("section", None, "col", "row"),
            P("section", None, "col", "row"),
            P("section", ("row", "col")),
            P("section", "col", "row"),
            P("section", "col", "row"),
            P("section", "col", "row"),
            P("section", "col", "row"),
            P("section", "col", "row"),
            P("section", "row", "col"),
            P("section", ("row", "col")),
            P("section", "col", "row"),
            P("section", "col", "row"),
            P("section", "row", "col"),
        ),
        check_vma=False,
    )
```

profile of v0, /device:TPU:0, one launch (start us, length us, event | category | flops | bytes accessed | tf_op | source)
XLA Modules:
  0.0 2357.3 jit_solution(2785872376221586914)
XLA Ops:
  62.7 15.2 all_gather.121
  77.8 21.4 all_gather.123
  99.2 21.2 all_gather.125
  120.5 18.7 all_gather.128
  194.2 14.7 all_gather.127
  214.6 26.1 %reduce-scatter.36.cloned.1.call-done = bf16[384,256]{1,0:T(8,128)(2,1)} async-done(((bf16[384,1024]{1,0:T(8,128)(2,1)}), bf16[384,256]{1,0:T(8,128)(2,1)}) %reduce-scatter.36.cloned.1.call-update) | async-done | bytes 196624 | tf_op jit(solution)/shard_map/reduce_scatter | solution.py:99
  251.8 14.7 all_gather.130
  281.0 32.0 %all-gather.21.cloned.1.call-done = bf16[1,1024,704]{1,2,0:T(8,128)(2,1)} async-done(((bf16[1,256,704]{1,2,0:T(8,128)(2,1)}), bf16[1,1024,704]{1,2,0:T(8,128)(2,1)}) %all-gather.21.cloned.1.call-update) | async-done | bytes 1441808 | tf_op jit(solution)/shard_map/all_gather | solution.py:53
  313.0 35.3 %all-gather.23.cloned.1.call-done = bf16[1,704,1024]{2,1,0:T(8,128)(2,1)} async-done(((bf16[1,704,256]{2,1,0:T(8,128)(2,1)}), bf16[1,704,1024]{2,1,0:T(8,128)(2,1)}) %all-gather.23.cloned.1.call-update) | async-done | bytes 1441808 | tf_op jit(solution)/shard_map/all_gather | solution.py:54
  354.9 22.5 reduce-scatter.38.cloned.1.call-done
  390.6 14.9 all_gather.134
  446.0 26.2 %reduce-scatter.40.cloned.1.call-done = bf16[384,256]{1,0:T(8,128)(2,1)} async-done(((bf16[384,1024]{1,0:T(8,128)(2,1)}), bf16[384,256]{1,0:T(8,128)(2,1)}) %reduce-scatter.40.cloned.1.call-update) | async-done | bytes 196624 | tf_op jit(solution)/shard_map/reduce_scatter | solution.py:99
  505.5 25.1 %reduce-scatter.42.cloned.1.call-done = bf16[384,256]{1,0:T(8,128)(2,1)} async-done(((bf16[384,1024]{1,0:T(8,128)(2,1)}), bf16[384,256]{1,0:T(8,128)(2,1)}) %reduce-scatter.42.cloned.1.call-update) | async-done | bytes 196624 | tf_op jit(solution)/shard_map/reduce_scatter | solution.py:99
  547.8 15.0 all_gather.138
  593.0 15.1 all_gather.140
  612.0 28.7 %reduce-scatter.44.cloned.1.call-done = bf16[384,256]{1,0:T(8,128)(2,1)} async-done(((bf16[384,1024]{1,0:T(8,128)(2,1)}), bf16[384,256]{1,0:T(8,128)(2,1)}) %reduce-scatter.44.cloned.1.call-update) | async-done | bytes 196624 | tf_op jit(solution)/shard_map/reduce_scatter | solution.py:99
  674.2 26.2 %reduce-scatter.46.cloned.1.call-done = bf16[384,256]{1,0:T(8,128)(2,1)} async-done(((bf16[384,1024]{1,0:T(8,128)(2,1)}), bf16[384,256]{1,0:T(8,128)(2,1)}) %reduce-scatter.46.cloned.1.call-update) | async-done | bytes 196624 | tf_op jit(solution)/shard_map/reduce_scatter | solution.py:99
  753.8 14.5 while.340
  769.2 14.6 all_gather.149
  804.0 18.8 reduce-scatter.52.cloned.1.call-done
  872.7 14.4 all_gather.162
  933.5 14.6 while.344
  949.0 14.6 all_gather.163
  972.7 14.6 while.342
  988.3 21.1 all_gather.156
  1027.6 21.5 all_gather.334
  1063.0 16.2 all_gather.151
  1091.5 24.9 %reduce-scatter.70.cloned.1.call-done = bf16[384,256]{1,0:T(8,128)(2,1)} async-done(((bf16[384,1024]{1,0:T(8,128)(2,1)}), bf16[384,256]{1,0:T(8,128)(2,1)}) %reduce-scatter.70.cloned.1.call-update) | async-done | bytes 196624 | tf_op jit(solution)/shard_map/reduce_scatter | solution.py:99
  1116.4 28.9 %reduce-scatter.54.cloned.1.call-done = bf16[384,256]{1,0:T(8,128)(2,1)} async-done(((bf16[384,1024]{1,0:T(8,128)(2,1)}), bf16[384,256]{1,0:T(8,128)(2,1)}) %reduce-scatter.54.cloned.1.call-update) | async-done | bytes 196624 | tf_op jit(solution)/shard_map/reduce_scatter | solution.py:109
  1159.1 14.4 all_gather.152
  1189.7 19.2 while.341
  1209.9 14.7 all-gather.5
  1239.1 23.4 reduce-scatter.56.cloned.1.call-done
  1278.4 19.8 all_gather.158
  1302.8 16.3 all_gather.157
  1324.8 24.4 %reduce-scatter.60.cloned.1.call-done = bf16[384,256]{1,0:T(8,128)(2,1)} async-done(((bf16[384,1024]{1,0:T(8,128)(2,1)}), bf16[384,256]{1,0:T(8,128)(2,1)}) %reduce-scatter.60.cloned.1.call-update) | async-done | bytes 196624 | tf_op jit(solution)/shard_map/reduce_scatter | solution.py:109
  1362.5 14.6 all_gather.159
  1393.3 23.3 while.343
  1417.5 14.8 all-gather.6
  1446.8 23.4 reduce-scatter.62.cloned.1.call-done
  1486.7 19.8 all_gather.329
  1511.0 16.3 all_gather.328
  1531.8 25.7 %reduce-scatter.66.cloned.1.call-done = bf16[384,256]{1,0:T(8,128)(2,1)} async-done(((bf16[384,1024]{1,0:T(8,128)(2,1)}), bf16[384,256]{1,0:T(8,128)(2,1)}) %reduce-scatter.66.cloned.1.call-update) | async-done | bytes 196624 | tf_op jit(solution)/shard_map/reduce_scatter | solution.py:109
  1600.6 19.2 while.345
  1620.7 14.8 all-gather.7
  1650.2 23.4 reduce-scatter.68.cloned.1.call-done
  1689.4 19.7 all_gather.336
  1713.7 16.3 all_gather.335
  1734.7 25.5 %reduce-scatter.72.cloned.1.call-done = bf16[384,256]{1,0:T(8,128)(2,1)} async-done(((bf16[384,1024]{1,0:T(8,128)(2,1)}), bf16[384,256]{1,0:T(8,128)(2,1)}) %reduce-scatter.72.cloned.1.call-update) | async-done | bytes 196624 | tf_op jit(solution)/shard_map/reduce_scatter | solution.py:109
  1772.7 14.4 all_gather.337
  1803.3 19.2 while.347
  1823.4 14.8 all-gather.8
  1850.8 23.4 reduce-scatter.74.cloned.1.call-done
  1875.5 17.6 all_gather.142
  1924.7 26.5 %reduce-scatter.48.cloned.1.call-done = bf16[384,256]{1,0:T(8,128)(2,1)} async-done(((bf16[384,1024]{1,0:T(8,128)(2,1)}), bf16[384,256]{1,0:T(8,128)(2,1)}) %reduce-scatter.48.cloned.1.call-update) | async-done | bytes 196624 | tf_op jit(solution)/shard_map/reduce_scatter | solution.py:99
  2044.1 18.9 all-reduce.18
  2078.0 20.7 reduce-scatter.78.cloned.1.call-done
  2100.3 21.1 reduce-scatter.76.cloned.1.call-done
  2123.1 32.4 %reduce-scatter.88.cloned.1.call-done = bf16[1,704,256]{2,1,0:T(8,128)(2,1)} async-done(((bf16[1,704,1024]{2,1,0:T(8,128)(2,1)}), bf16[1,704,256]{2,1,0:T(8,128)(2,1)}) %reduce-scatter.88.cloned.1.call-update) | async-done | bytes 360464 | tf_op jit(solution)/shard_map/reduce_scatter | solution.py:586
  2157.3 32.7 %reduce-scatter.86.cloned.1.call-done = bf16[1,256,704]{1,2,0:T(8,128)(2,1)} async-done(((bf16[1,1024,704]{1,2,0:T(8,128)(2,1)}), bf16[1,256,704]{1,2,0:T(8,128)(2,1)}) %reduce-scatter.86.cloned.1.call-update) | async-done | bytes 360464 | tf_op jit(solution)/shard_map/reduce_scatter | solution.py:583
  2191.9 32.5 %reduce-scatter.84.cloned.1.call-done = bf16[1,256,704]{1,2,0:T(8,128)(2,1)} async-done(((bf16[1,1024,704]{1,2,0:T(8,128)(2,1)}), bf16[1,256,704]{1,2,0:T(8,128)(2,1)}) %reduce-scatter.84.cloned.1.call-update) | async-done | bytes 360464 | tf_op jit(solution)/shard_map/reduce_scatter | solution.py:580
  2226.3 18.4 reduce-scatter.90.cloned.1.call-done
  2246.0 49.5 %all-gather.29.cloned.1.call-done = bf16[3,1536,256]{2,1,0:T(8,128)(2,1)} async-done(((bf16[3,384,256]{2,1,0:T(8,128)(2,1)}), bf16[3,1536,256]{2,1,0:T(8,128)(2,1)}) %all-gather.29.cloned.1.call-update) | async-done | bytes 2359312 | tf_op jit(solution)/shard_map/all_gather | solution.py:64
  2297.8 49.0 %all-gather.25.cloned.1.call-done = bf16[3,1536,256]{2,1,0:T(8,128)(2,1)} async-done(((bf16[3,384,256]{2,1,0:T(8,128)(2,1)}), bf16[3,1536,256]{2,1,0:T(8,128)(2,1)}) %all-gather.25.cloned.1.call-update) | async-done | bytes 2359312 | tf_op jit(solution)/shard_map/all_gather | solution.py:63
  (1548 shorter events, 1161.0 us)
Async XLA Ops:
  7.2 53.9 %copy-start.264 = (s32[3,24]{1,0:T(4,128)S(1)}, s32[3,24]{1,0:T(4,128)}, u32[]{:S(2)}) copy-start(s32[3,24]{1,0:T(4,128)} %param.69) | copy-start | bytes 868
  7.2 54.8 %copy-start.260 = (f32[1,3,384,2]{2,3,1,0:T(2,128)S(1)}, f32[1,3,384,2]{2,3,1,0:T(2,128)}, u32[]{:S(2)}) copy-start(f32[1,3,384,2]{2,3,1,0:T(2,128)} %param.72) | copy-start | bytes 27652
  7.2 55.5 %copy-start.235 = (bf16[1,256,256]{2,1,0:T(8,128)(2,1)S(1)}, bf16[1,256,256]{2,1,0:T(8,128)(2,1)}, u32[]{:S(2)}) copy-start(bf16[1,256,256]{2,1,0:T(8,128)(2,1)} %param.74) | copy-start | bytes 393220
  7.2 70.6 %copy-start.236 = (bf16[1,256,256]{2,1,0:T(8,128)(2,1)S(1)}, bf16[1,256,256]{2,1,0:T(8,128)(2,1)}, u32[]{:S(2)}) copy-start(bf16[1,256,256]{2,1,0:T(8,128)(2,1)} %param.75) | copy-start | bytes 393220
  7.2 132.0 %all-gather.27.cloned.1.call-start = ((), (), s32[]{:S(2)}) async-start(), calls=%async_computation.42 | async-start | bytes 2949120 | tf_op jit(solution)/shard_map/all_gather | solution.py:64
  7.3 92.0 %copy-start.237 = (bf16[1,256,256]{2,1,0:T(8,128)(2,1)S(1)}, bf16[1,256,256]{2,1,0:T(8,128)(2,1)}, u32[]{:S(2)}) copy-start(bf16[1,256,256]{2,1,0:T(8,128)(2,1)} %param.76) | copy-start | bytes 393220
  8.0 112.5 %copy-start.238 = (bf16[1,256,256]{2,1,0:T(8,128)(2,1)S(1)}, bf16[1,256,256]{2,1,0:T(8,128)(2,1)}, u32[]{:S(2)}) copy-start(bf16[1,256,256]{2,1,0:T(8,128)(2,1)} %param.79) | copy-start | bytes 393220
  8.0 133.6 %all-gather.17.cloned.1.call-start = ((), (), s32[]{:S(2)}) async-start(), calls=%async_computation.29 | async-start | bytes 2949120 | tf_op jit(solution)/shard_map/all_gather | solution.py:63
  8.7 232.0 %reduce-scatter.36.cloned.1.call-start = ((), (), s32[]{:S(2)}) async-start(), calls=%async_computation.30 | async-start | bytes 983040 | tf_op jit(solution)/shard_map/reduce_scatter | solution.py:99
  18.1 81.1 %copy-start.252 = (f32[6,2]{0,1:T(2,128)}, f32[6,2]{0,1:T(2,128)S(1)}, u32[]{:S(2)}) copy-start(f32[6,2]{0,1:T(2,128)S(1)} %get-tuple-element.2239) | copy-start | bytes 148
  18.1 335.3 %copy-start.254 = (f32[6,2]{0,1:T(2,128)}, f32[6,2]{0,1:T(2,128)S(1)}, u32[]{:S(2)}) copy-start(f32[6,2]{0,1:T(2,128)S(1)} %get-tuple-element.2237) | copy-start | bytes 148
  62.7 114.9 %copy-start.271 = (pred[64,64]{1,0:T(8,128)(4,1)}, pred[64,64]{1,0:T(8,128)(4,1)S(1)}, u32[]{:S(2)}) copy-start(pred[64,64]{1,0:T(8,128)(4,1)S(1)} %iota_compare_fusion) | copy-start | bytes 12292
  212.8 64.9 %all-gather.19.cloned.1.call-start = ((), (), s32[]{:S(2)}) async-start(), calls=%async_computation.31 | async-start | bytes 1802240 | tf_op jit(solution)/shard_map/all_gather | solution.py:52
  213.4 99.6 %all-gather.21.cloned.1.call-start = ((), (), s32[]{:S(2)}) async-start(), calls=%async_computation.32 | async-start | bytes 1802240 | tf_op jit(solution)/shard_map/all_gather | solution.py:53
  214.0 134.2 %all-gather.23.cloned.1.call-start = ((), (), s32[]{:S(2)}) async-start(), calls=%async_computation.33 | async-start | bytes 1802240 | tf_op jit(solution)/shard_map/all_gather | solution.py:54
  214.5 162.9 %reduce-scatter.38.cloned.1.call-start = ((), (), s32[]{:S(2)}) async-start(), calls=%async_computation.34 | async-start | bytes 983040 | tf_op jit(solution)/shard_map/reduce_scatter | solution.py:99
  352.9 119.3 %reduce-scatter.40.cloned.1.call-start = ((), (), s32[]{:S(2)}) async-start(), calls=%async_computation.35 | async-start | bytes 983040 | tf_op jit(solution)/shard_map/reduce_scatter | solution.py:99
  378.5 31.5 %copy-start.41 = (bf16[3,384,256]{2,1,0:T(8,128)(2,1)}, bf16[3,384,256]{2,1,0:T(8,128)(2,1)S(1)}, u32[]{:S(2)}) copy-start(bf16[3,384,256]{2,1,0:T(8,128)(2,1)S(1)} %get-tuple-element.2257) | copy-start | bytes 1769476
  378.5 2.8 collective-permute-start
  381.5 100.7 %copy-start.54 = (bf16[384,256]{1,0:T(8,128)(2,1)}, bf16[384,256]{1,0:T(8,128)(2,1)S(1)}, u32[]{:S(2)}) copy-start(bf16[384,256]{1,0:T(8,128)(2,1)S(1)} %get-tuple-element.2206) | copy-start | bytes 589828
  446.0 84.7 %reduce-scatter.42.cloned.1.call-start = ((), (), s32[]{:S(2)}) async-start(), calls=%async_computation.36 | async-start | bytes 983040 | tf_op jit(solution)/shard_map/reduce_scatter | solution.py:99
  504.3 30.7 %copy-start.256 = (f32[6,2]{0,1:T(2,128)S(1)}, f32[6,2]{0,1:T(2,128)}, u32[]{:S(2)}) copy-start(f32[6,2]{0,1:T(2,128)} %get-tuple-element.2241) | copy-start | bytes 148
  504.4 31.0 %copy-start.314 = (bf16[8]{0:T(256)(128)(2,1)S(1)}, bf16[8]{0:T(256)(128)(2,1)}, u32[]{:S(2)}) copy-start(bf16[8]{0:T(256)(128)(2,1)} %get-tuple-element.2165) | copy-start | bytes 52
  504.4 31.7 %copy-start.262 = (f32[1,1,384,2]{2,3,1,0:T(2,128)S(1)}, f32[1,1,384,2]{2,3,1,0:T(2,128)}, u32[]{:S(2)}) copy-start(f32[1,1,384,2]{2,3,1,0:T(2,128)} %get-tuple-element.2235) | copy-start | bytes 9220
  504.4 136.3 %reduce-scatter.44.cloned.1.call-start = ((), (), s32[]{:S(2)}) async-start(), calls=%async_computation.37 | async-start | bytes 983040 | tf_op jit(solution)/shard_map/reduce_scatter | solution.py:99
  532.7 3.5 collective-permute-start.1
  536.0 72.2 %copy-start.239 = (f32[5,2]{1,0:T(8,128)}, f32[5,2]{1,0:T(8,128)S(1)}, u32[]{:S(2)}) copy-start(f32[5,2]{1,0:T(8,128)S(1)} %copy.2074) | copy-start | bytes 124
  612.0 88.4 %reduce-scatter.46.cloned.1.call-start = ((), (), s32[]{:S(2)}) async-start(), calls=%async_computation.38 | async-start | bytes 983040 | tf_op jit(solution)/shard_map/reduce_scatter | solution.py:99
  674.1 31.5 %copy-start.313 = (bf16[8]{0:T(256)(128)(2,1)S(1)}, bf16[8]{0:T(256)(128)(2,1)}, u32[]{:S(2)}) copy-start(bf16[8]{0:T(256)(128)(2,1)} %get-tuple-element.2166) | copy-start | bytes 52
  674.1 32.2 %copy-start.261 = (f32[1,1,384,2]{2,3,1,0:T(2,128)S(1)}, f32[1,1,384,2]{2,3,1,0:T(2,128)}, u32[]{:S(2)}) copy-start(f32[1,1,384,2]{2,3,1,0:T(2,128)} %get-tuple-element.2232) | copy-start | bytes 9220
  674.2 148.6 %reduce-scatter.52.cloned.1.call-start = ((), (), s32[]{:S(2)}) async-start(), calls=%async_computation.43 | async-start | bytes 983040 | tf_op jit(solution)/shard_map/reduce_scatter | solution.py:99
  702.4 4.0 collective-permute-start.2
  789.0 302.5 %reduce-scatter.64.cloned.1.call-start = ((), (), s32[]{:S(2)}) async-start(), calls=%async_computation.49 | async-start | bytes 983040 | tf_op jit(solution)/shard_map/reduce_scatter | solution.py:99
  968.8 122.6 %reduce-scatter.58.cloned.1.call-start = ((), (), s32[]{:S(2)}) async-start(), calls=%async_computation.46 | async-start | bytes 983040 | tf_op jit(solution)/shard_map/reduce_scatter | solution.py:99
  1053.1 63.3 %reduce-scatter.70.cloned.1.call-start = ((), (), s32[]{:S(2)}) async-start(), calls=%async_computation.52 | async-start | bytes 983040 | tf_op jit(solution)/shard_map/reduce_scatter | solution.py:99
  1080.5 64.8 %reduce-scatter.54.cloned.1.call-start = ((), (), s32[]{:S(2)}) async-start(), calls=%async_computation.44 | async-start | bytes 983040 | tf_op jit(solution)/shard_map/reduce_scatter | solution.py:109
  1089.7 172.8 %reduce-scatter.56.cloned.1.call-start = ((), (), s32[]{:S(2)}) async-start(), calls=%async_computation.45 | async-start | bytes 983040 | tf_op jit(solution)/shard_map/reduce_scatter | solution.py:109
  1237.6 36.2 %copy-start.251 = (f32[384]{0:T(512)S(1)}, f32[384]{0:T(512)}, u32[]{:S(2)}) copy-start(f32[384]{0:T(512)} %copy-done.250) | copy-start | bytes 4612
  1239.0 110.2 %reduce-scatter.60.cloned.1.call-start = ((), (), s32[]{:S(2)}) async-start(), calls=%async_computation.47 | async-start | bytes 983040 | tf_op jit(solution)/shard_map/reduce_scatter | solution.py:109
  1277.0 23.8 %collective-permute-start.3 = (bf16[384,256]{1,0:T(8,128)(2,1)S(1)}, bf16[384,256]{1,0:T(8,128)(2,1)S(1)}, u32[]{:S(2)}, u32[]{:S(2)}) collective-permute-start(bf16[384,256]{1,0:T(8,128)(2,1)S(1)} %get-tuple-element.2188), channel_id=1, source_target_pairs={{16,0},{17,1},{18,2},{19,3},{20,4},{21,5},{22,6},{23,7},{24,8},{25... | collective-permute-start | bytes 589832 | tf_op jit(solution)/shard_map/ppermute | solution.py:39
  1323.0 147.2 %reduce-scatter.62.cloned.1.call-start = ((), (), s32[]{:S(2)}) async-start(), calls=%async_computation.48 | async-start | bytes 983040 | tf_op jit(solution)/shard_map/reduce_scatter | solution.py:109
  1446.8 110.7 %reduce-scatter.66.cloned.1.call-start = ((), (), s32[]{:S(2)}) async-start(), calls=%async_computation.50 | async-start | bytes 983040 | tf_op jit(solution)/shard_map/reduce_scatter | solution.py:109
  1485.3 23.8 %collective-permute-start.4 = (bf16[384,256]{1,0:T(8,128)(2,1)S(1)}, bf16[384,256]{1,0:T(8,128)(2,1)S(1)}, u32[]{:S(2)}, u32[]{:S(2)}) collective-permute-start(bf16[384,256]{1,0:T(8,128)(2,1)S(1)} %get-tuple-element.2186), channel_id=1, source_target_pairs={{16,0},{17,1},{18,2},{19,3},{20,4},{21,5},{22,6},{23,7},{24,8},{25... | collective-permute-start | bytes 589832 | tf_op jit(solution)/shard_map/ppermute | solution.py:39
  1529.5 39.1 %copy-start.270 = (f32[384]{0:T(512)S(1)}, f32[384]{0:T(512)}, u32[]{:S(2)}) copy-start(f32[384]{0:T(512)} %get-tuple-element.2152) | copy-start | bytes 4612
  1531.3 142.3 %reduce-scatter.68.cloned.1.call-start = ((), (), s32[]{:S(2)}) async-start(), calls=%async_computation.51 | async-start | bytes 983040 | tf_op jit(solution)/shard_map/reduce_scatter | solution.py:109
  1648.7 36.0 %copy-start.267 = (f32[384]{0:T(512)S(1)}, f32[384]{0:T(512)}, u32[]{:S(2)}) copy-start(f32[384]{0:T(512)} %get-tuple-element.2156) | copy-start | bytes 4612
  1650.1 110.0 %reduce-scatter.72.cloned.1.call-start = ((), (), s32[]{:S(2)}) async-start(), calls=%async_computation.53 | async-start | bytes 983040 | tf_op jit(solution)/shard_map/reduce_scatter | solution.py:109
  1688.0 23.8 %collective-permute-start.5 = (bf16[384,256]{1,0:T(8,128)(2,1)S(1)}, bf16[384,256]{1,0:T(8,128)(2,1)S(1)}, u32[]{:S(2)}, u32[]{:S(2)}) collective-permute-start(bf16[384,256]{1,0:T(8,128)(2,1)S(1)} %get-tuple-element.2184), channel_id=1, source_target_pairs={{16,0},{17,1},{18,2},{19,3},{20,4},{21,5},{22,6},{23,7},{24,8},{25... | collective-permute-start | bytes 589832 | tf_op jit(solution)/shard_map/ppermute | solution.py:39
  1732.2 39.2 %copy-start.269 = (f32[384]{0:T(512)S(1)}, f32[384]{0:T(512)}, u32[]{:S(2)}) copy-start(f32[384]{0:T(512)} %copy-done.268) | copy-start | bytes 4612
  1734.0 140.2 %reduce-scatter.74.cloned.1.call-start = ((), (), s32[]{:S(2)}) async-start(), calls=%async_computation.54 | async-start | bytes 983040 | tf_op jit(solution)/shard_map/reduce_scatter | solution.py:109
  1803.3 35.6 %copy-start.316 = (bf16[4,2]{1,0:T(4,128)(2,1)S(1)}, bf16[4,2]{1,0:T(4,128)(2,1)}, u32[]{:S(2)}) copy-start(bf16[4,2]{1,0:T(4,128)(2,1)} %get-tuple-element.3805) | copy-start | bytes 52
  1850.7 100.5 %reduce-scatter.48.cloned.1.call-start = ((), (), s32[]{:S(2)}) async-start(), calls=%async_computation.39 | async-start | bytes 983040 | tf_op jit(solution)/shard_map/reduce_scatter | solution.py:99
  1924.7 114.4 %reduce-scatter.50.cloned.1.call-start = ((), (), s32[]{:S(2)}) async-start(), calls=%async_computation.40 | async-start | bytes 983040 | tf_op jit(solution)/shard_map/reduce_scatter | solution.py:99
  1984.7 79.5 %reduce-scatter.92.cloned.1.call-start = ((), (), s32[]{:S(2)}) async-start(), calls=%async_computation.64 | async-start | bytes 81920
  1994.8 70.7 %reduce-scatter.82.cloned.1.call-start = ((), (), s32[]{:S(2)}) async-start(), calls=%async_computation.59 | async-start | bytes 655360 | tf_op jit(solution)/shard_map/reduce_scatter | solution.py:574
  1997.5 78.9 %reduce-scatter.80.cloned.1.call-start = ((), (), s32[]{:S(2)}) async-start(), calls=%async_computation.58 | async-start | bytes 655360 | tf_op jit(solution)/shard_map/reduce_scatter | solution.py:565
  2002.3 96.5 %reduce-scatter.78.cloned.1.call-start = ((), (), s32[]{:S(2)}) async-start(), calls=%async_computation.57 | async-start | bytes 655360 | tf_op jit(solution)/shard_map/reduce_scatter | solution.py:562
  2006.5 114.9 %reduce-scatter.76.cloned.1.call-start = ((), (), s32[]{:S(2)}) async-start(), calls=%async_computation.56 | async-start | bytes 655360 | tf_op jit(solution)/shard_map/reduce_scatter | solution.py:559
  2014.4 141.0 %reduce-scatter.88.cloned.1.call-start = ((), (), s32[]{:S(2)}) async-start(), calls=%async_computation.62 | async-start | bytes 1802240 | tf_op jit(solution)/shard_map/reduce_scatter | solution.py:586
  2021.9 168.1 %reduce-scatter.86.cloned.1.call-start = ((), (), s32[]{:S(2)}) async-start(), calls=%async_computation.61 | async-start | bytes 1802240 | tf_op jit(solution)/shard_map/reduce_scatter | solution.py:583
  2029.2 195.2 %reduce-scatter.84.cloned.1.call-start = ((), (), s32[]{:S(2)}) async-start(), calls=%async_computation.60 | async-start | bytes 1802240 | tf_op jit(solution)/shard_map/reduce_scatter | solution.py:580
  2036.0 208.7 %reduce-scatter.90.cloned.1.call-start = ((), (), s32[]{:S(2)}) async-start(), calls=%async_computation.63 | async-start | bytes 81920
  2037.3 258.2 %all-gather.29.cloned.1.call-start = ((), (), s32[]{:S(2)}) async-start(), calls=%async_computation.55 | async-start | bytes 2949120 | tf_op jit(solution)/shard_map/all_gather | solution.py:64
  2038.7 308.1 %all-gather.25.cloned.1.call-start = ((), (), s32[]{:S(2)}) async-start(), calls=%async_computation.41 | async-start | bytes 2949120 | tf_op jit(solution)/shard_map/all_gather | solution.py:63
  (304 other events, 1446.3 us)
Sparse Core Ops, SparseCore 0:
  9.6 55.8 all-gather.26
  67.1 71.8 all-gather.16
  212.9 27.7 reduce-scatter.35
  242.1 35.5 all-gather.18
  279.1 33.7 all-gather.20
  314.4 33.7 all-gather.22
  353.0 24.3 reduce-scatter.37
  446.1 26.0 reduce-scatter.39
  504.5 26.1 reduce-scatter.41
  612.1 28.5 reduce-scatter.43
  674.3 26.0 reduce-scatter.45
  789.1 33.6 reduce-scatter.51
  969.0 33.1 reduce-scatter.63
  1053.2 33.5 reduce-scatter.57
  1089.5 26.8 reduce-scatter.69
  1119.1 26.0 reduce-scatter.53
  1239.1 23.3 reduce-scatter.55
  1323.1 26.0 reduce-scatter.59
  1446.9 23.2 reduce-scatter.61
  1531.4 26.0 reduce-scatter.65
  1650.2 23.2 reduce-scatter.67
  1734.1 26.0 reduce-scatter.71
  1850.8 23.3 reduce-scatter.73
  1924.8 26.4 reduce-scatter.47
  1984.8 26.0 reduce-scatter.49
  2013.0 19.0 reduce-scatter.91
  2034.3 19.9 reduce-scatter.81
  2056.6 19.6 reduce-scatter.79
  2078.8 19.8 reduce-scatter.77
  2101.5 19.8 reduce-scatter.75
  2123.9 31.5 reduce-scatter.87
  2157.8 32.1 reduce-scatter.85
  2192.3 32.1 reduce-scatter.83
  2226.8 17.8 reduce-scatter.89
  2246.8 48.6 all-gather.28
  2297.5 49.2 all-gather.24
where the time goes:
time: 2370 us; the launch traced here: 2360 us
  blocking collectives  843 us (36%)
  waiting for transfers between devices  771 us (33%)
  other arithmetic  293 us (12%)
  matrix products  241 us (10%)
  local copies, waits for them, and re-layouts  174 us (7%)
    all_gather x16, blocking collectives, spread_features(): return lax.all_gather(local_rows, 'row', axis=1, tiled=True)  250 us
    reduce_scatter x12, waiting for transfers between devices, collect_partial(): lax.psum_scatter(partial_rows.astype(jnp.bfloat16), 'row', scatter_dimens...  225 us
    reduce_scatter x8, waiting for transfers between devices, collect_grads(): lax.psum_scatter(partial_rows.astype(jnp.bfloat16), 'row', scatter_dimens...  198 us
    all_gather x12, blocking collectives, prefix(): lax.all_gather(a.astype(kind), axis)  189 us
    all_gather x8, blocking collectives, spread_grads(): return lax.all_gather(local_rows, 'row', axis=1, tiled=True)  120 us
    dynamic_update_slice x72, other arithmetic, mixer_forward(): _, local_after = lax.scan(chain_step, zero_state, (update, keep_rows))  93.2 us
    psum x10, blocking collectives, norm_forward(): sq_total = lax.psum(jnp.sum(residual * residual, axis=1), 'row')  90.7 us
    psum x6, blocking collectives, norm_reverse(): cross_sum = lax.psum(jnp.sum(weighted * residual, axis=1), 'row')  56.3 us
  transfers between devices with their start and end apart: 42, of which 30 were waited for; matrix products, arithmetic and copies ran while one was open for 7% of the time, Pallas kernels for 0%

commit v1 on v0

v1 whole, which is shorter than its diff:
```python
import functools

import jax
import jax.numpy as jnp
from jax import lax
from jax.experimental import pallas as pl
from jax.experimental.pallas import tpu as pltpu
from jax.sharding import PartitionSpec as P

BLOCK = 64
EPS = 1e-06
MESH = pl.DeviceIdType.MESH
F32 = jnp.float32
BF16 = jnp.bfloat16
VMEM_LIMIT = 56 << 20
N_AG, N_RS = 8, 7


def dot(a, b, ca=1, cb=0):
    return lax.dot_general(a, b, (((ca,), (cb,)), ((), ())), preferred_element_type=F32)


class Rows:
    def __init__(self, rows, own, width, send, recv):
        self.rows, self.own, self.width, self.half = rows, own, width, width // 2
        self.send, self.recv = send, recv
        self.s, self.r, self.c = (lax.axis_index(a) for a in ("section", "row", "col"))
        self.rx = self.r + 1 - 2 * lax.rem(self.r, 2)
        self.ry = lax.rem(self.r + 2, 4)
        self.rd = lax.rem(self.rx + 2, 4)
        self.x = (self.s, self.rx, self.c)
        self.y = (self.s, self.ry, self.c)
        self.sib = (1 - self.s, self.r, self.c)
        self.started = []

    def greet(self, others=()):
        barrier = pltpu.get_barrier_semaphore()
        peers = [self.x, self.y, self.sib] + list(others)
        for peer in peers:
            pl.semaphore_signal(barrier, inc=1, device_id=peer, device_id_type=MESH)
        pl.semaphore_wait(barrier, len(peers))

    def copy(self, src, dst, m, k, peer):
        return pltpu.make_async_remote_copy(
            src_ref=src,
            dst_ref=dst,
            send_sem=self.send.at[m, k],
            recv_sem=self.recv.at[m, k],
            device_id=peer,
            device_id_type=MESH,
        )

    def go(self, copy):
        copy.start()
        self.started.append(copy)

    def finish(self):
        for copy in self.started:
            copy.wait_send()

    def span(self, m, s, r):
        return pl.ds(pl.multiple_of(m * self.rows + (s * 4 + r) * self.own, 16), self.own)

    def ag_copy(self, full, m, k):
        left, right = pl.ds(0, self.half), pl.ds(self.half, self.half)
        mine, atx, aty, atd = (
            self.span(m, self.s, r) for r in (self.r, self.rx, self.ry, self.rd)
        )
        if k == 0:
            return self.copy(full.at[mine, :], full.at[mine, :], m, 0, self.x)
        if k == 1:
            return self.copy(full.at[mine, :], full.at[mine, :], m, 1, self.y)
        if k == 2:
            return self.copy(full.at[mine, :], full.at[mine, :], m, 2, self.sib)
        if k == 3:
            return self.copy(full.at[atx, left], full.at[atx, left], m, 3, self.y)
        if k == 4:
            return self.copy(full.at[aty, right], full.at[aty, right], m, 4, self.x)
        if k == 5:
            return self.copy(full.at[atx, :], full.at[atx, :], m, 5, self.sib)
        if k == 6:
            return self.copy(full.at[aty, :], full.at[aty, :], m, 6, self.sib)
        return self.copy(full.at[atd, :], full.at[atd, :], m, 7, self.sib)

    def ag_start(self, full, m):
        for k in (0, 1, 2):
            self.go(self.ag_copy(full, m, k))

    def ag_pass(self, full, m):
        self.ag_copy(full, m, 0).wait_recv()
        self.go(self.ag_copy(full, m, 3))
        self.go(self.ag_copy(full, m, 5))
        self.ag_copy(full, m, 1).wait_recv()
        self.go(self.ag_copy(full, m, 4))
        self.go(self.ag_copy(full, m, 6))

    def ag_diag(self, full, m):
        self.ag_copy(full, m, 3).wait_recv()
        self.ag_copy(full, m, 4).wait_recv()
        self.go(self.ag_copy(full, m, 7))

    def ag_wait(self, full, m):
        for k in (2, 5, 6, 7):
            self.ag_copy(full, m, k).wait_recv()

    def rs_copy(self, m, k):
        part, pair, both, transit, final = self.buffers
        left, right = pl.ds(0, self.half), pl.ds(self.half, self.half)
        if k == 8:
            other = pl.ds(
                pl.multiple_of(m * self.rows + (1 - self.s) * 4 * self.own, 16), 4 * self.own
            )
            return self.copy(part.at[other, :], pair.at[m], m, 8, self.sib)
        if k == 9:
            return self.copy(both.at[m, self.rd, :, left], transit.at[m, 0], m, 9, self.x)
        if k == 10:
            return self.copy(both.at[m, self.rd, :, right], transit.at[m, 1], m, 10, self.y)
        if k == 11:
            return self.copy(both.at[m, self.rx, :, left], final.at[m, 0, :, left], m, 11, self.x)
        if k == 12:
            return self.copy(both.at[m, self.ry, :, right], final.at[m, 1, :, right], m, 12, self.y)
        if k == 13:
            return self.copy(both.at[m, self.ry, :, left], final.at[m, 1, :, left], m, 13, self.y)
        return self.copy(both.at[m, self.rx, :, right], final.at[m, 0, :, right], m, 14, self.x)

    def rs_start(self, m):
        self.go(self.rs_copy(m, 8))

    def rs_pair(self, m):
        part, pair, both, _, _ = self.buffers
        self.rs_copy(m, 8).wait_recv()
        for r in range(4):
            mine = part[self.span(m, self.s, r), :].astype(F32)
            theirs = pair[m, r * self.own : (r + 1) * self.own, :].astype(F32)
            both[m, r] = (mine + theirs).astype(BF16)
        for k in (9, 10, 11, 12):
            self.go(self.rs_copy(m, k))

    def rs_transit(self, m):
        _, _, both, transit, _ = self.buffers
        left, right = pl.ds(0, self.half), pl.ds(self.half, self.half)
        self.rs_copy(m, 9).wait_recv()
        total = both[m, self.ry, :, left].astype(F32) + transit[m, 0].astype(F32)
        both[m, self.ry, :, left] = total.astype(BF16)
        self.go(self.rs_copy(m, 13))
        self.rs_copy(m, 10).wait_recv()
        total = both[m, self.rx, :, right].astype(F32) + transit[m, 1].astype(F32)
        both[m, self.rx, :, right] = total.astype(BF16)
        self.go(self.rs_copy(m, 14))

    def rs_result(self, m):
        _, _, both, _, final = self.buffers
        for k in (11, 12, 13, 14):
            self.rs_copy(m, k).wait_recv()
        return both[m, self.r].astype(F32) + final[m, 0].astype(F32) + final[m, 1].astype(F32)


def row_scratch(micros, rows, own, width):
    return [
        pltpu.VMEM((micros * rows, width), BF16),
        pltpu.VMEM((micros, 4 * own, width), BF16),
        pltpu.VMEM((micros, 4, own, width), BF16),
        pltpu.VMEM((micros, 2, own, width // 2), BF16),
        pltpu.VMEM((micros, 2, own, width), BF16),
        pltpu.SemaphoreType.DMA((micros, N_AG + N_RS)),
        pltpu.SemaphoreType.DMA((micros, N_AG + N_RS)),
    ]


class Local:
    def __init__(self, sems):
        self.sems, self.used, self.open = sems, 0, []

    def start(self, src, dst):
        copy = pltpu.make_async_copy(src, dst, self.sems.at[self.used])
        self.used += 1
        copy.start()
        self.open.append(copy)
        return copy

    def wait(self, copy):
        copy.wait()
        self.open.remove(copy)

    def finish(self):
        for copy in list(self.open):
            copy.wait()


def inv_rms(values):
    return lax.rsqrt(jnp.mean(values * values, axis=1, keepdims=True) + EPS)


def norm_to(full, gain, values, span):
    full[span, :] = (values * inv_rms(values) * gain).astype(BF16)


def norm_back(values, gain, grad):
    scale = inv_rms(values)
    weighted = grad * gain
    inner = jnp.mean(weighted * values, axis=1, keepdims=True)
    back = scale * weighted - values * (scale * scale * scale * inner)
    return back, jnp.sum(grad * values * scale, axis=0, keepdims=True)


def ffn_forward_kernel(
    micros, rows, own, mid, gain, wg_h, wu_h, wd_h, in_o, gp_o, up_o, act_o, y_o,
    full, wg, wu, wd, gp, up, act, part, pair, both, transit, final, send, recv, sems,
):
    width = mid.shape[2]
    row = Rows(rows, own, width, send, recv)
    row.buffers = (part, pair, both, transit, final)
    loc = Local(sems)
    loads = [loc.start(a, b) for a, b in ((wg_h, wg), (wu_h, wu), (wd_h, wd))]
    scale = gain[...]
    for m in range(micros):
        norm_to(full, scale, mid[m], row.span(m, row.s, row.r))
    row.greet()

    def compute(m):
        here = pl.ds(m * rows, rows)
        loc.start(full.at[here, :], in_o.at[here, :])
        gate = dot(full[here, :], wg[...])
        lift = dot(full[here, :], wu[...])
        gp[here, :] = gate.astype(BF16)
        up[here, :] = lift.astype(BF16)
        act[here, :] = (gate * jax.nn.sigmoid(gate) * lift).astype(BF16)
        part[here, :] = dot(act[here, :], wd[...]).astype(BF16)
        for a, b in ((gp, gp_o), (up, up_o), (act, act_o)):
            loc.start(a.at[here, :], b.at[here, :])

    def result(m):
        y_o[m] = (mid[m] + row.rs_result(m)).astype(BF16)

    def before(m):
        if m == 0:
            for copy in loads:
                loc.wait(copy)

    schedule(row, full, micros, before, compute, result)
    row.finish()
    loc.finish()


def schedule(row, full, micros, before, compute, result, between=None):
    row.ag_start(full, 0)
    if micros > 1:
        row.ag_start(full, 1)
    row.ag_pass(full, 0)
    for m in range(2, micros):
        row.ag_start(full, m)
    if micros > 1:
        row.ag_pass(full, 1)
    row.ag_diag(full, 0)
    for m in range(micros):
        row.ag_wait(full, m)
        before(m)
        if m >= 1:
            row.rs_pair(m - 1)
        if m >= 2:
            row.rs_transit(m - 2)
        compute(m)
        row.rs_start(m)
        if m + 2 < micros:
            row.ag_pass(full, m + 2)
        if m + 1 < micros:
            row.ag_diag(full, m + 1)
    tail(row, micros, result, between)


def tail(row, micros, result, between=None):
    more = list(between) if between else []

    def step():
        if more:
            more.pop(0)()

    step()
    if micros > 1:
        row.rs_transit(micros - 2)
    row.rs_pair(micros - 1)
    for m in range(micros - 1):
        if m < micros - 2:
            step()
            result(m)
    step()
    row.rs_transit(micros - 1)
    if micros > 1:
        result(micros - 2)
    while more:
        step()
    result(micros - 1)


def ffn_backward_kernel(
    micros, rows, own, dy, mid, gain, wg_h, wu_h, wd_h, in_h, gp_h, up_h, act_h,
    dmid_o, dgain_o, gg_o, gu_o, gd_o,
    full, wg, wu, wd, xin, gp, up, act, dg, du, gg, gu, gd,
    part, pair, both, transit, final, send, recv, sems,
):
    width = mid.shape[2]
    row = Rows(rows, own, width, send, recv)
    row.buffers = (part, pair, both, transit, final)
    loc = Local(sems)
    early = [
        loc.start(a, b)
        for a, b in ((wd_h, wd), (gp_h, gp), (up_h, up), (wg_h, wg), (wu_h, wu))
    ]
    late = [loc.start(a, b) for a, b in ((act_h, act), (in_h, xin))]
    for m in range(micros):
        full[row.span(m, row.s, row.r), :] = dy[m]
    row.greet()
    scale = gain[...]
    dgain_o[...] = jnp.zeros_like(dgain_o)

    def before(m):
        if m == 0:
            for copy in early:
                loc.wait(copy)

    def compute(m):
        here = pl.ds(m * rows, rows)
        d_act = dot(full[here, :], wd[...], 1, 1)
        gate = gp[here, :].astype(F32)
        lift = up[here, :].astype(F32)
        sig = jax.nn.sigmoid(gate)
        silu = gate * sig
        dg[here, :] = (d_act * lift * (sig + silu * (1.0 - sig))).astype(BF16)
        du[here, :] = (d_act * silu).astype(BF16)
        total = dot(dg[here, :], wg[...], 1, 1) + dot(du[here, :], wu[...], 1, 1)
        part[here, :] = total.astype(BF16)

    def result(m):
        back, gains = norm_back(mid[m], scale, row.rs_result(m))
        dmid_o[m] = dy[m].astype(F32) + back
        dgain_o[...] += gains

    def down():
        for copy in late:
            loc.wait(copy)
        tiles(width, lambda at: store(gd, at, dot(act[...], full[:, at], 0, 0), True))
        loc.start(gd, gd_o)

    def gates():
        tiles(width, lambda at: store(gg, at, dot(xin[:, at], dg[...], 0, 0), False))
        loc.start(gg, gg_o)

    def ups():
        tiles(width, lambda at: store(gu, at, dot(xin[:, at], du[...], 0, 0), False))
        loc.start(gu, gu_o)

    schedule(row, full, micros, before, compute, result, [down, gates, ups])
    row.finish()
    loc.finish()


def store(ref, at, value, columns):
    if columns:
        ref[:, at] = value.astype(ref.dtype)
    else:
        ref[at, :] = value.astype(ref.dtype)


def tiles(width, body, tile=256):
    @pl.loop(0, width // tile)
    def _(i):
        body(pl.ds(pl.multiple_of(i * tile, tile), tile))


def pair_masks(size):
    rows_at = lax.broadcasted_iota(jnp.int32, (size, size), 0)
    cols_at = lax.broadcasted_iota(jnp.int32, (size, size), 1)
    return (rows_at >= cols_at) & (rows_at // BLOCK == cols_at // BLOCK)


def pair_probs(q, k, pk, mask, scale):
    inner = jnp.where(mask, dot(q, k, 1, 1) * scale, -1e30)
    outer = dot(q, pk, 1, 1) * scale
    top = jnp.maximum(
        jnp.max(inner, axis=1, keepdims=True), jnp.max(outer, axis=1, keepdims=True)
    )
    inner = jnp.exp(inner - top)
    outer = jnp.exp(outer - top)
    norm = 1.0 / (jnp.sum(inner, axis=1, keepdims=True) + jnp.sum(outer, axis=1, keepdims=True))
    return inner * norm, outer * norm


def col_peers(row, groups):
    return [(row.s, row.r, lax.rem(row.c + k, groups)) for k in range(1, groups)]


class States:
    def __init__(self, row, groups, mine, box, send, recv):
        self.row, self.groups, self.mine, self.box = row, groups, mine, box
        self.send, self.recv = send, recv

    def copies(self, m):
        for k in range(1, self.groups):
            yield pltpu.make_async_remote_copy(
                src_ref=self.mine.at[m],
                dst_ref=self.box.at[m, k],
                send_sem=self.send.at[m, k],
                recv_sem=self.recv.at[m, k],
                device_id=(self.row.s, self.row.r, lax.rem(self.row.c + k, self.groups)),
                device_id_type=MESH,
            )

    def start(self, m):
        for copy in self.copies(m):
            self.row.go(copy)

    def wait(self, m):
        for copy in self.copies(m):
            copy.wait_recv()

    def fold(self, m, through, entering, backward):
        entering[...] = jnp.zeros_like(entering)
        for k in range(self.groups - 1, 0, -1):
            if backward:

                @pl.when(self.row.c + k < self.groups)
                def _(k=k):
                    factor = through[m, lax.rem(self.row.c + k, self.groups)]
                    entering[...] = factor * entering[...] + self.box[
                        m, self.groups - k
                    ].astype(F32)
            else:

                @pl.when(self.row.c >= k)
                def _(k=k):
                    factor = through[m, lax.rem(self.row.c - k + self.groups, self.groups)]
                    entering[...] = factor * entering[...] + self.box[m, k].astype(F32)


def attn_forward_kernel(
    micros, rows, own, groups, x, gain, pk, pv, gate, keep, through, wqkv_h, wo_h,
    in_o, qkv_o, state_o, mixed_o, mid_o,
    full, wqkv, wo, qkv, state, mixed, update, entering, leaving, box,
    ssend, srecv, part, pair, both, transit, final, send, recv, sems,
):
    width, size = x.shape[2], pk.shape[1]
    blocks = rows // BLOCK
    factor = size ** (-0.5)
    row = Rows(rows, own, width, send, recv)
    row.buffers = (part, pair, both, transit, final)
    loc = Local(sems)
    loads = [loc.start(wqkv_h, wqkv), loc.start(wo_h, wo)]
    scale = gain[...]
    for m in range(micros):
        norm_to(full, scale, x[m].astype(F32), row.span(m, row.s, row.r))
    row.greet(col_peers(row, groups))
    states = States(row, groups, leaving, box, ssend, srecv)
    qs, ks, vs = (pl.ds(i * size, size) for i in range(3))
    mask = pair_masks(2 * BLOCK)

    row.ag_start(full, 0)
    row.ag_start(full, 1)
    row.ag_pass(full, 0)
    for m in range(2, micros):
        row.ag_start(full, m)
    row.ag_pass(full, 1)
    row.ag_diag(full, 0)
    for copy in loads:
        loc.wait(copy)
    for m in range(micros):
        row.ag_wait(full, m)
        here = pl.ds(m * rows, rows)
        loc.start(full.at[here, :], in_o.at[here, :])
        qkv[here, :] = dot(full[here, :], wqkv[...]).astype(BF16)
        loc.start(qkv.at[here, :], qkv_o.at[here, :])
        total = jnp.zeros((size, size), F32)
        for b in range(blocks):
            at = pl.ds(m * rows + b * BLOCK, BLOCK)
            keys = (qkv[at, ks].astype(F32) * gate[at, :]).astype(BF16)
            fresh = dot(keys, qkv[at, vs], 0, 0)
            update[m * blocks + b] = fresh
            total = keep[m, b] * total + fresh
        leaving[m] = total.astype(BF16)
        states.start(m)
        if m + 2 < micros:
            row.ag_pass(full, m + 2)
        if m + 1 < micros:
            row.ag_diag(full, m + 1)

    def compute(m):
        here = pl.ds(m * rows, rows)
        states.wait(m)
        states.fold(m, through, entering, False)
        memory = entering[...]
        for b in range(0, blocks, 2):
            at = pl.ds(m * rows + b * BLOCK, 2 * BLOCK)
            q, k, v = qkv[at, qs], qkv[at, ks], qkv[at, vs]
            inner, outer = pair_probs(q, k, pk[...], mask, factor)
            value = dot(inner.astype(BF16), v) + dot(outer.astype(BF16), pv[...])
            reads = []
            for i in range(2):
                now = keep[m, b + i] * memory
                low = now.astype(BF16)
                state[m * blocks + b + i] = low
                reads.append(dot(q[i * BLOCK : (i + 1) * BLOCK, :], low) * factor)
                memory = now + update[m * blocks + b + i]
            mixed[at, :] = (value + jnp.concatenate(reads, axis=0)).astype(BF16)
        part[here, :] = dot(mixed[here, :], wo[...]).astype(BF16)
        loc.start(mixed.at[here, :], mixed_o.at[here, :])

    def result(m):
        mid_o[m] = x[m].astype(F32) + row.rs_result(m)

    for m in range(micros):
        compute(m)
        row.rs_start(m)
        if m >= 1:
            row.rs_pair(m - 1)
        if m >= 2:
            row.rs_transit(m - 2)
    loc.start(state, state_o)
    tail(row, micros, result)
    row.finish()
    loc.finish()


def attn_backward_kernel(
    micros, rows, own, groups, dmid, x, gain, pk, pv, gate, keep, through, wqkv_h, wo_h,
    in_h, qkv_h, state_h, mixed_h,
    dx_o, dgain_o, dpk_o, dpv_o, gqkv_o, go_o,
    full, wqkv, wo, xin, qkv, state, mixed, dmix, dqkv, update, entering, leaving, box, gqkv, go,
    ssend, srecv, part, pair, both, transit, final, send, recv, sems,
):
    width, size = x.shape[2], pk.shape[1]
    blocks = rows // BLOCK
    factor = size ** (-0.5)
    row = Rows(rows, own, width, send, recv)
    row.buffers = (part, pair, both, transit, final)
    loc = Local(sems)
    first = [loc.start(wo_h, wo), loc.start(qkv_h, qkv)]
    second = [loc.start(state_h, state), loc.start(wqkv_h, wqkv)]
    third = [loc.start(mixed_h, mixed), loc.start(in_h, xin)]
    for m in range(micros):
        full[row.span(m, row.s, row.r), :] = dmid[m].astype(BF16)
    row.greet(col_peers(row, groups))
    states = States(row, groups, leaving, box, ssend, srecv)
    qs, ks, vs = (pl.ds(i * size, size) for i in range(3))
    mask = pair_masks(2 * BLOCK)
    scale = gain[...]
    dgain_o[...] = jnp.zeros_like(dgain_o)
    dpk_o[...] = jnp.zeros_like(dpk_o)
    dpv_o[...] = jnp.zeros_like(dpv_o)

    row.ag_start(full, 0)
    row.ag_start(full, 1)
    row.ag_pass(full, 0)
    for m in range(2, micros):
        row.ag_start(full, m)
    row.ag_pass(full, 1)
    row.ag_diag(full, 0)
    for copy in first:
        loc.wait(copy)
    for m in range(micros):
        row.ag_wait(full, m)
        here = pl.ds(m * rows, rows)
        dmix[here, :] = dot(full[here, :], wo[...], 1, 1).astype(BF16)
        total = jnp.zeros((size, size), F32)
        for b in reversed(range(blocks)):
            at = pl.ds(m * rows + b * BLOCK, BLOCK)
            fresh = dot(qkv[at, qs], dmix[at, :], 0, 0) * factor
            update[m * blocks + b] = fresh
            total = keep[m, b] * (fresh + total)
        leaving[m] = total.astype(BF16)
        states.start(m)
        if m + 2 < micros:
            row.ag_pass(full, m + 2)
        if m + 1 < micros:
            row.ag_diag(full, m + 1)
    for copy in second:
        loc.wait(copy)

    def compute(m):
        here = pl.ds(m * rows, rows)
        states.wait(m)
        states.fold(m, through, entering, True)
        memory = entering[...]
        for b in reversed(range(0, blocks, 2)):
            at = pl.ds(m * rows + b * BLOCK, 2 * BLOCK)
            q, k, v, d = qkv[at, qs], qkv[at, ks], qkv[at, vs], dmix[at, :]
            inner, outer = pair_probs(q, k, pk[...], mask, factor)
            d_inner = dot(d, v, 1, 1)
            d_outer = dot(d, pv[...], 1, 1)
            centre = jnp.sum(inner * d_inner, axis=1, keepdims=True) + jnp.sum(
                outer * d_outer, axis=1, keepdims=True
            )
            d_inner = (inner * (d_inner - centre)).astype(BF16)
            d_outer = (outer * (d_outer - centre)).astype(BF16)
            inner, outer = inner.astype(BF16), outer.astype(BF16)
            dpk_o[...] += dot(d_outer, q, 0, 0) * factor
            dpv_o[...] += dot(outer, d, 0, 0)
            dq = dot(d_inner, k) + dot(d_outer, pk[...])
            dk = dot(d_inner, q, 0, 0) * factor
            dv = dot(inner, d, 0, 0)
            keys = (k.astype(F32) * gate[at, :]).astype(BF16)
            parts = [None, None]
            for i in (1, 0):
                sub = slice(i * BLOCK, (i + 1) * BLOCK)
                low = memory.astype(BF16)
                parts[i] = (
                    dot(d[sub, :], state[m * blocks + b + i], 1, 1),
                    dot(v[sub, :], low, 1, 1),
                    dot(keys[sub, :], low),
                )
                memory = keep[m, b + i] * (update[m * blocks + b + i] + memory)
            more_q, more_k, more_v = (jnp.concatenate(pieces, axis=0) for pieces in zip(*parts))
            dqkv[at, qs] = ((dq + more_q) * factor).astype(BF16)
            dqkv[at, ks] = (dk + gate[at, :] * more_k).astype(BF16)
            dqkv[at, vs] = (dv + more_v).astype(BF16)
        part[here, :] = dot(dqkv[here, :], wqkv[...], 1, 1).astype(BF16)

    def result(m):
        back, gains = norm_back(x[m].astype(F32), scale, row.rs_result(m))
        dx_o[m] = (dmid[m] + back).astype(BF16)
        dgain_o[...] += gains

    for m in range(micros):
        compute(m)
        row.rs_start(m)
        if m >= 1:
            row.rs_pair(m - 1)
        if m >= 2:
            row.rs_transit(m - 2)

    def out_grad():
        for copy in third:
            loc.wait(copy)
        tiles(width, lambda at: store(go, at, dot(mixed[...], full[:, at], 0, 0), True))
        loc.start(go, go_o)

    def qkv_grad():
        tiles(width, lambda at: store(gqkv, at, dot(xin[:, at], dqkv[...], 0, 0), False))
        loc.start(gqkv, gqkv_o)

    tail(row, micros, result, [out_grad, qkv_grad])
    row.finish()
    loc.finish()


def others():
    s, r, c = (lax.axis_index(a) for a in ("section", "row", "col"))
    for k in range(1, 8):
        ps = lax.rem(s + k // 4, 2)
        low = r + (k % 2) * (1 - 2 * lax.rem(r, 2))
        pr = lax.rem(low + 2 * ((k // 2) % 2), 4)
        yield k, (ps, pr, c)


def deal_kernel(own, features, x, o, send, recv, local):
    s, r = lax.axis_index("section"), lax.axis_index("row")
    barrier = pltpu.get_barrier_semaphore()
    for _, peer in others():
        pl.semaphore_signal(barrier, inc=1, device_id=peer, device_id_type=MESH)
    pl.semaphore_wait(barrier, 7)
    mine = pl.ds(pl.multiple_of(r * features, 128), features)

    def rows_of(ps, pr):
        return pl.ds(pl.multiple_of((ps * 4 + pr) * own, 16), own)

    keep = pltpu.make_async_copy(x.at[:, rows_of(s, r), :], o.at[s, :, :, mine], local)
    keep.start()
    copies = []
    for k, peer in others():
        copy = pltpu.make_async_remote_copy(
            src_ref=x.at[:, rows_of(peer[0], peer[1]), :],
            dst_ref=o.at[s, :, :, mine],
            send_sem=send.at[k],
            recv_sem=recv.at[k],
            device_id=peer,
            device_id_type=MESH,
        )
        copy.start()
        copies.append(copy)
    for copy in copies:
        copy.wait()
    keep.wait()


def undeal_kernel(own, features, y, o, send, recv, local):
    s, r = lax.axis_index("section"), lax.axis_index("row")
    barrier = pltpu.get_barrier_semaphore()
    for _, peer in others():
        pl.semaphore_signal(barrier, inc=1, device_id=peer, device_id_type=MESH)
    pl.semaphore_wait(barrier, 7)
    mine = pl.ds(pl.multiple_of((s * 4 + r) * own, 16), own)

    def columns(pr):
        return pl.ds(pl.multiple_of(pr * features, 128), features)

    keep = pltpu.make_async_copy(y.at[s, :, :, columns(r)], o.at[:, mine, :], local)
    keep.start()
    copies = []
    for k, peer in others():
        copy = pltpu.make_async_remote_copy(
            src_ref=y.at[peer[0], :, :, columns(peer[1])],
            dst_ref=o.at[:, mine, :],
            send_sem=send.at[k],
            recv_sem=recv.at[k],
            device_id=peer,
            device_id_type=MESH,
        )
        copy.start()
        copies.append(copy)
    for copy in copies:
        copy.wait()
    keep.wait()


def shape(dims, dtype):
    return jax.ShapeDtypeStruct(dims, dtype)


VM = pl.BlockSpec(memory_space=pltpu.VMEM)
SM = pl.BlockSpec(memory_space=pltpu.SMEM)
HB = pl.BlockSpec(memory_space=pl.ANY)


def params(collective):
    return pltpu.CompilerParams(
        collective_id=collective, has_side_effects=True, vmem_limit_bytes=VMEM_LIMIT
    )


def local(
    tokens, cotangent, block_order, lengths, decay, write_gate, gain_attn, w_query, w_key, w_value,
    persist_key, persist_value, w_output, gain_ffn, w_gate, w_up, w_down,
):
    sec, row_id, col = (lax.axis_index(a) for a in ("section", "row", "col"))
    groups = lax.axis_size("col")
    micros, rows, features = tokens.shape
    width = features * lax.axis_size("row")
    own = rows // 8
    blocks = rows // BLOCK
    all_rows = micros * rows
    size = features // 2
    ffh = w_gate.shape[2] // 2
    persist = persist_key.shape[1] * groups

    total_blocks = block_order.shape[1]
    my_blocks = col * blocks + jnp.arange(blocks, dtype=jnp.int32)
    deal_picks = lax.dynamic_slice_in_dim(block_order, col * blocks, blocks, 1)
    matches = (block_order[:, :, None] == my_blocks[None, None, :]).astype(jnp.int32)
    positions = jnp.arange(total_blocks, dtype=jnp.int32)
    back_picks = jnp.sum(matches * positions[None, :, None], axis=1)

    def pick(shard, picks):
        whole = lax.all_gather(shard, "col", axis=1, tiled=True)
        parts = whole.reshape(micros, total_blocks, BLOCK, features)
        chosen = jnp.take_along_axis(parts, picks[:, :, None, None], axis=1)
        return chosen.reshape(micros, rows, features)

    exchange_scratch = [
        pltpu.SemaphoreType.DMA((8,)),
        pltpu.SemaphoreType.DMA((8,)),
        pltpu.SemaphoreType.DMA(()),
    ]
    dealt = pick(jnp.where(sec == 0, tokens, cotangent), deal_picks)
    inputs = pl.pallas_call(
        functools.partial(deal_kernel, own, features),
        out_shape=shape((2, micros, own, width), BF16),
        in_specs=[VM],
        out_specs=VM,
        scratch_shapes=exchange_scratch,
        compiler_params=params(0),
        name="deal",
    )(dealt)

    smalls = (gain_attn[0], gain_ffn[0], persist_key[0], persist_value[0], decay[0], write_gate[0])
    packed = jnp.concatenate([a.astype(F32).reshape(-1) for a in smalls])
    spread = lax.all_gather(packed, ("section", "row", "col"))
    spread = spread.reshape(2, 4, groups, -1)
    offsets, at = [], 0
    for a in smalls:
        offsets.append((at, at + a.size))
        at += a.size
    gains_a = spread[..., offsets[0][0] : offsets[0][1]].reshape(2, 1, width)
    gains_f = spread[..., offsets[1][0] : offsets[1][1]].reshape(2, 1, width)
    line = lax.dynamic_index_in_dim(spread, row_id, 1, False)

    def head(a):
        return lax.dynamic_slice_in_dim(a, sec * (a.shape[-1] // 2), a.shape[-1] // 2, a.ndim - 1)

    def section_of(i, dims):
        return line[..., offsets[i][0] : offsets[i][1]].reshape((2, groups) + dims)

    pks = head(section_of(2, persist_key.shape[1:])).reshape(2, persist, size).astype(BF16)
    pvs = head(section_of(3, persist_value.shape[1:])).reshape(2, persist, size).astype(BF16)
    decays = head(section_of(4, decay.shape[1:]))[..., 0]
    gates = head(section_of(5, write_gate.shape[1:]))
    gates = lax.dynamic_index_in_dim(gates, col, 1, False).reshape(2, all_rows, 1) / BLOCK
    ends = jnp.cumsum(lengths, axis=1)
    is_start = jnp.any(positions[None, :, None] == (ends - lengths)[:, None, :], axis=2)
    is_start = is_start.reshape(micros, groups, blocks).transpose(1, 0, 2)
    keeps = jnp.where(is_start[None], 0.0, decays)
    through = jnp.prod(keeps, axis=3).transpose(0, 2, 1)
    keep = lax.dynamic_index_in_dim(keeps, col, 1, False)

    def halves(w, axis):
        half = w.shape[axis] // 2
        mine = lax.dynamic_slice_in_dim(w, sec * half, half, axis)
        theirs = lax.dynamic_slice_in_dim(w, (1 - sec) * half, half, axis)
        return mine, theirs

    pairs = [halves(w[0], 1) for w in (w_query, w_key, w_value)]
    stacks = [tuple(jnp.concatenate(side, axis=1) for side in zip(*pairs))]
    stacks += [halves(w_output[0], 0), halves(w_gate[0], 1), halves(w_up[0], 1)]
    stacks += [halves(w_down[0], 0)]
    swap = [(0, 1), (1, 0)]

    def layers_of(mine, theirs):
        got = lax.ppermute(theirs, "section", swap)
        return jnp.where(sec == 0, mine, got), jnp.where(sec == 0, got, mine)

    sides = [layers_of(mine, theirs) for mine, theirs in stacks]
    axes = (0, 1, 0, 0, 1)
    weights = [
        [lax.all_gather(pair[l], "col", axis=a, tiled=True) for pair, a in zip(sides, axes)]
        for l in range(2)
    ]

    row_bufs = row_scratch(micros, rows, own, width)
    full_buf = pltpu.VMEM((all_rows, width), BF16)

    def vm(dims, dtype=BF16):
        return pltpu.VMEM(dims, dtype)

    state_bufs = [
        vm((micros * blocks, size, size), F32),
        vm((size, size), F32),
        vm((micros, size, size)),
        vm((micros, groups, size, size)),
    ]
    state_sems = [pltpu.SemaphoreType.DMA((micros, groups))] * 2

    def attn_forward(x, l):
        wqkv, wo = weights[l][:2]
        return pl.pallas_call(
            functools.partial(attn_forward_kernel, micros, rows, own, groups),
            out_shape=(
                shape((all_rows, width), BF16),
                shape((all_rows, 3 * size), BF16),
                shape((micros * blocks, size, size), BF16),
                shape((all_rows, size), BF16),
                shape((micros, own, width), F32),
            ),
            in_specs=[VM, VM, VM, VM, VM, SM, SM, HB, HB],
            out_specs=(HB, HB, HB, HB, VM),
            scratch_shapes=[
                full_buf, vm((width, 3 * size)), vm((size, width)), vm((all_rows, 3 * size)),
                vm((micros * blocks, size, size)), vm((all_rows, size)), *state_bufs,
                *state_sems, *row_bufs, pltpu.SemaphoreType.DMA((16,)),
            ],
            compiler_params=params(1),
            name="attn_forward",
        )(x, gains_a[l], pks[l], pvs[l], gates[l], keep[l], through[l], wqkv, wo)

    def ffn_forward(mid, l):
        wg, wu, wd = weights[l][2:]
        return pl.pallas_call(
            functools.partial(ffn_forward_kernel, micros, rows, own),
            out_shape=(
                shape((all_rows, width), BF16),
                shape((all_rows, ffh), BF16),
                shape((all_rows, ffh), BF16),
                shape((all_rows, ffh), BF16),
                shape((micros, own, width), BF16),
            ),
            in_specs=[VM, VM, HB, HB, HB],
            out_specs=(HB, HB, HB, HB, VM),
            scratch_shapes=[
                full_buf, vm((width, ffh)), vm((width, ffh)), vm((ffh, width)),
                vm((all_rows, ffh)), vm((all_rows, ffh)), vm((all_rows, ffh)),
                *row_bufs, pltpu.SemaphoreType.DMA((16,)),
            ],
            compiler_params=params(2),
            name="ffn_forward",
        )(mid, gains_f[l], wg, wu, wd)

    def ffn_backward(dy, mid, kept, l):
        wg, wu, wd = weights[l][2:]
        return pl.pallas_call(
            functools.partial(ffn_backward_kernel, micros, rows, own),
            out_shape=(
                shape((micros, own, width), F32),
                shape((1, width), F32),
                shape((width, ffh), BF16),
                shape((width, ffh), BF16),
                shape((ffh, width), BF16),
            ),
            in_specs=[VM, VM, VM] + [HB] * 7,
            out_specs=(VM, VM, HB, HB, HB),
            scratch_shapes=[
                full_buf, vm((width, ffh)), vm((width, ffh)), vm((ffh, width)),
                full_buf, *[vm((all_rows, ffh))] * 5,
                vm((width, ffh)), vm((width, ffh)), vm((ffh, width)),
                *row_bufs, pltpu.SemaphoreType.DMA((16,)),
            ],
            compiler_params=params(3),
            name="ffn_backward",
        )(dy, mid, gains_f[l], wg, wu, wd, *kept)

    def attn_backward(dmid, x, kept, l):
        wqkv, wo = weights[l][:2]
        return pl.pallas_call(
            functools.partial(attn_backward_kernel, micros, rows, own, groups),
            out_shape=(
                shape((micros, own, width), BF16),
                shape((1, width), F32),
                shape((persist, size), F32),
                shape((persist, size), F32),
                shape((width, 3 * size), BF16),
                shape((size, width), BF16),
            ),
            in_specs=[VM] * 6 + [SM, SM] + [HB] * 6,
            out_specs=(VM, VM, VM, VM, HB, HB),
            scratch_shapes=[
                full_buf, vm((width, 3 * size)), vm((size, width)), full_buf,
                vm((all_rows, 3 * size)), vm((micros * blocks, size, size)), vm((all_rows, size)),
                vm((all_rows, size)), vm((all_rows, 3 * size)), *state_bufs,
                vm((width, 3 * size)), vm((size, width)),
                *state_sems, *row_bufs, pltpu.SemaphoreType.DMA((16,)),
            ],
            compiler_params=params(4),
            name="attn_backward",
        )(dmid, x, gains_a[l], pks[l], pvs[l], gates[l], keep[l], through[l], wqkv, wo, *kept)

    def restore(pair):
        spread_out = pl.pallas_call(
            functools.partial(undeal_kernel, own, features),
            out_shape=shape((micros, rows, features), BF16),
            in_specs=[VM],
            out_specs=VM,
            scratch_shapes=exchange_scratch,
            compiler_params=params(5),
            name="undeal",
        )(jnp.stack(pair))
        return pick(spread_out, back_picks)

    layer_in = inputs[0]
    kept = []
    outs = []
    for l in range(2):
        *attn_kept, mid = attn_forward(layer_in, l)
        *ffn_kept, layer_out = ffn_forward(mid, l)
        kept.append((layer_in, attn_kept, mid, ffn_kept))
        outs.append(layer_out)
        layer_in = layer_out
    activations = restore(outs)

    upstream = inputs[1]
    input_grads = [None, None]
    gains = [None, None]
    persists = [None, None]
    sums = [None, None]
    for l in (1, 0):
        layer_in, attn_kept, mid, ffn_kept = kept[l]
        dmid, dgain_f, gg, gu, gd = ffn_backward(upstream, mid, ffn_kept, l)
        upstream, dgain_a, dpk, dpv, gqkv, go = attn_backward(dmid, layer_in, attn_kept, l)
        input_grads[l] = upstream
        gains[l] = jnp.concatenate([dgain_a, dgain_f], axis=0)
        persists[l] = jnp.stack([dpk, dpv])
        sums[l] = [
            lax.psum_scatter(g, "col", scatter_dimension=a, tiled=True)
            for g, a in zip((gqkv, go, gg, gu, gd), axes)
        ]
    restored = restore(input_grads)

    def join(first, second, axis):
        mine = jnp.where(sec == 0, first, second)
        got = lax.ppermute(jnp.where(sec == 0, second, first), "section", swap)
        low = jnp.where(sec == 0, mine, got)
        high = jnp.where(sec == 0, got, mine)
        return jnp.concatenate([low, high], axis=axis).astype(F32)[None]

    heads = [
        join(sums[0][0][:, i * size : (i + 1) * size], sums[1][0][:, i * size : (i + 1) * size], 1)
        for i in range(3)
    ]
    grad_out = join(sums[0][1], sums[1][1], 0)
    grad_gate = join(sums[0][2], sums[1][2], 1)
    grad_up = join(sums[0][3], sums[1][3], 1)
    grad_down = join(sums[0][4], sums[1][4], 0)
    gain_sum = lax.psum(jnp.stack(gains), ("section", "row", "col"))
    share = width // (4 * groups)
    my_gain = lax.dynamic_slice_in_dim(
        lax.dynamic_index_in_dim(gain_sum, sec, 0, False), (row_id * groups + col) * share, share, 1
    )
    persist_sum = lax.psum(jnp.stack(persists), "col")
    each = persist // groups
    persist_sum = lax.dynamic_slice_in_dim(persist_sum, col * each, each, 2)
    grad_persist = join(persist_sum[0], persist_sum[1], 2)[0]
    return (
        activations[None],
        restored[None],
        my_gain[0][None],
        heads[0],
        heads[1],
        heads[2],
        grad_persist[0][None],
        grad_persist[1][None],
        grad_out,
        my_gain[1][None],
        grad_gate,
        grad_up,
        grad_down,
    )


def solution(mesh):
    weight = P("section", "col", "row")
    across = P("section", "row", "col")
    gain = P("section", ("row", "col"))
    rows = P("section", None, "col", "row")
    return jax.shard_map(
        local,
        mesh=mesh,
        in_specs=(
            P(None, "col", "row"), P(None, "col", "row"), P(), P(), rows, rows, gain, weight, weight,
            weight, weight, weight, across, gain, weight, weight, across,
        ),
        out_specs=(
            rows, rows, gain, weight, weight, weight, weight, weight, across, gain, weight, weight,
            across,
        ),
        check_vma=False,
    )
```

time: 2370 us -> 898 us (0.38)
  blocking collectives: 843 us -> 252 us
  waiting for transfers between devices: 771 us -> 235 us
  Pallas kernels: 0 us -> 315 us
  other arithmetic: 293 us -> 24.4 us
  matrix products: 241 us -> 0 us
  local copies, waits for them, and re-layouts: 174 us -> 40.9 us
    all_gather x42 -> x10, blocking collectives: 663 us -> 196 us  [local(): lax.all_gather(pair[l], 'col', axis=a, tiled=True)]
    reduce_scatter x27 -> x10, waiting for transfers between devices: 572 us -> 139 us  [local(): lax.psum_scatter(g, 'col', scatter_dimension=a, tiled=True)]
    pallas_call x0 -> x11, Pallas kernels: none -> 315 us  [the longest x2 79.4 us: attn_backward(): pl.pallas_call(functools.partial(attn_backward_kernel, micros, rows, own,...]
    dot_general x200 -> x0, matrix products: 241 us -> none  [the longest x4 19 us: layer_forward(): jnp.dot(ffn_act, w_down, preferred_element_type=jnp.float32)]
    dynamic_update_slice x72 -> x0, other arithmetic: 93.2 us -> none  [mixer_forward(): _, local_after = lax.scan(chain_step, zero_state, (update, keep_rows))]
    psum x16 -> x2, blocking collectives: 147 us -> 55.9 us  [the longest x1 38.2 us: local(): gain_sum = lax.psum(jnp.stack(gains), ('section', 'row', 'col'))]
    all_gather x7 -> x3, waiting for transfers between devices: 177 us -> 89.7 us  [pick(): whole = lax.all_gather(shard, 'col', axis=1, tiled=True)]
    convert_element_type x51 -> x8, other arithmetic: 44.1 us -> 4.08 us  [the longest x7 4.08 us: join(): return jnp.concatenate([low, high], axis=axis).astype(F32)[None]]
  transfers between devices with their start and end apart: 42 -> 27, of which waited for: 30 -> 11; matrix products, arithmetic and copies ran while one was open for 7% -> 6% of each run, Pallas kernels for 0% -> 3%
where the time goes in v1:
time: 898 us; the launch traced here: 888 us
  Pallas kernels  315 us (35%)
  blocking collectives  252 us (28%)
  waiting for transfers between devices  235 us (26%)
  local copies, waits for them, and re-layouts  40.9 us (5%)
  other arithmetic  24.4 us (3%)
  between operations  17.2 us (2%)
    all_gather x10, blocking collectives, local(): lax.all_gather(pair[l], 'col', axis=a, tiled=True)  196 us
    reduce_scatter x10, waiting for transfers between devices, local(): lax.psum_scatter(g, 'col', scatter_dimension=a, tiled=True)  139 us
    all_gather x3, waiting for transfers between devices, pick(): whole = lax.all_gather(shard, 'col', axis=1, tiled=True)  89.7 us
    pallas_call x2, Pallas kernels, attn_backward(): pl.pallas_call(functools.partial(attn_backward_kernel, micros, rows, own,...  79.4 us
    pallas_call x2, Pallas kernels, attn_forward(): pl.pallas_call(functools.partial(attn_forward_kernel, micros, rows, own,...  75.8 us
    pallas_call x2, Pallas kernels, ffn_backward(): pl.pallas_call(functools.partial(ffn_backward_kernel, micros, rows, own),...  63.1 us
    pallas_call x2, Pallas kernels, ffn_forward(): pl.pallas_call(functools.partial(ffn_forward_kernel, micros, rows, own),...  60 us
    psum x1, blocking collectives, local(): gain_sum = lax.psum(jnp.stack(gains), ('section', 'row', 'col'))  38.2 us
  transfers between devices with their start and end apart: 27, of which 11 were waited for; matrix products, arithmetic and copies ran while one was open for 6% of the time, Pallas kernels for 3%

profile of v1, /device:TPU:0, one launch (start us, length us, event | category | flops | bytes accessed | tf_op | source)
XLA Modules:
  0.0 887.9 jit_solution(13763716183966657446)
XLA Ops:
  8.1 1.0 dynamic-slice_bitcast_fusion.7
  9.1 1.0 dynamic-slice_bitcast_fusion.5
  10.6 1.5 dynamic-slice_bitcast_fusion.1
  12.1 1.0 copy.73
  16.9 0.9 broadcast_select_fusion.3
  18.9 0.9 bitcast_select_fusion.6
  19.7 17.3 %all_gather.49.wo_h = bf16[128,1024]{1,0:T(8,128)(2,1)} all-gather(bf16[128,256]{1,0:T(8,128)(2,1)S(1)} %get-tuple-element.193), channel_id=1, replica_groups=mesh['section'=2,'row'=4,'col'=4] {'col'}, dimensions={1}, use_global_device_ids=true | all-gather | bytes 327680 | tf_op jit(solution)/shard_map/all_gather | solution.py:821
  37.0 16.9 %all_gather.54.wo_h = bf16[128,1024]{1,0:T(8,128)(2,1)} all-gather(bf16[128,256]{1,0:T(8,128)(2,1)S(1)} %get-tuple-element.192), channel_id=1, replica_groups=mesh['section'=2,'row'=4,'col'=4] {'col'}, dimensions={1}, use_global_device_ids=true | all-gather | bytes 327680 | tf_op jit(solution)/shard_map/all_gather | solution.py:821
  54.0 1.0 bitcast_select_fusion.2
  54.9 29.6 %all_gather.50.wg_h = bf16[1024,352]{1,0:T(8,128)(2,1)} all-gather(bf16[256,352]{1,0:T(8,128)(2,1)S(1)} %get-tuple-element.183), channel_id=1, replica_groups=mesh['section'=2,'row'=4,'col'=4] {'col'}, dimensions={0}, use_global_device_ids=true | all-gather | bytes 901120 | tf_op jit(solution)/shard_map/all_gather | solution.py:821
  84.6 21.1 %all_gather.51.wu_h = bf16[1024,352]{1,0:T(8,128)(2,1)} all-gather(bf16[256,352]{1,0:T(8,128)(2,1)S(1)} %get-tuple-element.181), channel_id=1, replica_groups=mesh['section'=2,'row'=4,'col'=4] {'col'}, dimensions={0}, use_global_device_ids=true | all-gather | bytes 901120 | tf_op jit(solution)/shard_map/all_gather | solution.py:821
  105.7 1.0 bitcast_select_fusion.4
  106.7 18.7 %all_gather.52.wd_h = bf16[352,1024]{1,0:T(8,128)(2,1)} all-gather(bf16[352,256]{1,0:T(8,128)(2,1)S(1)} %get-tuple-element.169), channel_id=1, replica_groups=mesh['section'=2,'row'=4,'col'=4] {'col'}, dimensions={1}, use_global_device_ids=true | all-gather | bytes 901120 | tf_op jit(solution)/shard_map/all_gather | solution.py:821
  125.4 19.2 %all_gather.55.wg_h = bf16[1024,352]{1,0:T(8,128)(2,1)} all-gather(bf16[256,352]{1,0:T(8,128)(2,1)S(1)} %get-tuple-element.182), channel_id=1, replica_groups=mesh['section'=2,'row'=4,'col'=4] {'col'}, dimensions={0}, use_global_device_ids=true | all-gather | bytes 901120 | tf_op jit(solution)/shard_map/all_gather | solution.py:821
  144.6 18.5 %all_gather.56.wu_h = bf16[1024,352]{1,0:T(8,128)(2,1)} all-gather(bf16[256,352]{1,0:T(8,128)(2,1)S(1)} %get-tuple-element.180), channel_id=1, replica_groups=mesh['section'=2,'row'=4,'col'=4] {'col'}, dimensions={0}, use_global_device_ids=true | all-gather | bytes 901120 | tf_op jit(solution)/shard_map/all_gather | solution.py:821
  163.1 18.4 %all_gather.57.wd_h = bf16[352,1024]{1,0:T(8,128)(2,1)} all-gather(bf16[352,256]{1,0:T(8,128)(2,1)S(1)} %get-tuple-element.168), channel_id=1, replica_groups=mesh['section'=2,'row'=4,'col'=4] {'col'}, dimensions={1}, use_global_device_ids=true | all-gather | bytes 901120 | tf_op jit(solution)/shard_map/all_gather | solution.py:821
  181.5 1.0 broadcast_select_fusion.8
  182.6 20.4 %all_gather.48.wqkv_h = bf16[1024,384]{1,0:T(8,128)(2,1)} all-gather(bf16[256,384]{1,0:T(8,128)(2,1)S(1)} %get-tuple-element.185), channel_id=1, replica_groups=mesh['section'=2,'row'=4,'col'=4] {'col'}, dimensions={0}, use_global_device_ids=true | all-gather | bytes 983040 | tf_op jit(solution)/shard_map/all_gather | solution.py:821
  203.0 16.3 %all_gather.53.wqkv_h = bf16[1024,384]{1,0:T(8,128)(2,1)} all-gather(bf16[256,384]{1,0:T(8,128)(2,1)S(1)} %get-tuple-element.184), channel_id=1, replica_groups=mesh['section'=2,'row'=4,'col'=4] {'col'}, dimensions={0}, use_global_device_ids=true | all-gather | bytes 983040 | tf_op jit(solution)/shard_map/all_gather | solution.py:821
  219.3 1.5 reshape.365
  220.8 4.6 copy.74
  226.2 2.4 slice.179
  229.6 1.6 copy.77
  231.2 2.4 fusion.5
  238.5 2.5 dynamic-slice_multiply_fusion
  242.8 1.1 fusion.6
  243.9 2.3 gather_fusion
  246.2 0.9 broadcast_select_fusion.2
  247.2 11.8 %deal.1 = bf16[2,3,48,1024]{3,2,1,0:T(8,128)(2,1)} custom-call(bf16[3,384,256]{2,1,0:T(8,128)(2,1)} %bitcast.168), custom_call_target="tpu_custom_call" | custom-call | tf_op jit(solution)/shard_map/deal/pallas_call | solution.py:762
  259.0 1.9 slice_bitcast_fusion
  260.9 37.4 %attn_forward.2 = (bf16[1152,1024]{1,0:T(8,128)(2,1)}, bf16[1152,384]{1,0:T(8,128)(2,1)}, bf16[18,128,128]{2,1,0:T(8,128)(2,1)}, bf16[1152,128]{1,0:T(8,128)(2,1)}, f32[3,48,1024]{2,1,0:T(8,128)}) custom-call(bf16[3,48,1024]{2,1,0:T(8,128)(2,1)} %get-tuple-element.161.x, f32[1,1024]{1,0:T(1,128)} %squeeze.44.gain, bf16[16,128]{1,0:T(8,128)(2,1)} %bitcast.182, ...), custom_call_target="tpu_custom_call" | custom-call | tf_op jit(solution)/shard_map/attn_forward/pallas_call | solution.py:841
  298.3 30.0 %ffn_forward.2 = (bf16[1152,1024]{1,0:T(8,128)(2,1)}, bf16[1152,352]{1,0:T(8,128)(2,1)}, bf16[1152,352]{1,0:T(8,128)(2,1)}, bf16[1152,352]{1,0:T(8,128)(2,1)}, bf16[3,48,1024]{2,1,0:T(8,128)(2,1)}) custom-call(f32[3,48,1024]{2,1,0:T(8,128)} %get-tuple-element.56.mid, f32[1,1024]{1,0:T(1,128)} %squeeze.97.gain, bf16[1024,352]{1,0:T(8,128)(2,1)} %all_gather.50.wg_h, ...), custom_call_target="tpu_custom_call" | custom-call | tf_op jit(solution)/shard_map/ffn_forward/pallas_call | solution.py:863
  328.2 38.4 %attn_forward.3 = (bf16[1152,1024]{1,0:T(8,128)(2,1)}, bf16[1152,384]{1,0:T(8,128)(2,1)}, bf16[18,128,128]{2,1,0:T(8,128)(2,1)}, bf16[1152,128]{1,0:T(8,128)(2,1)}, f32[3,48,1024]{2,1,0:T(8,128)}) custom-call(bf16[3,48,1024]{2,1,0:T(8,128)(2,1)} %get-tuple-element.57.x, f32[1,1024]{1,0:T(1,128)} %squeeze.98.gain, bf16[16,128]{1,0:T(8,128)(2,1)} %bitcast.186, ...), custom_call_target="tpu_custom_call" | custom-call | tf_op jit(solution)/shard_map/attn_forward/pallas_call | solution.py:841
  366.7 30.0 %ffn_forward.3 = (bf16[1152,1024]{1,0:T(8,128)(2,1)}, bf16[1152,352]{1,0:T(8,128)(2,1)}, bf16[1152,352]{1,0:T(8,128)(2,1)}, bf16[1152,352]{1,0:T(8,128)(2,1)}, bf16[3,48,1024]{2,1,0:T(8,128)(2,1)}) custom-call(f32[3,48,1024]{2,1,0:T(8,128)} %get-tuple-element.58.mid, f32[1,1024]{1,0:T(1,128)} %squeeze.104.gain, bf16[1024,352]{1,0:T(8,128)(2,1)} %all_gather.55.wg_h, ...), custom_call_target="tpu_custom_call" | custom-call | tf_op jit(solution)/shard_map/ffn_forward/pallas_call | solution.py:863
  396.7 31.7 %ffn_backward.2 = (f32[3,48,1024]{2,1,0:T(8,128)}, f32[1,1024]{1,0:T(1,128)}, bf16[1024,352]{1,0:T(8,128)(2,1)}, bf16[1024,352]{1,0:T(8,128)(2,1)}, bf16[352,1024]{1,0:T(8,128)(2,1)}) custom-call(bf16[3,48,1024]{2,1,0:T(8,128)(2,1)} %get-tuple-element.160.dy, f32[3,48,1024]{2,1,0:T(8,128)} %get-tuple-element.58.mid, f32[1,1024]{1,0:T(1,128)} %squeeze.104.gain, ...), custom_call_target="tpu_custom_call" | custom-call | tf_op jit(solution)/shard_map/ffn_backward/pallas_call | solution.py:885
  428.3 40.1 %attn_backward.2 = (bf16[3,48,1024]{2,1,0:T(8,128)(2,1)}, f32[1,1024]{1,0:T(1,128)}, f32[16,128]{1,0:T(8,128)}, f32[16,128]{1,0:T(8,128)}, bf16[1024,384]{1,0:T(8,128)(2,1)}, /*index=5*/bf16[128,1024]{1,0:T(8,128)(2,1)}) custom-call(f32[3,48,1024]{2,1,0:T(8,128)} %get-tuple-element.64.dmid, bf16[3,48,1024]{2,1,0:T(8,128)(2,1)} %get-tuple-element.57.x, ...), custom_call_target="tpu_custom_call" | custom-call | tf_op jit(solution)/shard_map/attn_backward/pallas_call | solution.py:908
  468.5 31.4 %ffn_backward.3 = (f32[3,48,1024]{2,1,0:T(8,128)}, f32[1,1024]{1,0:T(1,128)}, bf16[1024,352]{1,0:T(8,128)(2,1)}, bf16[1024,352]{1,0:T(8,128)(2,1)}, bf16[352,1024]{1,0:T(8,128)(2,1)}) custom-call(bf16[3,48,1024]{2,1,0:T(8,128)(2,1)} %get-tuple-element.69.dy, f32[3,48,1024]{2,1,0:T(8,128)} %get-tuple-element.56.mid, f32[1,1024]{1,0:T(1,128)} %squeeze.97.gain, ...), custom_call_target="tpu_custom_call" | custom-call | tf_op jit(solution)/shard_map/ffn_backward/pallas_call | solution.py:885
  499.9 39.3 %attn_backward.3 = (bf16[3,48,1024]{2,1,0:T(8,128)(2,1)}, f32[1,1024]{1,0:T(1,128)}, f32[16,128]{1,0:T(8,128)}, f32[16,128]{1,0:T(8,128)}, bf16[1024,384]{1,0:T(8,128)(2,1)}, /*index=5*/bf16[128,1024]{1,0:T(8,128)(2,1)}) custom-call(f32[3,48,1024]{2,1,0:T(8,128)} %get-tuple-element.74.dmid, bf16[3,48,1024]{2,1,0:T(8,128)(2,1)} %get-tuple-element.161.x, ...), custom_call_target="tpu_custom_call" | custom-call | tf_op jit(solution)/shard_map/attn_backward/pallas_call | solution.py:908
  545.3 0.9 pad_maximum_fusion.y
  546.1 11.8 %undeal.2 = bf16[3,384,256]{2,1,0:T(8,128)(2,1)} custom-call(bf16[2,3,48,1024]{3,2,1,0:T(8,128)(2,1)} %pad_maximum_fusion.y), custom_call_target="tpu_custom_call" | custom-call | tf_op jit(solution)/shard_map/undeal/pallas_call | solution.py:932
  558.5 17.6 %psum.15 = f32[2,2,16,128]{3,2,1,0:T(8,128)S(1)} all-reduce(f32[2,2,16,128]{3,2,1,0:T(8,128)S(1)} %pad_maximum_fusion.4), channel_id=1, replica_groups=mesh['section'=2,'row'=4,'col'=4] {'col'}, use_global_device_ids=true, to_apply=%region_7.9 | all-reduce | flops 8192 | bytes 65536 | tf_op jit(solution)/shard_map/psum | solution.py:992
  576.3 38.2 %psum.14 = f32[2,2,1024]{2,1,0:T(2,128)S(1)} all-reduce(f32[2,2,1024]{2,1,0:T(2,128)S(1)} %pad_maximum_fusion.5), channel_id=1, replica_groups=mesh['section'=2,'row'=4,'col'=4] {'section','row','col'}, use_global_device_ids=true, to_apply=%region_4.6 | all-reduce | flops 4096 | bytes 32768 | tf_op jit(solution)/shard_map/psum | solution.py:987
  615.1 0.9 pad_maximum_fusion.1.y
  616.0 12.6 %undeal.3 = bf16[3,384,256]{2,1,0:T(8,128)(2,1)} custom-call(bf16[2,3,48,1024]{3,2,1,0:T(8,128)(2,1)} %pad_maximum_fusion.1.y), custom_call_target="tpu_custom_call" | custom-call | tf_op jit(solution)/shard_map/undeal/pallas_call | solution.py:932
  632.5 1.0 broadcast_select_fusion.10
  633.9 16.4 %reduce-scatter.23.cloned.1.call-done = bf16[256,352]{1,0:T(8,128)(2,1)} async-done(((bf16[1024,352]{1,0:T(8,128)(2,1)}), bf16[256,352]{1,0:T(8,128)(2,1)}) %reduce-scatter.23.cloned.1.call-update) | async-done | bytes 180240 | tf_op jit(solution)/shard_map/reduce_scatter | solution.py:967
  650.3 24.8 %reduce-scatter.25.cloned.1.call-done = bf16[256,352]{1,0:T(8,128)(2,1)} async-done(((bf16[1024,352]{1,0:T(8,128)(2,1)}), bf16[256,352]{1,0:T(8,128)(2,1)}) %reduce-scatter.25.cloned.1.call-update) | async-done | bytes 180240 | tf_op jit(solution)/shard_map/reduce_scatter | solution.py:967
  675.1 1.0 broadcast_select_fusion.4
  676.2 23.8 %reduce-scatter.19.cloned.1.call-done = bf16[256,352]{1,0:T(8,128)(2,1)} async-done(((bf16[1024,352]{1,0:T(8,128)(2,1)}), bf16[256,352]{1,0:T(8,128)(2,1)}) %reduce-scatter.19.cloned.1.call-update) | async-done | bytes 180240 | tf_op jit(solution)/shard_map/reduce_scatter | solution.py:967
  700.0 24.8 %reduce-scatter.21.cloned.1.call-done = bf16[256,352]{1,0:T(8,128)(2,1)} async-done(((bf16[1024,352]{1,0:T(8,128)(2,1)}), bf16[256,352]{1,0:T(8,128)(2,1)}) %reduce-scatter.21.cloned.1.call-update) | async-done | bytes 180240 | tf_op jit(solution)/shard_map/reduce_scatter | solution.py:967
  724.8 1.0 broadcast_select_fusion.6
  725.8 23.9 %reduce-scatter.11.cloned.1.call-done = bf16[256,384]{1,0:T(8,128)(2,1)} async-done(((bf16[1024,384]{1,0:T(8,128)(2,1)}), bf16[256,384]{1,0:T(8,128)(2,1)}) %reduce-scatter.11.cloned.1.call-update) | async-done | bytes 196624 | tf_op jit(solution)/shard_map/reduce_scatter | solution.py:967
  749.8 24.8 %reduce-scatter.13.cloned.1.call-done = bf16[256,384]{1,0:T(8,128)(2,1)} async-done(((bf16[1024,384]{1,0:T(8,128)(2,1)}), bf16[256,384]{1,0:T(8,128)(2,1)}) %reduce-scatter.13.cloned.1.call-update) | async-done | bytes 196624 | tf_op jit(solution)/shard_map/reduce_scatter | solution.py:967
  774.6 0.9 broadcast_select_fusion.12
  775.5 1.0 select_bitcast_fusion.1
  776.5 1.0 select_bitcast_fusion.3
  777.7 1.1 copy.88
  779.0 1.1 copy.87
  780.1 0.9 maximum_convert_fusion.2
  784.4 41.4 %all-gather.7.cloned.1.call-done = bf16[3,1536,256]{2,1,0:T(8,128)(2,1)} async-done(((bf16[3,384,256]{2,1,0:T(8,128)(2,1)}), bf16[3,1536,256]{2,1,0:T(8,128)(2,1)}) %all-gather.7.cloned.1.call-update) | async-done | bytes 2359312 | tf_op jit(solution)/shard_map/all_gather | solution.py:751
  825.8 2.3 gather_fusion.1
  828.1 48.3 %all-gather.9.cloned.1.call-done = bf16[3,1536,256]{2,1,0:T(8,128)(2,1)} async-done(((bf16[3,384,256]{2,1,0:T(8,128)(2,1)}), bf16[3,1536,256]{2,1,0:T(8,128)(2,1)}) %all-gather.9.cloned.1.call-update) | async-done | bytes 2359312 | tf_op jit(solution)/shard_map/all_gather | solution.py:751
  876.4 2.3 gather_fusion.2
  878.7 1.2 broadcast_select_fusion
  (199 shorter events, 28.6 us)
Async XLA Ops:
  8.0 5.5 copy-start.27
  8.0 5.7 copy-start.28
  8.0 5.7 copy-start.29
  8.0 5.7 copy-start.31
  8.1 5.7 copy-start.30
  8.1 7.2 copy-start.13
  8.1 7.2 copy-start.12
  8.1 211.2 %all-reduce.3.cloned.1.call-start = ((), (), s32[]{:S(2)}) async-start(), calls=%async_computation.23 | async-start | bytes 1163264
  10.1 171.4 %collective-permute-start = (bf16[256,384]{1,0:T(8,128)(2,1)S(1)}, bf16[256,384]{1,0:T(8,128)(2,1)}, u32[]{:S(2)}, u32[]{:S(2)}) collective-permute-start(bf16[256,384]{1,0:T(8,128)(2,1)S(1)} %pad_maximum_fusion.3), channel_id=1, source_target_pairs={{0,16},{16,0},{1,17},{17,1},{2,18},{18,2},{3,19},{19,3},{4,20},{20... | collective-permute-start | bytes 589832 | tf_op jit(solution)/shard_map/ppermute | solution.py:815
  12.1 6.8 collective-permute-start.1
  12.1 4.2 copy-start.11
  13.1 3.7 copy-start.9
  13.2 3.7 copy-start.10
  14.4 0.8 copy-start.2
  15.2 228.7 %all-gather.5.cloned.1.call-start = ((), (), s32[]{:S(2)}) async-start(), calls=%async_computation.10 | async-start | bytes 2949120 | tf_op jit(solution)/shard_map/all_gather | solution.py:751
  15.3 2.6 copy-start.17
  15.3 2.8 copy-start.18
  15.4 3.5 copy-start.16
  15.5 38.4 %collective-permute-start.2 = (bf16[256,352]{1,0:T(8,128)(2,1)S(1)}, bf16[256,352]{1,0:T(8,128)(2,1)}, u32[]{:S(2)}, u32[]{:S(2)}) collective-permute-start(bf16[256,352]{1,0:T(8,128)(2,1)S(1)} %bitcast.177), channel_id=1, source_target_pairs={{0,16},{16,0},{1,17},{17,1},{2,18},{18,2},{3,19},{19,3},{4,20},{20... | collective-permute-start | bytes 540680 | tf_op jit(solution)/shard_map/ppermute | solution.py:815
  16.2 68.3 %collective-permute-start.3 = (bf16[256,352]{1,0:T(8,128)(2,1)S(1)}, bf16[256,352]{1,0:T(8,128)(2,1)S(1)}, u32[]{:S(2)}, u32[]{:S(2)}) collective-permute-start(bf16[256,352]{1,0:T(8,128)(2,1)S(1)} %bitcast.176), channel_id=1, source_target_pairs={{0,16},{16,0},{1,17},{17,1},{2,18},{18,2},{3,19},{19,3},{4,20},{20... | collective-permute-start | bytes 540680 | tf_op jit(solution)/shard_map/ppermute | solution.py:815
  16.4 89.4 %collective-permute-start.4 = (bf16[352,256]{1,0:T(8,128)(2,1)S(1)}, bf16[352,256]{1,0:T(8,128)(2,1)}, u32[]{:S(2)}, u32[]{:S(2)}) collective-permute-start(bf16[352,256]{1,0:T(8,128)(2,1)S(1)} %dynamic-slice_bitcast_fusion), channel_id=1, source_target_pairs={{0,16},{16,0},{1,17},{17,1},{2,18},{18,2},{3,19},{19,3},{4,20},{20... | collective-permute-start | bytes 540680 | tf_op jit(solution)/shard_map/ppermute | solution.py:815
  17.8 610.9 %reduce-scatter.15.cloned.1.call-start = ((), (), s32[]{:S(2)}) async-start(), calls=%async_computation.15 | async-start | bytes 327680 | tf_op jit(solution)/shard_map/reduce_scatter | solution.py:967
  220.8 4.7 copy-start.4
  231.2 7.3 copy-start
  539.3 89.5 %reduce-scatter.17.cloned.1.call-start = ((), (), s32[]{:S(2)}) async-start(), calls=%async_computation.16 | async-start | bytes 327680 | tf_op jit(solution)/shard_map/reduce_scatter | solution.py:967
  539.8 92.7 %reduce-scatter.27.cloned.1.call-start = ((), (), s32[]{:S(2)}) async-start(), calls=%async_computation.21 | async-start | bytes 901120 | tf_op jit(solution)/shard_map/reduce_scatter | solution.py:967
  540.6 92.0 %reduce-scatter.29.cloned.1.call-start = ((), (), s32[]{:S(2)}) async-start(), calls=%async_computation.22 | async-start | bytes 901120 | tf_op jit(solution)/shard_map/reduce_scatter | solution.py:967
  541.3 109.0 %reduce-scatter.23.cloned.1.call-start = ((), (), s32[]{:S(2)}) async-start(), calls=%async_computation.19 | async-start | bytes 983040 | tf_op jit(solution)/shard_map/reduce_scatter | solution.py:967
  541.4 3.9 copy-start.1
  541.4 3.9 copy-start.15
  542.1 133.1 %reduce-scatter.25.cloned.1.call-start = ((), (), s32[]{:S(2)}) async-start(), calls=%async_computation.20 | async-start | bytes 983040 | tf_op jit(solution)/shard_map/reduce_scatter | solution.py:967
  542.7 157.3 %reduce-scatter.19.cloned.1.call-start = ((), (), s32[]{:S(2)}) async-start(), calls=%async_computation.17 | async-start | bytes 983040 | tf_op jit(solution)/shard_map/reduce_scatter | solution.py:967
  543.2 181.5 %reduce-scatter.21.cloned.1.call-start = ((), (), s32[]{:S(2)}) async-start(), calls=%async_computation.18 | async-start | bytes 983040 | tf_op jit(solution)/shard_map/reduce_scatter | solution.py:967
  543.8 14.6 %copy-start.21 = (f32[16,128]{1,0:T(8,128)S(1)}, f32[16,128]{1,0:T(8,128)}, u32[]{:S(2)}) copy-start(f32[16,128]{1,0:T(8,128)} %get-tuple-element.86) | copy-start | bytes 24580
  543.8 14.6 %copy-start.22 = (f32[16,128]{1,0:T(8,128)S(1)}, f32[16,128]{1,0:T(8,128)}, u32[]{:S(2)}) copy-start(f32[16,128]{1,0:T(8,128)} %get-tuple-element.87) | copy-start | bytes 24580
  543.8 14.6 %copy-start.19 = (f32[16,128]{1,0:T(8,128)S(1)}, f32[16,128]{1,0:T(8,128)}, u32[]{:S(2)}) copy-start(f32[16,128]{1,0:T(8,128)} %get-tuple-element.88) | copy-start | bytes 24580
  543.8 14.6 %copy-start.20 = (f32[16,128]{1,0:T(8,128)S(1)}, f32[16,128]{1,0:T(8,128)}, u32[]{:S(2)}) copy-start(f32[16,128]{1,0:T(8,128)} %get-tuple-element.89) | copy-start | bytes 24580
  543.9 205.9 %reduce-scatter.11.cloned.1.call-start = ((), (), s32[]{:S(2)}) async-start(), calls=%async_computation.13 | async-start | bytes 983040 | tf_op jit(solution)/shard_map/reduce_scatter | solution.py:967
  543.9 32.3 %copy-start.25 = (f32[1,1024]{1,0:T(1,128)S(1)}, f32[1,1024]{1,0:T(1,128)}, u32[]{:S(2)}) copy-start(f32[1,1024]{1,0:T(1,128)} %get-tuple-element.81) | copy-start | bytes 12292
  543.9 32.3 %copy-start.26 = (f32[1,1024]{1,0:T(1,128)S(1)}, f32[1,1024]{1,0:T(1,128)}, u32[]{:S(2)}) copy-start(f32[1,1024]{1,0:T(1,128)} %get-tuple-element.80) | copy-start | bytes 12292
  543.9 32.3 %copy-start.23 = (f32[1,1024]{1,0:T(1,128)S(1)}, f32[1,1024]{1,0:T(1,128)}, u32[]{:S(2)}) copy-start(f32[1,1024]{1,0:T(1,128)} %get-tuple-element.83) | copy-start | bytes 12292
  543.9 32.3 %copy-start.24 = (f32[1,1024]{1,0:T(1,128)S(1)}, f32[1,1024]{1,0:T(1,128)}, u32[]{:S(2)}) copy-start(f32[1,1024]{1,0:T(1,128)} %get-tuple-element.82) | copy-start | bytes 12292
  543.9 71.2 %copy-start.3 = (bf16[3,48,1024]{2,1,0:T(8,128)(2,1)S(1)}, bf16[3,48,1024]{2,1,0:T(8,128)(2,1)}, u32[]{:S(2)}) copy-start(bf16[3,48,1024]{2,1,0:T(8,128)(2,1)} %get-tuple-element.69.dy) | copy-start | bytes 884740
  544.0 71.2 %copy-start.14 = (bf16[3,48,1024]{2,1,0:T(8,128)(2,1)S(1)}, bf16[3,48,1024]{2,1,0:T(8,128)(2,1)}, u32[]{:S(2)}) copy-start(bf16[3,48,1024]{2,1,0:T(8,128)(2,1)} %get-tuple-element.79) | copy-start | bytes 884740
  544.6 230.0 %reduce-scatter.13.cloned.1.call-start = ((), (), s32[]{:S(2)}) async-start(), calls=%async_computation.14 | async-start | bytes 983040 | tf_op jit(solution)/shard_map/reduce_scatter | solution.py:967
  545.2 280.6 %all-gather.7.cloned.1.call-start = ((), (), s32[]{:S(2)}) async-start(), calls=%async_computation.11 | async-start | bytes 2949120 | tf_op jit(solution)/shard_map/all_gather | solution.py:751
  558.0 318.4 %all-gather.9.cloned.1.call-start = ((), (), s32[]{:S(2)}) async-start(), calls=%async_computation.12 | async-start | bytes 2949120 | tf_op jit(solution)/shard_map/all_gather | solution.py:751
  576.1 52.6 %collective-permute-start.8 = (f32[2,4,128]{2,1,0:T(4,128)S(1)}, f32[2,4,128]{2,1,0:T(4,128)S(1)}, u32[]{:S(2)}, u32[]{:S(2)}) collective-permute-start(f32[2,4,128]{2,1,0:T(4,128)S(1)} %select_bitcast_fusion.14), channel_id=1, source_target_pairs={{0,16},{16,0},{1,17},{17,1},{2,18},{18,2},{3,19},{19,3},{4,20},{20... | collective-permute-start | bytes 12296 | tf_op jit(solution)/shard_map/ppermute | solution.py:974
  629.6 1.3 collective-permute-start.9
  633.5 146.6 %collective-permute-start.12 = (bf16[352,256]{1,0:T(8,128)(2,1)S(1)}, bf16[352,256]{1,0:T(8,128)(2,1)S(1)}, u32[]{:S(2)}, u32[]{:S(2)}) collective-permute-start(bf16[352,256]{1,0:T(8,128)(2,1)S(1)} %broadcast_select_fusion.10), channel_id=1, source_target_pairs={{0,16},{16,0},{1,17},{17,1},{2,18},{18,2},{3,19},{19,3},{4,20},{20... | collective-permute-start | bytes 540680 | tf_op jit(solution)/shard_map/ppermute | solution.py:974
  676.1 99.4 %collective-permute-start.11 = (bf16[256,352]{1,0:T(8,128)(2,1)S(1)}, bf16[256,352]{1,0:T(8,128)(2,1)S(1)}, u32[]{:S(2)}, u32[]{:S(2)}) collective-permute-start(bf16[256,352]{1,0:T(8,128)(2,1)S(1)} %broadcast_select_fusion.4), channel_id=1, source_target_pairs={{0,16},{16,0},{1,17},{17,1},{2,18},{18,2},{3,19},{19,3},{4,20},{20... | collective-permute-start | bytes 540680 | tf_op jit(solution)/shard_map/ppermute | solution.py:974
  725.7 50.8 %collective-permute-start.10 = (bf16[256,352]{1,0:T(8,128)(2,1)S(1)}, bf16[256,352]{1,0:T(8,128)(2,1)S(1)}, u32[]{:S(2)}, u32[]{:S(2)}) collective-permute-start(bf16[256,352]{1,0:T(8,128)(2,1)S(1)} %broadcast_select_fusion.6), channel_id=1, source_target_pairs={{0,16},{16,0},{1,17},{17,1},{2,18},{18,2},{3,19},{19,3},{4,20},{20... | collective-permute-start | bytes 540680 | tf_op jit(solution)/shard_map/ppermute | solution.py:974
  775.5 5.6 collective-permute-start.7
  777.7 2.4 copy-start.7
  777.7 2.4 copy-start.8
  778.8 2.2 copy-start.5
  778.8 2.2 copy-start.6
  781.1 1.5 collective-permute-start.5
  781.6 1.3 collective-permute-start.6
Sparse Core Ops, SparseCore 0:
  15.3 187.8 all-reduce.2
Sparse Core Ops, SparseCore 1:
  17.9 76.2 all-gather.4
  539.3 18.1 reduce-scatter.14
  559.7 18.0 reduce-scatter.16
  580.1 21.2 reduce-scatter.26
  603.8 21.9 reduce-scatter.28
  628.2 22.1 reduce-scatter.22
  652.6 22.5 reduce-scatter.24
  677.4 22.5 reduce-scatter.18
  702.2 22.5 reduce-scatter.20
  727.2 22.5 reduce-scatter.10
  752.0 22.5 reduce-scatter.12
  776.2 49.5 all-gather.6
  827.3 49.0 all-gather.8

commit v2 on v1

v2 whole, which is shorter than its diff:
```python
from types import SimpleNamespace

import jax
import jax.numpy as jnp
from jax import lax
from jax.experimental import pallas as pl
from jax.experimental.pallas import tpu as pltpu
from jax.sharding import PartitionSpec as P

BLOCK = 64
EPS = 1e-06
MESH = pl.DeviceIdType.MESH
F32 = jnp.float32
BF16 = jnp.bfloat16
VMEM_LIMIT = 56 << 20
N_AG, N_RS = 8, 7


def dot(a, b, ca=1, cb=0):
    return lax.dot_general(a, b, (((ca,), (cb,)), ((), ())), preferred_element_type=F32)


class Rows:
    def __init__(self, rows, own, width, send, recv):
        self.rows, self.own, self.width, self.half = rows, own, width, width // 2
        self.send, self.recv = send, recv
        self.s, self.r, self.c = (lax.axis_index(a) for a in ("section", "row", "col"))
        self.rx = self.r + 1 - 2 * lax.rem(self.r, 2)
        self.ry = lax.rem(self.r + 2, 4)
        self.rd = lax.rem(self.rx + 2, 4)
        self.x = (self.s, self.rx, self.c)
        self.y = (self.s, self.ry, self.c)
        self.sib = (1 - self.s, self.r, self.c)
        self.started = []

    def greet(self, others=()):
        barrier = pltpu.get_barrier_semaphore()
        peers = [self.x, self.y, self.sib] + list(others)
        for peer in peers:
            pl.semaphore_signal(barrier, inc=1, device_id=peer, device_id_type=MESH)
        pl.semaphore_wait(barrier, len(peers))

    def copy(self, src, dst, m, k, peer):
        return pltpu.make_async_remote_copy(
            src_ref=src,
            dst_ref=dst,
            send_sem=self.send.at[m, k],
            recv_sem=self.recv.at[m, k],
            device_id=peer,
            device_id_type=MESH,
        )

    def go(self, copy):
        copy.start()
        self.started.append(copy)

    def finish(self):
        for copy in self.started:
            copy.wait_send()

    def span(self, m, s, r):
        return pl.ds(pl.multiple_of(m * self.rows + (s * 4 + r) * self.own, 16), self.own)

    def ag_copy(self, full, m, k):
        left, right = pl.ds(0, self.half), pl.ds(self.half, self.half)
        mine, atx, aty, atd = (
            self.span(m, self.s, r) for r in (self.r, self.rx, self.ry, self.rd)
        )
        if k == 0:
            return self.copy(full.at[mine, :], full.at[mine, :], m, 0, self.x)
        if k == 1:
            return self.copy(full.at[mine, :], full.at[mine, :], m, 1, self.y)
        if k == 2:
            return self.copy(full.at[mine, :], full.at[mine, :], m, 2, self.sib)
        if k == 3:
            return self.copy(full.at[atx, left], full.at[atx, left], m, 3, self.y)
        if k == 4:
            return self.copy(full.at[aty, right], full.at[aty, right], m, 4, self.x)
        if k == 5:
            return self.copy(full.at[atx, :], full.at[atx, :], m, 5, self.sib)
        if k == 6:
            return self.copy(full.at[aty, :], full.at[aty, :], m, 6, self.sib)
        return self.copy(full.at[atd, :], full.at[atd, :], m, 7, self.sib)

    def ag_start(self, full, m):
        for k in (0, 1, 2):
            self.go(self.ag_copy(full, m, k))

    def ag_pass(self, full, m):
        self.ag_copy(full, m, 0).wait_recv()
        self.go(self.ag_copy(full, m, 3))
        self.go(self.ag_copy(full, m, 5))
        self.ag_copy(full, m, 1).wait_recv()
        self.go(self.ag_copy(full, m, 4))
        self.go(self.ag_copy(full, m, 6))

    def ag_diag(self, full, m):
        self.ag_copy(full, m, 3).wait_recv()
        self.ag_copy(full, m, 4).wait_recv()
        self.go(self.ag_copy(full, m, 7))

    def ag_wait(self, full, m):
        for k in (2, 5, 6, 7):
            self.ag_copy(full, m, k).wait_recv()

    def rs_copy(self, m, k):
        part, pair, both, transit, final = self.buffers
        left, right = pl.ds(0, self.half), pl.ds(self.half, self.half)
        if k == 8:
            other = pl.ds(
                pl.multiple_of(m * self.rows + (1 - self.s) * 4 * self.own, 16), 4 * self.own
            )
            return self.copy(part.at[other, :], pair.at[m], m, 8, self.sib)
        if k == 9:
            return self.copy(both.at[m, self.rd, :, left], transit.at[m, 0], m, 9, self.x)
        if k == 10:
            return self.copy(both.at[m, self.rd, :, right], transit.at[m, 1], m, 10, self.y)
        if k == 11:
            return self.copy(both.at[m, self.rx, :, left], final.at[m, 0, :, left], m, 11, self.x)
        if k == 12:
            return self.copy(both.at[m, self.ry, :, right], final.at[m, 1, :, right], m, 12, self.y)
        if k == 13:
            return self.copy(both.at[m, self.ry, :, left], final.at[m, 1, :, left], m, 13, self.y)
        return self.copy(both.at[m, self.rx, :, right], final.at[m, 0, :, right], m, 14, self.x)

    def rs_start(self, m):
        self.go(self.rs_copy(m, 8))

    def rs_pair(self, m):
        part, pair, both, _, _ = self.buffers
        self.rs_copy(m, 8).wait_recv()
        for r in range(4):
            mine = part[self.span(m, self.s, r), :].astype(F32)
            theirs = pair[m, r * self.own : (r + 1) * self.own, :].astype(F32)
            both[m, r] = (mine + theirs).astype(BF16)
        for k in (9, 10, 11, 12):
            self.go(self.rs_copy(m, k))

    def rs_transit(self, m):
        _, _, both, transit, _ = self.buffers
        left, right = pl.ds(0, self.half), pl.ds(self.half, self.half)
        self.rs_copy(m, 9).wait_recv()
        total = both[m, self.ry, :, left].astype(F32) + transit[m, 0].astype(F32)
        both[m, self.ry, :, left] = total.astype(BF16)
        self.go(self.rs_copy(m, 13))
        self.rs_copy(m, 10).wait_recv()
        total = both[m, self.rx, :, right].astype(F32) + transit[m, 1].astype(F32)
        both[m, self.rx, :, right] = total.astype(BF16)
        self.go(self.rs_copy(m, 14))

    def rs_result(self, m):
        _, _, both, _, final = self.buffers
        for k in (11, 12, 13, 14):
            self.rs_copy(m, k).wait_recv()
        return both[m, self.r].astype(F32) + final[m, 0].astype(F32) + final[m, 1].astype(F32)


class Local:
    def __init__(self, sems):
        self.sems, self.used, self.open = sems, 0, []

    def start(self, src, dst):
        copy = pltpu.make_async_copy(src, dst, self.sems.at[self.used])
        self.used += 1
        copy.start()
        self.open.append(copy)
        return copy

    def wait(self, copy):
        copy.wait()
        self.open.remove(copy)

    def finish(self):
        for copy in list(self.open):
            copy.wait()


def inv_rms(values):
    return lax.rsqrt(jnp.mean(values * values, axis=1, keepdims=True) + EPS)


def norm_to(full, gain, values, span):
    full[span, :] = (values * inv_rms(values) * gain).astype(BF16)


def norm_back(values, gain, grad):
    scale = inv_rms(values)
    weighted = grad * gain
    inner = jnp.mean(weighted * values, axis=1, keepdims=True)
    back = scale * weighted - values * (scale * scale * scale * inner)
    return back, jnp.sum(grad * values * scale, axis=0, keepdims=True)


def wait_both(copies):
    for condition, copy in copies:

        @pl.when(condition)
        def _(copy=copy):
            copy.wait_send()


class Side:
    def __init__(self, tag):
        self.tag = tag

    def ref(self, name):
        return getattr(self.ns, self.tag + name)

    def bind(self, ns, row, groups):
        self.ns, self.row, self.c, self.groups = ns, row, row.c, groups
        self.sent = []

    def when(self, condition, copy):
        @pl.when(condition)
        def _():
            copy.start()

        self.sent.append((condition, copy))

    def arrived(self, condition, copy):
        @pl.when(condition)
        def _():
            copy.wait_recv()

    def remote(self, src, dst, send, recv, to):
        return pltpu.make_async_remote_copy(
            src_ref=src,
            dst_ref=dst,
            send_sem=send,
            recv_sem=recv,
            device_id=(self.row.s, self.row.r, to),
            device_id_type=MESH,
        )


def part_of(ref, at, per, axis):
    where = pl.ds(pl.multiple_of(at * per, per), per)
    return ref.at[(slice(None),) * axis + (where,)]


class Gather(Side):
    def __init__(self, tag, array, dims, groups, axis, view=None, home=None):
        super().__init__(tag)
        self.array, self.axis, self.view, self.home = array, axis, view, home
        self.per = dims[axis]
        self.dims = dims[:axis] + (dims[axis] * groups,) + dims[axis + 1 :]

    def declare(self, ins, outs, scratch, groups):
        if self.array is not None:
            ins[self.tag + "src"] = (self.array, HB)
        if self.home is None:
            outs[self.tag + "dst"] = (self.dims, BF16, HB)
        else:
            scratch[self.tag + "dst"] = pltpu.VMEM(self.dims, BF16)
        scratch[self.tag + "send"] = pltpu.SemaphoreType.DMA((2, groups))
        scratch[self.tag + "recv"] = pltpu.SemaphoreType.DMA((groups,))
        scratch[self.tag + "own"] = pltpu.SemaphoreType.DMA((1,))

    def slot(self, j):
        return part_of(self.ref("dst"), jnp.clip(j, 0, self.groups - 1), self.per, self.axis)

    def source(self):
        return self.view(self.ns, self.row) if self.view else self.ref("src")

    def move(self, j, side, src=None):
        to = jnp.clip(self.c + (1 - 2 * side), 0, self.groups - 1)
        j = jnp.clip(j, 0, self.groups - 1)
        src = self.slot(j) if src is None else src
        return self.remote(
            src, self.slot(j), self.ref("send").at[side, j], self.ref("recv").at[j], to
        )

    def start(self):
        c, n = self.c, self.groups
        self.at, self.done = 1, False
        self.own = pltpu.make_async_copy(self.source(), self.slot(c), self.ref("own").at[0])
        self.own.start()
        self.when(c + 1 < n, self.move(c, 0, self.source()))
        self.when(c >= 1, self.move(c, 1, self.source()))

    def step(self):
        c, n, k = self.c, self.groups, self.at
        if k < n:
            self.arrived(c >= k, self.move(c - k, 0))
            self.arrived(c + k < n, self.move(c + k, 1))
            if k < n - 1:
                self.when((c >= k) & (c + 1 < n), self.move(c - k, 0))
                self.when((c + k < n) & (c >= 1), self.move(c + k, 1))
        self.at += 1

    def finish(self):
        if not self.done:
            while self.at < self.groups:
                self.step()
            self.own.wait()
            self.done = True

    def drain(self):
        wait_both(self.sent)


class Total(Side):
    def __init__(self, tag, parts, groups, span=None, home=None):
        super().__init__(tag)
        self.parts, self.span, self.home = parts, span, home
        self.per = parts.shape[1] // groups
        self.count = span[1] if span else parts.shape[0]
        self.dims = (self.count, self.per, parts.shape[2])

    def declare(self, ins, outs, scratch, groups):
        if self.home is None:
            outs[self.tag + "sum"] = (self.dims, BF16, VM)
        else:
            scratch[self.tag + "sum"] = pltpu.VMEM(self.dims, BF16)
        ins[self.tag + "parts"] = (self.parts, HB)
        whole = (self.count, self.per * groups, self.dims[2])
        scratch[self.tag + "mine"] = pltpu.VMEM(whole, BF16)
        scratch[self.tag + "box"] = pltpu.VMEM((2, groups) + self.dims, BF16)
        scratch[self.tag + "send"] = pltpu.SemaphoreType.DMA((2, groups))
        scratch[self.tag + "recv"] = pltpu.SemaphoreType.DMA((2, groups))
        scratch[self.tag + "load"] = pltpu.SemaphoreType.DMA((1,))

    def clip(self, j):
        return jnp.clip(j, 0, self.groups - 1)

    def piece(self, ref, d, p=None):
        d = self.clip(d)
        where = pl.ds(pl.multiple_of(d * self.per, self.per), self.per)
        return ref.at[:, where, :] if p is None else ref[p, where, :]

    def source(self):
        parts = self.ref("parts")
        return parts.at[pl.ds(*self.span)] if self.span else parts

    def move(self, side, d, src):
        d = self.clip(d)
        to = self.clip(self.c + (1 - 2 * side))
        return self.remote(
            src,
            self.ref("box").at[side, d],
            self.ref("send").at[side, d],
            self.ref("recv").at[side, d],
            to,
        )

    def boxed(self, side, d):
        return self.ref("box").at[side, self.clip(d)]

    def start(self):
        c, n = self.c, self.groups
        self.at, self.done = 1, False
        self.load = pltpu.make_async_copy(self.source(), self.ref("mine"), self.ref("load").at[0])
        self.load.start()
        self.ends(0)

    def ends(self, t):
        c, n = self.c, self.groups
        self.when(c == 0, self.move(0, n - 1 - t, self.piece(self.source(), n - 1 - t)))
        self.when(c == n - 1, self.move(1, t, self.piece(self.source(), t)))

    def step(self):
        c, n, t = self.c, self.groups, self.at
        box, mine = self.ref("box"), self.ref("mine")
        if t == 1:
            self.load.wait()
        if t < n - 1:
            self.ends(t)
            for side, place, d in ((0, c, n - 1 - t + c), (1, n - 1 - c, t + c - (n - 1))):
                here = (place >= 1) & (place <= t)
                self.arrived(here, self.move(side, d, self.boxed(side, d)))

                @pl.when(here)
                def _(side=side, d=d):
                    for p in range(self.count):
                        total = self.piece(mine, d, p).astype(F32)
                        total = total + box[side, self.clip(d), p].astype(F32)
                        box[side, self.clip(d), p] = total.astype(BF16)

                self.when(here, self.move(side, d, self.boxed(side, d)))
        self.at += 1

    def finish(self):
        if self.done:
            return
        self.done = True
        c, n = self.c, self.groups
        while self.at < n - 1:
            self.step()
        box, mine = self.ref("box"), self.ref("mine")
        above, below = c >= 1, c + 1 < n
        self.arrived(above, self.move(0, c, self.boxed(0, c)))
        self.arrived(below, self.move(1, c, self.boxed(1, c)))
        for p in range(self.count):
            first = jnp.where(c >= 1, 0, 1)
            total = self.piece(mine, c, p).astype(F32) + box[first, c, p].astype(F32)
            self.ref("sum")[p] = total.astype(BF16)

            @pl.when(above & below)
            def _(p=p, total=total):
                self.ref("sum")[p] = (total + box[1, c, p].astype(F32)).astype(BF16)

    def drain(self):
        wait_both(self.sent)


def others(row):
    for k in range(1, 8):
        ps = lax.rem(row.s + k // 4, 2)
        low = row.rx if k % 2 else row.r
        pr = lax.rem(low + 2 * ((k // 2) % 2), 4)
        yield k, ps, pr


class Swap:
    def __init__(self, tag):
        self.tag = tag

    def declare(self, scratch):
        scratch[self.tag + "send"] = pltpu.SemaphoreType.DMA((8,))
        scratch[self.tag + "recv"] = pltpu.SemaphoreType.DMA((8,))
        scratch[self.tag + "own"] = pltpu.SemaphoreType.DMA((1,))

    def start(self, ns, row, own, lanes, src, dst, to_tokens):
        send, recv, local = (getattr(ns, self.tag + a) for a in ("send", "recv", "own"))

        def tokens_of(s, r):
            return pl.ds(pl.multiple_of((s * 4 + r) * own, 16), own)

        def lanes_of(s, r):
            return pl.ds(pl.multiple_of((r * 2 + s) * lanes, 128), lanes)

        def ends(ps, pr):
            if to_tokens:
                return src.at[:, tokens_of(ps, pr), :], dst.at[:, :, lanes_of(row.s, row.r)]
            return src.at[:, :, lanes_of(ps, pr)], dst.at[:, tokens_of(row.s, row.r), :]

        a, b = ends(row.s, row.r)
        self.mine = pltpu.make_async_copy(a, b, local.at[0])
        self.mine.start()
        self.copies = []
        for k, ps, pr in others(row):
            a, b = ends(ps, pr)
            copy = pltpu.make_async_remote_copy(
                src_ref=a,
                dst_ref=b,
                send_sem=send.at[k],
                recv_sem=recv.at[k],
                device_id=(ps, pr, row.c),
                device_id_type=MESH,
            )
            copy.start()
            self.copies.append(copy)

    def wait(self):
        for copy in self.copies:
            copy.wait_recv()
        self.mine.wait()

    def drain(self):
        for copy in self.copies:
            copy.wait_send()


def plane_peers(row):
    return [
        (ps, pr, row.c) for k, ps, pr in others(row) if k not in (1, 2, 4)
    ]


def schedule(row, full, micros, compute, result, hook, between=()):
    gather_first(row, full, micros)
    hook("gathering")
    for m in range(micros):
        row.ag_wait(full, m)
        hook(f"gathered{m}")
        if m >= 1:
            row.rs_pair(m - 1)
        if m >= 2:
            row.rs_transit(m - 2)
        compute(m)
        row.rs_start(m)
        if m + 2 < micros:
            row.ag_pass(full, m + 2)
        if m + 1 < micros:
            row.ag_diag(full, m + 1)
        hook(f"computed{m}")
    tail(row, micros, result, hook, between)


def gather_first(row, full, micros):
    row.ag_start(full, 0)
    if micros > 1:
        row.ag_start(full, 1)
    row.ag_pass(full, 0)
    for m in range(2, micros):
        row.ag_start(full, m)
    if micros > 1:
        row.ag_pass(full, 1)
    row.ag_diag(full, 0)


def tail(row, micros, result, hook, between=()):
    more = list(between)

    def step():
        if more:
            more.pop(0)()

    step()
    if micros > 1:
        row.rs_transit(micros - 2)
    row.rs_pair(micros - 1)
    for m in range(micros - 1):
        if m < micros - 2:
            step()
            result(m)
    step()
    row.rs_transit(micros - 1)
    hook("tail")
    if micros > 1:
        result(micros - 2)
    while more:
        step()
    hook("last")
    result(micros - 1)


def ffn_forward_kernel(k, row, loc, cfg, begin, hook, end):
    micros, rows = cfg.micros, cfg.rows
    loads = cfg.load_weights(k, loc)
    scale = gain_row(k, cfg, cfg.layer, 1)
    for m in range(micros):
        norm_to(k.full, scale, k.mid[m], row.span(m, row.s, row.r))
    begin()

    def compute(m):
        here = pl.ds(m * rows, rows)
        loc.start(k.full.at[here, :], k.xin_o.at[here, :])
        if m == 0:
            for copy in loads:
                loc.wait(copy)
        gate = dot(k.full[here, :], k.w[0])
        lift = dot(k.full[here, :], k.w[1])
        k.gp[here, :] = gate.astype(BF16)
        k.up[here, :] = lift.astype(BF16)
        k.act[here, :] = (gate * jax.nn.sigmoid(gate) * lift).astype(BF16)
        k.part[here, :] = dot(k.act[here, :], k.w[2], 1, 1).astype(BF16)
        for a, b in ((k.gp, k.gp_o), (k.up, k.up_o), (k.act, k.act_o)):
            loc.start(a.at[here, :], b.at[here, :])

    def result(m):
        k.y_o[m] = (k.mid[m] + row.rs_result(m)).astype(BF16)

    schedule(row, k.full, micros, compute, result, hook)
    end()


def ffn_backward_kernel(k, row, loc, cfg, begin, hook, end):
    micros, rows = cfg.micros, cfg.rows
    width = cfg.width
    early = cfg.load_weights(k, loc)
    early += [loc.start(a, b) for a, b in ((k.gp_h, k.gp), (k.up_h, k.up))]
    late = [loc.start(a, b) for a, b in ((k.act_h, k.act), (k.xin_h, k.xin))]
    for m in range(micros):
        k.full[row.span(m, row.s, row.r), :] = k.dy[m]
    begin()
    scale = gain_row(k, cfg, cfg.layer, 1)
    k.dgain_o[...] = jnp.zeros_like(k.dgain_o)

    def compute(m):
        if m == 0:
            for copy in early:
                loc.wait(copy)
        here = pl.ds(m * rows, rows)
        d_act = dot(k.full[here, :], k.w[2])
        gate = k.gp[here, :].astype(F32)
        lift = k.up[here, :].astype(F32)
        sig = jax.nn.sigmoid(gate)
        silu = gate * sig
        k.dg[here, :] = (d_act * lift * (sig + silu * (1.0 - sig))).astype(BF16)
        k.du[here, :] = (d_act * silu).astype(BF16)
        total = dot(k.dg[here, :], k.w[0], 1, 1) + dot(k.du[here, :], k.w[1], 1, 1)
        k.part[here, :] = total.astype(BF16)

    def result(m):
        back, gains = norm_back(k.mid[m], scale, row.rs_result(m))
        k.dmid_o[m] = k.dy[m].astype(F32) + back
        k.dgain_o[...] += gains

    def grad(i, left, right):
        def body():
            if i == 2:
                for copy in late:
                    loc.wait(copy)

            @pl.loop(0, width // 256)
            def _(t):
                at = pl.ds(pl.multiple_of(t * 256, 256), 256)
                k.grad[i, at, :] = dot(left[:, at], right[...], 0, 0).astype(BF16)

            loc.start(k.grad.at[i], k.grad_o.at[i])

        return body

    grads = [grad(2, k.full, k.act), grad(0, k.xin, k.dg), grad(1, k.xin, k.du)]
    schedule(row, k.full, micros, compute, result, hook, grads)
    end()


def pair_masks(size):
    rows_at = lax.broadcasted_iota(jnp.int32, (size, size), 0)
    cols_at = lax.broadcasted_iota(jnp.int32, (size, size), 1)
    return (rows_at >= cols_at) & (rows_at // BLOCK == cols_at // BLOCK)


def gate_columns(gates, columns):
    count, size = gates.shape
    rows_at = lax.broadcasted_iota(jnp.int32, (size, size), 0)
    cols_at = lax.broadcasted_iota(jnp.int32, (size, size), 1)
    for i in range(count):
        spread = jnp.where(rows_at == cols_at, gates[i : i + 1, :], 0.0)
        columns[i * size : (i + 1) * size, :] = jnp.sum(spread, axis=1, keepdims=True)


def gain_row(k, cfg, layer, kind):
    rows_each = cfg.width // 4 // 128
    pieces = [
        k.gains[layer, r, kind * rows_each + h : kind * rows_each + h + 1, :]
        for r in range(4)
        for h in range(rows_each)
    ]
    return jnp.concatenate(pieces, axis=1)


class Heads:
    def __init__(self, k, row, cfg, layer):
        self.k, self.row, self.cfg, self.layer = k, row, cfg, layer

    def persist(self):
        k, cfg = self.k, self.cfg
        out = []
        for kind in range(2):
            start = pl.multiple_of(8 + (2 * kind + self.row.s) * 8, 8)
            for j in range(cfg.groups):
                block = k.line[self.layer, j, pl.ds(start, 8), :]
                k.persist[j * cfg.per : (j + 1) * cfg.per, :] = block[: cfg.per, :]
            out.append(k.persist[...].astype(BF16))
        return out

    def keeps(self, j):
        decays = self.k.line[self.layer, j, 40:48, :] * self.k.starts[j]
        return jnp.where(self.row.s == 0, decays[0:1, :], decays[1:2, :])

    def own(self):
        keeps = self.keeps(self.row.c)
        blocks = self.cfg.blocks

        def of(m, b):
            return keeps[:, m * blocks + b : m * blocks + b + 1]

        return of

    def through(self, m, j):
        keeps = self.keeps(j)
        product = None
        for b in range(self.cfg.blocks):
            at = m * self.cfg.blocks + b
            one = keeps[:, at : at + 1]
            product = one if product is None else product * one
        return product


def pair_probs(q, k, pk, mask, scale):
    inner = jnp.where(mask, dot(q, k, 1, 1) * scale, -1e30)
    outer = dot(q, pk, 1, 1) * scale
    top = jnp.maximum(
        jnp.max(inner, axis=1, keepdims=True), jnp.max(outer, axis=1, keepdims=True)
    )
    inner = jnp.exp(inner - top)
    outer = jnp.exp(outer - top)
    norm = 1.0 / (jnp.sum(inner, axis=1, keepdims=True) + jnp.sum(outer, axis=1, keepdims=True))
    return inner * norm, outer * norm


class States:
    def __init__(self, row, groups, k, backward):
        self.backward, self.sent = backward, []
        self.row, self.groups, self.mine, self.box = row, groups, k.leaving, k.box
        self.send, self.recv, self.entering = k.ssend, k.srecv, k.entering

    def copy(self, m, k):
        n = self.groups
        to = self.row.c + (-k if self.backward else k)
        return pltpu.make_async_remote_copy(
            src_ref=self.mine.at[m],
            dst_ref=self.box.at[m, k],
            send_sem=self.send.at[m, k],
            recv_sem=self.recv.at[m, k],
            device_id=(self.row.s, self.row.r, jnp.clip(to, 0, n - 1)),
            device_id_type=MESH,
        )

    def after(self, k):
        c, n = self.row.c, self.groups
        return (c >= k) if self.backward else (c + k < n)

    def before(self, k):
        c, n = self.row.c, self.groups
        return (c + k < n) if self.backward else (c >= k)

    def start(self, m):
        for k in range(1, self.groups):

            @pl.when(self.after(k))
            def _(k=k):
                self.copy(m, k).start()

            self.sent.append((self.after(k), self.copy(m, k)))

    def wait(self, m):
        for k in range(1, self.groups):

            @pl.when(self.before(k))
            def _(k=k):
                self.copy(m, k).wait_recv()

    def drain(self):
        wait_both(self.sent)

    def fold(self, m, through):
        entering = self.entering
        entering[...] = jnp.zeros_like(entering)
        for k in range(self.groups - 1, 0, -1):

            @pl.when(self.before(k))
            def _(k=k):
                source = self.row.c + (k if self.backward else -k)
                factor = through(m, jnp.clip(source, 0, self.groups - 1))
                entering[...] = factor * entering[...] + self.box[m, k].astype(F32)


def attn_forward_kernel(k, row, loc, cfg, begin, hook, end):
    micros, rows, size = cfg.micros, cfg.rows, cfg.size
    blocks = rows // BLOCK
    factor = size ** (-0.5)
    load = loc.start(k.weights, k.w)
    scale = gain_row(k, cfg, cfg.layer, 0)
    for m in range(micros):
        norm_to(k.full, scale, k.x[m].astype(F32), row.span(m, row.s, row.r))
    begin()
    states = States(row, cfg.groups, k, False)
    qs, ks, vs = (pl.ds(i * size, size) for i in range(3))
    mask = pair_masks(2 * BLOCK)
    gather_first(row, k.full, micros)
    gate_columns(k.gates[cfg.layer, 0 : cfg.micros * cfg.rows // 128, :], k.gate)
    heads = Heads(k, row, cfg, cfg.layer)
    pk, pv = heads.persist()
    keep = heads.own()
    loc.wait(load)
    for m in range(micros):
        row.ag_wait(k.full, m)
        here = pl.ds(m * rows, rows)
        loc.start(k.full.at[here, :], k.xin_o.at[here, :])
        k.qkv[here, :] = dot(k.full[here, :], k.w[0]).astype(BF16)
        loc.start(k.qkv.at[here, :], k.qkv_o.at[here, :])
        total = jnp.zeros((size, size), F32)
        for b in range(blocks):
            at = pl.ds(m * rows + b * BLOCK, BLOCK)
            keys = (k.qkv[at, ks].astype(F32) * k.gate[at, :]).astype(BF16)
            fresh = dot(keys, k.qkv[at, vs], 0, 0)
            k.update[m * blocks + b] = fresh
            total = keep(m, b) * total + fresh
        k.leaving[m] = total.astype(BF16)
        states.start(m)
        if m + 2 < micros:
            row.ag_pass(k.full, m + 2)
        if m + 1 < micros:
            row.ag_diag(k.full, m + 1)
        hook(f"states{m}")

    def compute(m):
        here = pl.ds(m * rows, rows)
        states.wait(m)
        states.fold(m, heads.through)
        memory = k.entering[...]
        for b in range(0, blocks, 2):
            at = pl.ds(m * rows + b * BLOCK, 2 * BLOCK)
            q, ky, v = k.qkv[at, qs], k.qkv[at, ks], k.qkv[at, vs]
            inner, outer = pair_probs(q, ky, pk, mask, factor)
            value = dot(inner.astype(BF16), v) + dot(outer.astype(BF16), pv)
            reads = []
            for i in range(2):
                now = keep(m, b + i) * memory
                low = now.astype(BF16)
                k.state[m * blocks + b + i] = low
                reads.append(dot(q[i * BLOCK : (i + 1) * BLOCK, :], low) * factor)
                memory = now + k.update[m * blocks + b + i]
            k.mixed[at, :] = (value + jnp.concatenate(reads, axis=0)).astype(BF16)
        if m == 0:
            hook("out")
        k.part[here, :] = dot(k.mixed[here, :], k.wo_dst[0], 1, 1).astype(BF16)
        loc.start(k.mixed.at[here, :], k.mixed_o.at[here, :])

    def result(m):
        k.mid_o[m] = k.x[m].astype(F32) + row.rs_result(m)
        if m == 0:
            loc.start(k.wo_dst, k.wo_o)

    for m in range(micros):
        compute(m)
        row.rs_start(m)
        if m >= 1:
            row.rs_pair(m - 1)
        if m >= 2:
            row.rs_transit(m - 2)
        hook(f"computed{m}")
    loc.start(k.state, k.state_o)
    tail(row, micros, result, hook)
    states.drain()
    end()


def attn_backward_kernel(k, row, loc, cfg, begin, hook, end):
    micros, rows, size, width = cfg.micros, cfg.rows, cfg.size, cfg.width
    blocks = rows // BLOCK
    factor = size ** (-0.5)
    first = [loc.start(k.weights, k.w), loc.start(k.wo_h, k.wo), loc.start(k.qkv_h, k.qkv)]
    second = [loc.start(k.state_h, k.state)]
    third = [loc.start(k.mixed_h, k.mixed), loc.start(k.xin_h, k.xin)]
    for m in range(micros):
        k.full[row.span(m, row.s, row.r), :] = k.dmid[m].astype(BF16)
    begin()
    states = States(row, cfg.groups, k, True)
    qs, ks, vs = (pl.ds(i * size, size) for i in range(3))
    in_cols, out_cols = pl.ds(0, 3 * size), pl.ds(3 * size, size)
    mask = pair_masks(2 * BLOCK)
    scale = gain_row(k, cfg, cfg.layer, 0)
    k.dgain_o[...] = jnp.zeros_like(k.dgain_o)
    k.dpersist_o[...] = jnp.zeros_like(k.dpersist_o)
    gather_first(row, k.full, micros)
    gate_columns(k.gates[cfg.layer, 0 : cfg.micros * cfg.rows // 128, :], k.gate)
    heads = Heads(k, row, cfg, cfg.layer)
    pk, pv = heads.persist()
    keep = heads.own()
    for copy in first:
        loc.wait(copy)
    for m in range(micros):
        row.ag_wait(k.full, m)
        here = pl.ds(m * rows, rows)
        k.dmix[here, :] = dot(k.full[here, :], k.wo[0]).astype(BF16)
        total = jnp.zeros((size, size), F32)
        for b in reversed(range(blocks)):
            at = pl.ds(m * rows + b * BLOCK, BLOCK)
            fresh = dot(k.qkv[at, qs], k.dmix[at, :], 0, 0) * factor
            k.update[m * blocks + b] = fresh
            total = keep(m, b) * (fresh + total)
        k.leaving[m] = total.astype(BF16)
        states.start(m)
        if m + 2 < micros:
            row.ag_pass(k.full, m + 2)
        if m + 1 < micros:
            row.ag_diag(k.full, m + 1)
        hook(f"states{m}")
    for copy in second:
        loc.wait(copy)

    def compute(m):
        here = pl.ds(m * rows, rows)
        states.wait(m)
        states.fold(m, heads.through)
        memory = k.entering[...]
        for b in reversed(range(0, blocks, 2)):
            at = pl.ds(m * rows + b * BLOCK, 2 * BLOCK)
            q, ky, v, d = k.qkv[at, qs], k.qkv[at, ks], k.qkv[at, vs], k.dmix[at, :]
            inner, outer = pair_probs(q, ky, pk, mask, factor)
            d_inner = dot(d, v, 1, 1)
            d_outer = dot(d, pv, 1, 1)
            centre = jnp.sum(inner * d_inner, axis=1, keepdims=True) + jnp.sum(
                outer * d_outer, axis=1, keepdims=True
            )
            d_inner = (inner * (d_inner - centre)).astype(BF16)
            d_outer = (outer * (d_outer - centre)).astype(BF16)
            inner, outer = inner.astype(BF16), outer.astype(BF16)
            k.dpersist_o[0] += dot(d_outer, q, 0, 0) * factor
            k.dpersist_o[1] += dot(outer, d, 0, 0)
            dq = dot(d_inner, ky) + dot(d_outer, pk)
            dk = dot(d_inner, q, 0, 0) * factor
            dv = dot(inner, d, 0, 0)
            keys = (ky.astype(F32) * k.gate[at, :]).astype(BF16)
            parts = [None, None]
            for i in (1, 0):
                sub = slice(i * BLOCK, (i + 1) * BLOCK)
                low = memory.astype(BF16)
                parts[i] = (
                    dot(d[sub, :], k.state[m * blocks + b + i], 1, 1),
                    dot(v[sub, :], low, 1, 1),
                    dot(keys[sub, :], low),
                )
                memory = keep(m, b + i) * (k.update[m * blocks + b + i] + memory)
            more_q, more_k, more_v = (jnp.concatenate(pieces, axis=0) for pieces in zip(*parts))
            k.dqkv[at, qs] = ((dq + more_q) * factor).astype(BF16)
            k.dqkv[at, ks] = (dk + k.gate[at, :] * more_k).astype(BF16)
            k.dqkv[at, vs] = (dv + more_v).astype(BF16)
        k.part[here, :] = dot(k.dqkv[here, :], k.w[0], 1, 1).astype(BF16)

    def result(m):
        back, gains = norm_back(k.x[m].astype(F32), scale, row.rs_result(m))
        k.dx_o[m] = (k.dmid[m] + back).astype(BF16)
        k.dgain_o[...] += gains

    for m in range(micros):
        compute(m)
        row.rs_start(m)
        if m >= 1:
            row.rs_pair(m - 1)
        if m >= 2:
            row.rs_transit(m - 2)
        hook(f"computed{m}")

    def out_grad():
        for copy in third:
            loc.wait(copy)

        @pl.loop(0, width // 256)
        def _(t):
            at = pl.ds(pl.multiple_of(t * 256, 256), 256)
            k.grad[0, at, out_cols] = dot(k.full[:, at], k.mixed[...], 0, 0).astype(BF16)

    def qkv_grad():
        @pl.loop(0, width // 256)
        def _(t):
            at = pl.ds(pl.multiple_of(t * 256, 256), 256)
            k.grad[0, at, in_cols] = dot(k.xin[:, at], k.dqkv[...], 0, 0).astype(BF16)

        loc.start(k.grad, k.grad_o)

    tail(row, micros, result, hook, [out_grad, qkv_grad])
    states.drain()
    end()


VM = pl.BlockSpec(memory_space=pltpu.VMEM)
SM = pl.BlockSpec(memory_space=pltpu.SMEM)
HB = pl.BlockSpec(memory_space=pl.ANY)


def vm(dims, dtype=BF16):
    return pltpu.VMEM(dims, dtype)


def launch(name, collective, body, ins, outs, scratch):
    names = list(ins) + list(outs) + list(scratch)

    def kernel(*refs):
        body(SimpleNamespace(**dict(zip(names, refs))))

    results = pl.pallas_call(
        kernel,
        out_shape=tuple(jax.ShapeDtypeStruct(d, t) for d, t, _ in outs.values()),
        in_specs=[spec for _, spec in ins.values()],
        out_specs=tuple(spec for _, _, spec in outs.values()),
        scratch_shapes=list(scratch.values()),
        compiler_params=pltpu.CompilerParams(
            collective_id=collective, has_side_effects=True, vmem_limit_bytes=VMEM_LIMIT
        ),
        name=name,
    )(*[a for a, _ in ins.values()])
    return SimpleNamespace(**dict(zip(outs, results)))


def local(
    tokens, cotangent, block_order, lengths, decay, write_gate, gain_attn, w_query, w_key, w_value,
    persist_key, persist_value, w_output, gain_ffn, w_gate, w_up, w_down,
):
    sec, row_id, col = (lax.axis_index(a) for a in ("section", "row", "col"))
    groups = lax.axis_size("col")
    micros, rows, features = tokens.shape
    width = features * 4
    own, blocks, all_rows, size = rows // 8, rows // BLOCK, micros * rows, features // 2
    ffh = w_gate.shape[2] // 2
    per = persist_key.shape[1]
    persist = per * groups
    cfg = SimpleNamespace(
        micros=micros, rows=rows, own=own, size=size, width=width, groups=groups, blocks=blocks, per=per
    )
    total_blocks = block_order.shape[1]
    positions = jnp.arange(total_blocks, dtype=jnp.int32)
    my_blocks = col * blocks + jnp.arange(blocks, dtype=jnp.int32)
    deal_picks = lax.dynamic_slice_in_dim(block_order, col * blocks, blocks, 1)
    matches = (block_order[:, :, None] == my_blocks[None, None, :]).astype(jnp.int32)
    back_picks = jnp.sum(matches * positions[None, :, None], axis=1)

    def lanes(a):
        return jnp.pad(a, ((0, 0),) * (a.ndim - 1) + ((0, 128 - a.shape[-1]),))

    def eights(a):
        return jnp.pad(a, ((0, 0),) * (a.ndim - 2) + ((0, -a.shape[-2] % 8), (0, 0)))

    share = gain_attn.shape[1]
    own_gains = jnp.concatenate([gain_attn, gain_ffn], axis=0).astype(F32)
    placed = lax.dynamic_update_slice(
        jnp.zeros((2, features), F32), own_gains, (jnp.zeros_like(col), col * share)
    )
    packed = jnp.concatenate(
        [eights(placed.reshape(-1, 128))]
        + [
            eights(a[0].reshape(per, 2, size).transpose(1, 0, 2)).reshape(16, size).astype(F32)
            for a in (persist_key, persist_value)
        ]
        + [eights(lanes(decay[0].transpose(2, 0, 1).reshape(2, -1)))],
        axis=0,
    )
    gate_rows = eights(write_gate[0].transpose(2, 0, 1).reshape(2, -1, 128)) / BLOCK
    ends = jnp.cumsum(lengths, axis=1)
    is_start = jnp.any(positions[None, :, None] == (ends - lengths)[:, None, :], axis=2)
    starts = jnp.where(is_start, 0.0, 1.0).reshape(micros, groups, blocks).transpose(1, 0, 2)
    starts = jnp.broadcast_to(lanes(starts.reshape(groups, -1))[:, None], (groups, 8, 128))

    def cols_split(w):
        return w.reshape(w.shape[0], 2, -1).transpose(1, 0, 2)

    def rows_split(w):
        return w.reshape(2, -1, w.shape[1]).transpose(0, 2, 1)

    blocks_a = jnp.concatenate(
        [cols_split(w[0]) for w in (w_query, w_key, w_value)] + [rows_split(w_output[0])], axis=2
    )[:, None]
    blocks_b = jnp.stack(
        [cols_split(w_gate[0]), cols_split(w_up[0]), rows_split(w_down[0])], axis=1
    )

    def row_scratch():
        return {
            "part": vm((all_rows, width)),
            "pair": vm((micros, 4 * own, width)),
            "both": vm((micros, 4, own, width)),
            "transit": vm((micros, 2, own, width // 2)),
            "final": vm((micros, 2, own, width)),
            "send": pltpu.SemaphoreType.DMA((micros, N_AG + N_RS)),
            "recv": pltpu.SemaphoreType.DMA((micros, N_AG + N_RS)),
            "sems": pltpu.SemaphoreType.DMA((24,)),
            "full": vm((all_rows, width)),
        }

    def run(
        name, collective, kernel, ins, outs, scratch, sides=(), swaps=(), plan=(), layer=0,
        load_weights=None,
    ):
        ins, outs, scratch, plan = dict(ins), dict(outs), dict(scratch), dict(plan)
        ins["gains"] = (opened.gains, VM)
        own_cfg = SimpleNamespace(**vars(cfg), layer=layer, load_weights=load_weights)
        scratch.update(row_scratch())
        for side in sides:
            side.declare(ins, outs, scratch, groups)
        for swap in swaps:
            swap.declare(scratch)

        def body(k):
            row = Rows(rows, own, width, k.send, k.recv)
            row.buffers = (k.part, k.pair, k.both, k.transit, k.final)
            loc = Local(k.sems)

            def at(point):
                for action in plan.get(point, ()):
                    action(k, row)

            def begin():
                peers = [(row.s, row.r, lax.rem(row.c + i, groups)) for i in range(1, groups)]
                row.greet(peers + (plane_peers(row) if swaps else []))
                for side in sides:
                    side.bind(k, row, groups)
                at("begin")

            def end():
                for side in sides:
                    side.finish()
                at("end")
                row.finish()
                for side in sides:
                    side.drain()
                for swap in swaps:
                    swap.drain()
                loc.finish()

            kernel(k, row, loc, own_cfg, begin, at, end)

        return launch(name, collective, body, ins, outs, scratch)

    def starts_of(*sides):
        return [lambda k, row, side=side: side.start() for side in sides]

    def steps_of(*sides):
        return [lambda k, row, side=side: side.step() for side in sides]

    def ends_of(*sides):
        return [lambda k, row, side=side: side.finish() for side in sides]

    stage_dims = (micros, rows, size)
    by_block = (micros, blocks, BLOCK, size)

    def lanes_of_core(name):
        def view(k, row):
            mine = pl.ds(pl.multiple_of(row.s * size, 128), size)
            return getattr(k, name).at[:, :, :, mine]

        return view

    tokens_b = tokens.reshape(micros, blocks, BLOCK, features)
    cotangent_b = cotangent.reshape(micros, blocks, BLOCK, features)

    def chosen(k, buf, picks, stage, lead=()):
        for m in range(micros):
            for b in range(blocks):
                stage[lead + (m, pl.ds(b * BLOCK, BLOCK))] = buf[lead + (m, picks[m, b])]

    def head_body(k):
        row = Rows(rows, own, width, None, None)
        peers = [row.x, row.y, row.sib] + plane_peers(row)
        peers += [(row.s, row.r, lax.rem(row.c + i, groups)) for i in range(1, groups)]
        barrier = pltpu.get_barrier_semaphore()
        for peer in peers:
            pl.semaphore_signal(barrier, inc=1, device_id=peer, device_id_type=MESH)
        pl.semaphore_wait(barrier, len(peers))
        copies, keeps_here = [], []
        for i, (src, dst) in enumerate(((k.blocks_a, k.shards_a), (k.blocks_b, k.shards_b))):
            keep_here = pltpu.make_async_copy(src.at[row.s], dst.at[row.s], k.locals.at[i])
            copy = pltpu.make_async_remote_copy(
                src_ref=src.at[1 - row.s],
                dst_ref=dst.at[row.s],
                send_sem=k.xsend.at[i],
                recv_sem=k.xrecv.at[i],
                device_id=row.sib,
                device_id_type=MESH,
            )
            keep_here.start()
            copy.start()
            copies.append(copy)
            keeps_here.append(keep_here)
        deal.bind(k, row, groups)
        deal.start()

        def push(src, dst, i, to):
            copy = pltpu.make_async_remote_copy(
                src_ref=src,
                dst_ref=dst,
                send_sem=k.psend.at[i],
                recv_sem=k.precv.at[i],
                device_id=to,
                device_id_type=MESH,
            )
            copy.start()
            return copy

        k.line[row.s, row.c] = k.packed[...]
        k.gates[row.s] = k.gate_rows[row.s]
        small = [
            push(
                k.packed,
                k.line.at[row.s, row.c],
                i,
                (row.s, row.r, lax.rem(row.c + i, groups)),
            )
            for i in range(1, groups)
        ]
        crossing = [push(k.gate_rows.at[1 - row.s], k.gates.at[row.s], 0, row.sib)]
        copies[0].wait_recv()
        keeps_here[0].wait()
        first.bind(k, row, groups)
        first.start()
        copies[1].wait_recv()
        keeps_here[1].wait()
        down0.bind(k, row, groups)
        down0.start()
        for copy in small:
            copy.wait_recv()
        total = k.line[row.s, 0, 0:8, :]
        for j in range(1, groups):
            total = total + k.line[row.s, j, 0:8, :]
        k.gains[row.s, row.r] = total
        for i, ps, pr in others(row):
            mine = k.gains.at[row.s, row.r]
            crossing.append(push(mine, mine, groups + i, (ps, pr, row.c)))
        crossing.append(push(k.line.at[row.s], k.line.at[row.s], groups + 8, row.sib))
        deal.step()
        first.step()
        down0.step()
        deal.step()
        first.step()
        down0.step()
        deal.finish()
        chosen(k, k.deal_dst, k.picks, k.stage)
        swap.start(k, row, own, size, k.stage, k.x, True)
        first.finish()
        swap.wait()
        down0.finish()
        for copy in copies + small:
            copy.wait_send()
        for copy in crossing:
            copy.wait()
        deal.drain()
        first.drain()
        down0.drain()
        swap.drain()

    a_dims, b_dims = blocks_a.shape[1:], blocks_b.shape[1:]
    deal = Gather("deal_", tokens_b, by_block, groups, 1, lanes_of_core("deal_src"), "scratch")
    q_dims, o_dims = (1, a_dims[1], 3 * size), (1, a_dims[1], size)
    first = Gather("first_", None, q_dims, groups, 1, lambda k, row: q_of(k.shards_a, 0))

    down0 = Gather(
        "down_", None, (1,) + b_dims[1:], groups, 1, lambda k, row: k.shards_b.at[0, pl.ds(2, 1)]
    )

    def q_of(ref, layer):
        return ref.at[layer, :, :, pl.ds(0, 3 * size)]

    def o_of(ref, layer):
        return ref.at[layer, :, :, pl.ds(3 * size, size)]

    swap = Swap("swap_")
    ins = {
        "picks": (deal_picks, SM),
        "blocks_a": (blocks_a, HB),
        "blocks_b": (blocks_b, HB),
        "packed": (packed, VM),
        "gate_rows": (gate_rows, VM),
    }
    outs = {
        "x": ((micros, own, width), BF16, VM),
        "shards_a": (blocks_a.shape, BF16, HB),
        "shards_b": (blocks_b.shape, BF16, HB),
        "line": ((2, groups) + packed.shape, F32, VM),
        "gains": ((2, 4, 8, 128), F32, VM),
        "gates": ((2,) + gate_rows.shape[1:], F32, VM),
    }
    scratch = {
        "stage": vm((micros, rows, size)),
        "xsend": pltpu.SemaphoreType.DMA((2,)),
        "xrecv": pltpu.SemaphoreType.DMA((2,)),
        "locals": pltpu.SemaphoreType.DMA((2,)),
        "psend": pltpu.SemaphoreType.DMA((groups + 9,)),
        "precv": pltpu.SemaphoreType.DMA((groups + 9,)),
    }
    for side in (deal, first, down0):
        side.declare(ins, outs, scratch, groups)
    swap.declare(scratch)
    opened = launch("deal", 0, head_body, ins, outs, scratch)

    state_scratch = {
        "update": vm((micros * blocks, size, size), F32),
        "entering": vm((size, size), F32),
        "leaving": vm((micros, size, size)),
        "box": vm((micros, groups, size, size)),
        "ssend": pltpu.SemaphoreType.DMA((micros, groups)),
        "srecv": pltpu.SemaphoreType.DMA((micros, groups)),
        "gate": vm((all_rows, 1), F32),
        "persist": vm((persist, size), F32),
        "w": vm((1, width, 3 * size)),
        "qkv": vm((all_rows, 3 * size)),
        "state": vm((micros * blocks, size, size)),
        "mixed": vm((all_rows, size)),
    }
    def ffn_ins(weights):
        return {f"weights{i}": (w, HB) for i, w in enumerate(weights)}

    def ffn_loads(weights):
        def load(k, loc):
            return [
                loc.start(getattr(k, f"weights{i}"), k.w.at[pl.ds(i, 1)])
                for i in range(len(weights))
            ]

        return load

    ffn_scratch = {
        "w": vm((3, width, ffh)),
        "gp": vm((all_rows, ffh)),
        "up": vm((all_rows, ffh)),
        "act": vm((all_rows, ffh)),
    }

    def attn_ins(weights):
        return {
            "line": (opened.line, VM),
            "gates": (opened.gates, VM),
            "starts": (starts, VM),
            "weights": (weights, HB),
        }

    def attn_forward(collective, l, x, weights, more_outs=(), **more):
        outs = {
            "xin_o": ((all_rows, width), BF16, HB),
            "qkv_o": ((all_rows, 3 * size), BF16, HB),
            "state_o": ((micros * blocks, size, size), BF16, HB),
            "mixed_o": ((all_rows, size), BF16, HB),
            "mid_o": ((micros, own, width), F32, VM),
            "wo_o": ((1, width, size), BF16, HB),
            **dict(more_outs),
        }
        ins = {"x": (x, VM), **attn_ins(weights)}
        return run(
            f"attn_forward_{l}", collective, attn_forward_kernel, ins, outs, state_scratch,
            layer=l, **more,
        )

    def ffn_forward(collective, l, mid, weights, more_ins=(), more_outs=(), more_scratch=(), **more):
        outs = {
            "xin_o": ((all_rows, width), BF16, HB),
            "gp_o": ((all_rows, ffh), BF16, HB),
            "up_o": ((all_rows, ffh), BF16, HB),
            "act_o": ((all_rows, ffh), BF16, HB),
            "y_o": ((micros, own, width), BF16, VM),
            **dict(more_outs),
        }
        ins = {
            "mid": (mid, VM), **ffn_ins(weights), **dict(more_ins),
        }
        return run(
            f"ffn_forward_{l}", collective, ffn_forward_kernel, ins, outs,
            {**ffn_scratch, **dict(more_scratch)}, layer=l, load_weights=ffn_loads(weights), **more,
        )

    def ffn_backward(
        collective, l, dy, mid, kept, weights, more_ins=(), more_outs=(), more_scratch=(), **more
    ):
        outs = {
            "dmid_o": ((micros, own, width), F32, VM),
            "dgain_o": ((1, width), F32, VM),
            "grad_o": ((3, width, ffh), BF16, HB),
            **dict(more_outs),
        }
        ins = {
            "dy": (dy, VM), "mid": (mid, VM), **ffn_ins(weights), "xin_h": (kept.xin_o, HB), "gp_h": (kept.gp_o, HB),
            "up_h": (kept.up_o, HB), "act_h": (kept.act_o, HB), **dict(more_ins),
        }
        scratch = {
            **ffn_scratch, **dict(more_scratch), "xin": vm((all_rows, width)), "dg": vm((all_rows, ffh)),
            "du": vm((all_rows, ffh)), "grad": vm((3, width, ffh)),
        }
        return run(
            f"ffn_backward_{l}", collective, ffn_backward_kernel, ins, outs, scratch,
            layer=l, load_weights=ffn_loads(weights), **more,
        )

    def attn_backward(collective, l, dmid, x, kept, weights, more_ins=(), more_outs=(), **more):
        outs = {
            "dx_o": ((micros, own, width), BF16, VM),
            "dgain_o": ((1, width), F32, VM),
            "dpersist_o": ((2, persist, size), F32, VM),
            "grad_o": ((1, width, 4 * size), BF16, HB),
        }
        ins = {
            "dmid": (dmid, VM), "x": (x, VM), **attn_ins(weights), "wo_h": (kept.wo_o, HB), "xin_h": (kept.xin_o, HB),
            "qkv_h": (kept.qkv_o, HB), "state_h": (kept.state_o, HB), "mixed_h": (kept.mixed_o, HB),
        }
        scratch = {
            **state_scratch, "wo": vm((1, width, size)), "xin": vm((all_rows, width)), "dmix": vm((all_rows, size)),
            "dqkv": vm((all_rows, 3 * size)), "grad": vm((1, width, 4 * size)),
        }
        return run(
            f"attn_backward_{l}", collective, attn_backward_kernel, ins, outs, scratch,
            layer=l, **more,
        )

    def shard(name, layer, span=None):
        def view(k, row):
            ref = getattr(k, name).at[layer]
            return ref if span is None else ref.at[pl.ds(*span)]

        return view

    x0, q0 = opened.x, opened.first_dst

    def one_b(tag, layer, which, home=None):
        dims = (1,) + b_dims[1:]
        view = shard(tag + "src", layer, (which, 1))
        return Gather(tag, opened.shards_b, dims, groups, 1, view, home)

    def wo_side(layer):
        return Gather(
            "wo_", opened.shards_a, o_dims, groups, 1, lambda k, row: o_of(k.wo_src, layer), "scratch"
        )

    def attn_sides(layer):
        wo, gate, up = wo_side(layer), one_b("gate_", layer, 0), one_b("up_", layer, 1)
        plan = {
            "begin": starts_of(wo, gate, up),
            "states0": steps_of(wo, gate),
            "states1": steps_of(wo, up),
            "states2": steps_of(gate, up),
            "out": ends_of(wo),
        }
        return [wo, gate, up], plan

    def leave(swap, source, dst="stage_o"):
        return lambda k, row: swap.start(
            k, row, own, size, getattr(k, source), getattr(k, dst), False
        )

    def waited(swap):
        return lambda k, row: swap.wait()

    def staged(tag, array):
        return Gather(tag, array.reshape(by_block), by_block, groups, 1)

    sides, plan = attn_sides(0)
    fa0 = attn_forward(1, 0, x0, q0, sides=sides, plan=plan)
    b0 = [fa0.gate_dst, fa0.up_dst, opened.down_dst]
    next_down = one_b("down_", 1, 2)
    next_q = Gather("q_", opened.shards_a, q_dims, groups, 1, lambda k, row: q_of(k.q_src, 1))
    ff0 = ffn_forward(
        2, 0, fa0.mid_o, b0, sides=[next_q, next_down],
        plan={
            "begin": starts_of(next_q, next_down), "computed0": steps_of(next_q, next_down),
            "computed1": steps_of(next_q, next_down),
        },
    )
    sides, plan = attn_sides(1)
    swap_y0 = Swap("swap_")
    plan["begin"] = plan["begin"] + [leave(swap_y0, "x")]
    plan["end"] = [waited(swap_y0)]
    fa1 = attn_forward(
        3, 1, ff0.y_o, ff0.q_dst, more_outs={"stage_o": (stage_dims, BF16, HB)},
        sides=sides, swaps=[swap_y0], plan=plan,
    )
    b1 = [fa1.gate_dst, fa1.up_dst, ff0.down_dst]
    cot = Gather("cot_", cotangent_b, by_block, groups, 1, lanes_of_core("cot_src"), "scratch")
    swap_cot = Swap("swap_")

    def deal_cot(k, row):
        cot.finish()
        chosen(k, k.cot_dst, k.picks, k.stage)
        swap_cot.start(k, row, own, size, k.stage, k.dy_o, True)

    ff1 = ffn_forward(
        4, 1, fa1.mid_o, b1,
        more_ins={"picks": (deal_picks, SM)},
        more_outs={"dy_o": ((micros, own, width), BF16, VM)},
        more_scratch={"stage": vm(stage_dims)},
        sides=[cot], swaps=[swap_cot],
        plan={
            "begin": starts_of(cot), "computed0": steps_of(cot), "computed1": steps_of(cot),
            "tail": [deal_cot], "end": [waited(swap_cot)],
        },
    )

    swap_y1 = Swap("swap_")
    y0 = staged("y0_", fa1.stage_o)
    fb1 = ffn_backward(
        5, 1, ff1.dy_o, fa1.mid_o, ff1, b1,
        more_ins={"y1": (ff1.y_o, VM)}, more_outs={"stage_o": (stage_dims, BF16, HB)},
        sides=[y0], swaps=[swap_y1],
        plan={
            "begin": starts_of(y0) + [leave(swap_y1, "y1")],
            "computed0": steps_of(y0), "computed1": steps_of(y0), "end": [waited(swap_y1)],
        },
    )
    down1, gate1 = Total("td_", fb1.grad_o, groups, (2, 1)), Total("tg_", fb1.grad_o, groups, (0, 1))
    ab1 = attn_backward(
        6, 1, fb1.dmid_o, ff0.y_o, fa1, ff0.q_dst, sides=[down1, gate1],
        plan={
            "begin": starts_of(down1), "states0": steps_of(down1), "states1": steps_of(down1),
            "states2": starts_of(gate1), "computed0": steps_of(gate1), "computed1": steps_of(gate1),
        },
    )
    up1, a1 = Total("tu_", fb1.grad_o, groups, (1, 1)), Total("ta_", ab1.grad_o, groups)
    swap_g, y1 = Swap("swap_"), staged("y1_", fb1.stage_o)
    fb0 = ffn_backward(
        7, 0, ab1.dx_o, fa0.mid_o, ff0, b0, more_outs={"stage_o": (stage_dims, BF16, HB)},
        sides=[up1, a1, y1], swaps=[swap_g],
        plan={
            "begin": starts_of(y1, up1, a1) + [leave(swap_g, "dy")],
            "computed0": steps_of(y1, up1, a1), "computed1": steps_of(y1, up1, a1),
            "end": [waited(swap_g)],
        },
    )
    down0, gate0 = Total("td_", fb0.grad_o, groups, (2, 1)), Total("tg_", fb0.grad_o, groups, (0, 1))
    g1 = staged("g_", fb0.stage_o)
    ab0 = attn_backward(
        8, 0, fb0.dmid_o, x0, fa0, q0, sides=[g1, down0, gate0],
        plan={
            "begin": starts_of(g1, down0), "states2": steps_of(g1, down0) + starts_of(gate0),
            "computed1": steps_of(g1, down0, gate0), "computed2": steps_of(gate0),
        },
    )

    small_rows = 4 * width // 128 + 4 * persist
    smalls = jnp.concatenate(
        [a.reshape(-1, 128) for a in (ab0.dgain_o, fb0.dgain_o, ab1.dgain_o, fb1.dgain_o)]
        + [a.reshape(-1, 128) for a in (ab0.dpersist_o, ab1.dpersist_o)],
        axis=0,
    )
    gain_rows = 4 * width // 128
    swap_last, total_a0 = Swap("swap_"), Total("ta_", ab0.grad_o, groups, home="scratch")
    up0 = Total("tu_", fb0.grad_o, groups, (1, 1), "scratch")

    last = Gather("last_", None, by_block, groups, 1, lambda k, row: k.staged, "scratch")

    def tail_body(k):
        row = Rows(rows, own, width, None, None)
        peers = [row.x, row.y, row.sib] + plane_peers(row)
        peers += [(row.s, row.r, lax.rem(row.c + i, groups)) for i in range(1, groups)]
        barrier = pltpu.get_barrier_semaphore()
        for peer in peers:
            pl.semaphore_signal(barrier, inc=1, device_id=peer, device_id_type=MESH)
        pl.semaphore_wait(barrier, len(peers))
        swap_last.start(k, row, own, size, k.dx, k.stage, False)
        up0.bind(k, row, groups)
        up0.start()
        total_a0.bind(k, row, groups)
        total_a0.start()
        loads = []
        for i, (a, b) in enumerate(
            ((k.y0_buf, k.y_v.at[0]), (k.y1_buf, k.y_v.at[1]), (k.g_buf, k.g_v),
             (k.bg0, k.res_b.at[0, pl.ds(0, 1)]), (k.bd0, k.res_b.at[0, pl.ds(2, 1)]),
             (k.bg1, k.res_b.at[1, pl.ds(0, 1)]), (k.bu1, k.res_b.at[1, pl.ds(1, 1)]),
             (k.bd1, k.res_b.at[1, pl.ds(2, 1)]), (k.a1, k.res_a.at[1]))
        ):
            load = pltpu.make_async_copy(a, b, k.loads.at[i])
            load.start()
            loads.append(load)

        def push(src, dst, i, to):
            copy = pltpu.make_async_remote_copy(
                src_ref=src,
                dst_ref=dst,
                send_sem=k.psend.at[i],
                recv_sem=k.precv.at[i],
                device_id=to,
                device_id_type=MESH,
            )
            copy.start()
            return copy

        pushes = []
        for i in range(1, groups):
            to = (row.s, row.r, lax.rem(row.c + i, groups))
            pushes.append(push(k.smalls, k.small_box.at[i], i, to))
        swap_last.wait()
        for m in range(micros):
            for b in range(blocks):
                k.staged[m, b] = k.stage[m, b * BLOCK : (b + 1) * BLOCK, :]
        last.bind(k, row, groups)
        last.start()
        for copy in pushes:
            copy.wait_recv()
        total = k.smalls[...]
        for i in range(1, groups):
            total = total + k.small_box[i]
        k.small_sum[...] = total
        gains = []
        for i, ps, pr in others(row):
            gains.append(
                push(
                    k.small_sum.at[pl.ds(0, gain_rows), :],
                    k.gain_box.at[i],
                    groups + i,
                    (ps, pr, row.c),
                )
            )
        for load in loads:
            load.wait()
        for l in range(2):
            chosen(k, k.y_v, k.back, k.halves, (l,))
        for m in range(micros):
            for b in range(blocks):
                k.halves[3, m, pl.ds(b * BLOCK, BLOCK), :] = k.g_v[m, k.back[m, b]]
        last.step()
        up0.step()
        total_a0.step()

        mine_lanes = pl.ds(pl.multiple_of(row.s * size, 128), size)
        moved, kept_here = [], []

        def give(i, pair, out):
            base = groups + 8 + i
            copy = push(pair.at[1 - row.s], out, base, row.sib)
            moved.append(copy)
            here = pltpu.make_async_copy(pair.at[row.s], out, k.loads.at[9 + i])
            here.start()
            kept_here.append(here)

        give(0, k.halves.at[pl.ds(0, 2)], k.acts_o.at[:, :, mine_lanes])
        last.step()
        up0.step()
        total_a0.step()
        for copy in gains:
            copy.wait_recv()
        total = k.small_sum[0:gain_rows, :]
        for i in range(1, 8):
            total = total + k.gain_box[i]
        k.gain_o[...] = total
        k.persist_o[...] = k.small_sum[gain_rows:, :]
        up0.finish()
        k.res_b[0, pl.ds(1, 1)] = k.tu_sum[...]
        give(1, k.res_b, k.grad_b.at[row.s])
        total_a0.finish()
        k.res_a[0] = k.ta_sum[...]
        give(2, k.res_a, k.grad_a.at[row.s])
        last.finish()
        for m in range(micros):
            for b in range(blocks):
                k.halves[2, m, pl.ds(b * BLOCK, BLOCK), :] = k.last_dst[m, k.back[m, b]]
        give(3, k.halves.at[pl.ds(2, 2)], k.grads_o.at[:, :, mine_lanes])
        for copy in moved:
            copy.wait()
        for here in kept_here:
            here.wait()
        for copy in pushes + gains:
            copy.wait_send()
        swap_last.drain()
        total_a0.drain()
        up0.drain()
        last.drain()

    ins = {
        "dx": (ab0.dx_o, VM),
        "y0_buf": (fb1.y0_dst, HB),
        "y1_buf": (fb0.y1_dst, HB),
        "g_buf": (ab0.g_dst, HB),
        "bg0": (ab0.tg_sum, HB),
        "bd0": (ab0.td_sum, HB),
        "bg1": (ab1.tg_sum, HB),
        "bu1": (fb0.tu_sum, HB),
        "bd1": (ab1.td_sum, HB),
        "a1": (fb0.ta_sum, HB),
        "smalls": (smalls, VM),
        "back": (back_picks, SM),
    }
    outs = {
        "acts_o": ((micros, rows, features), BF16, VM),
        "grads_o": ((micros, rows, features), BF16, VM),
        "grad_a": ((2,) + total_a0.dims, BF16, VM),
        "grad_b": ((2, 3) + up0.dims[1:], BF16, VM),
        "gain_o": ((gain_rows, 128), F32, VM),
        "persist_o": ((4 * persist, 128), F32, VM),
    }
    scratch = {
        "stage": vm(stage_dims),
        "staged": vm(by_block),
        "y_v": vm((2,) + last.dims),
        "g_v": vm(last.dims),
        "halves": vm((4,) + stage_dims),
        "res_a": vm((2,) + total_a0.dims),
        "res_b": vm((2, 3) + up0.dims[1:]),
        "small_box": vm((groups, small_rows, 128), F32),
        "small_sum": vm((small_rows, 128), F32),
        "gain_box": vm((8, gain_rows, 128), F32),
        "loads": pltpu.SemaphoreType.DMA((13,)),
        "psend": pltpu.SemaphoreType.DMA((groups + 12,)),
        "precv": pltpu.SemaphoreType.DMA((groups + 12,)),
    }
    for side in (total_a0, up0, last):
        side.declare(ins, outs, scratch, groups)
    swap_last.declare(scratch)
    closed = launch("restore", 9, tail_body, ins, outs, scratch)

    def cols_join(pair):
        return jnp.concatenate([pair[0], pair[1]], axis=1).astype(F32)[None]

    def rows_join(pair):
        return jnp.concatenate([pair[0].T, pair[1].T], axis=0).astype(F32)[None]

    grad_a, grad_b = closed.grad_a[:, 0], closed.grad_b
    heads = [cols_join(grad_a[:, :, i * size : (i + 1) * size]) for i in range(3)]
    grad_out = rows_join(grad_a[:, :, 3 * size :])
    grad_gate, grad_up = cols_join(grad_b[:, 0]), cols_join(grad_b[:, 1])
    grad_down = rows_join(grad_b[:, 2])
    gain_sum = closed.gain_o.reshape(2, 2, width)
    my_gain = lax.dynamic_slice_in_dim(
        lax.dynamic_index_in_dim(gain_sum, sec, 0, False), (row_id * groups + col) * share, share, 1
    )
    persist_sum = closed.persist_o.reshape(2, 2, persist, size)
    persist_sum = lax.dynamic_slice_in_dim(persist_sum, col * per, per, 2)
    mine_p = lax.dynamic_index_in_dim(persist_sum, sec, 0, False)
    got_p = lax.ppermute(
        lax.dynamic_index_in_dim(persist_sum, 1 - sec, 0, False), "section", [(0, 1), (1, 0)]
    )
    grad_persist = jnp.concatenate(
        [jnp.where(sec == 0, mine_p, got_p), jnp.where(sec == 0, got_p, mine_p)], axis=2
    )
    return (
        closed.acts_o[None],
        closed.grads_o[None],
        my_gain[0][None],
        heads[0],
        heads[1],
        heads[2],
        grad_persist[0][None],
        grad_persist[1][None],
        grad_out,
        my_gain[1][None],
        grad_gate,
        grad_up,
        grad_down,
    )


def solution(mesh):
    weight = P("section", "col", "row")
    across = P("section", "row", "col")
    gain = P("section", ("row", "col"))
    rows = P("section", None, "col", "row")
    return jax.shard_map(
        local,
        mesh=mesh,
        in_specs=(
            P(None, "col", "row"), P(None, "col", "row"), P(), P(), rows, rows, gain, weight, weight,
            weight, weight, weight, across, gain, weight, weight, across,
        ),
        out_specs=(
            rows, rows, gain, weight, weight, weight, weight, weight, across, gain, weight, weight,
            across,
        ),
        check_vma=False,
    )
```

time: 898 us -> 535 us (0.60)
  blocking collectives: 252 us -> 0 us
  waiting for transfers between devices: 235 us -> 0.01 us
  Pallas kernels: 315 us -> 501 us
  local copies, waits for them, and re-layouts: 40.9 us -> 16.7 us
  between operations: 17.2 us -> 1.55 us
  other arithmetic: 24.4 us -> 9.13 us
    all_gather x10 -> x0, blocking collectives: 196 us -> none  [local(): lax.all_gather(pair[l], 'col', axis=a, tiled=True)]
    pallas_call x11 -> x10, Pallas kernels: 315 us -> 501 us  [launch(): pl.pallas_call(kernel, out_shape=tuple((jax.ShapeDtypeStruct(d, t) for d,...]
    reduce_scatter x10 -> x0, waiting for transfers between devices: 139 us -> none  [local(): lax.psum_scatter(g, 'col', scatter_dimension=a, tiled=True)]
    all_gather x3 -> x0, waiting for transfers between devices: 89.7 us -> none  [pick(): whole = lax.all_gather(shard, 'col', axis=1, tiled=True)]
    psum x2 -> x0, blocking collectives: 55.9 us -> none  [the longest x1 38.2 us: local(): gain_sum = lax.psum(jnp.stack(gains), ('section', 'row', 'col'))]
    select_n x15 -> x2, other arithmetic: 11.6 us -> 0.73 us  [the longest x1 0.73 us: local(): jnp.where(sec == 0, got_p, mine_p)]
    slice x9 -> x0, local copies, waits for them, and re-layouts: 10.4 us -> none  [the longest x4 7.25 us: section_of(): return line[..., offsets[i][0]:offsets[i][1]].reshape((2, groups) + dims)]
  transfers between devices with their start and end apart: 27 -> 1, of which waited for: 11 -> 0; matrix products, arithmetic and copies ran while one was open for 6% -> 2% of each run, Pallas kernels for 3% -> 0%
where the time goes in v2:
time: 535 us; the launch traced here: 529 us
  Pallas kernels  501 us (94%)
  local copies, waits for them, and re-layouts  16.7 us (3%)
  other arithmetic  9.13 us (2%)
    pallas_call x10, Pallas kernels, launch(): pl.pallas_call(kernel, out_shape=tuple((jax.ShapeDtypeStruct(d, t) for d,...  501 us
  transfers between devices with their start and end apart: 1, of which 0 were waited for; matrix products, arithmetic and copies ran while one was open for 2% of the time, Pallas kernels for 0%

profile of v2, /device:TPU:0, one launch (start us, length us, event | category | flops | bytes accessed | tf_op | source)
XLA Modules:
  0.0 528.7 jit_solution(18194247721991538352)
XLA Ops:
  0.7 0.7 maximum_convert_fusion.7
  1.4 0.2 dynamic_update_slice.3
  1.6 0.7 copy.70
  2.3 0.1 reshape.306
  2.4 1.2 copy.65
  3.6 0.0 copy-start.5
  3.6 0.0 copy-start.6
  3.6 1.2 copy.66
  4.8 0.0 copy-start.7
  4.9 0.0 copy-start.12
  4.9 0.2 copy.67
  5.1 0.0 copy-start.13
  5.1 0.0 copy-start.17
  5.2 0.1 copy.58
  5.3 0.1 copy.59
  5.4 0.1 copy.60
  5.5 0.1 copy.61
  5.6 0.1 copy.62
  5.7 0.1 copy.63
  5.9 0.1 copy.64
  6.0 0.6 pad_multiply_fusion.refs_4_
  6.7 0.2 reduce_window_sum.11
  6.8 0.1 fusion.1
  6.9 0.1 select_n.52
  7.0 0.1 reshape.309
  7.1 0.7 constant_dynamic-slice_fusion.1.refs_0_.refs_4_
  7.8 1.3 pad_maximum_fusion.refs_2_
  9.1 0.6 select_maximum_fusion.refs_3_
  9.7 0.9 maximum_bitcast_fusion.refs_1_
  10.6 70.0 %deal.1 = (bf16[3,48,1024]{2,1,0:T(8,128)(2,1)}, bf16[2,1,256,512]{3,2,1,0:T(8,128)(2,1)}, bf16[2,3,256,352]{3,2,1,0:T(8,128)(2,1)}, f32[2,4,48,128]{3,2,1,0:T(8...) custom-call(s32[3,6]{1,0:T(4,128)} %constant_dynamic-slice_fusion.1., ...), custom_call_target="tpu_custom_call" | custom-call | tf_op jit(solution)/shard_map/deal/pallas_call | solution.py:957
  80.6 0.6 broadcast_in_dim.22.refs_3_.refs_4_
  81.2 45.8 %attn_forward_0.1 = (bf16[1152,1024]{1,0:T(8,128)(2,1)}, bf16[1152,384]{1,0:T(8,128)(2,1)}, bf16[18,128,128]{2,1,0:T(8,128)(2,1)}, bf16[1152,128]{1,0:T(8,128)(2...) custom-call(bf16[3,48,1024]{2,1,0:T(8,128)(2,1)} %get-tuple-element., ...), custom_call_target="tpu_custom_call" | custom-call | tf_op jit(solution)/shard_map/attn_forward_0/pallas_call | solution.py:957
  127.0 41.9 %ffn_forward_0.1 = (bf16[1152,1024]{1,0:T(8,128)(2,1)}, bf16[1152,352]{1,0:T(8,128)(2,1)}, bf16[1152,352]{1,0:T(8,128)(2,1)}, bf16[1152,352]{1,0:T(8,128)(2,1)},...) custom-call(f32[3,48,1024]{2,1,0:T(8,128)} %get-tuple-element.89.refs_0_.refs_1_, ...), custom_call_target="tpu_custom_call" | custom-call | tf_op jit(solution)/shard_map/ffn_forward_0/pallas_call | solution.py:957
  169.0 49.1 %attn_forward_1.1 = (bf16[1152,1024]{1,0:T(8,128)(2,1)}, bf16[1152,384]{1,0:T(8,128)(2,1)}, bf16[18,128,128]{2,1,0:T(8,128)(2,1)}, bf16[1152,128]{1,0:T(8,128)(2...) custom-call(bf16[3,48,1024]{2,1,0:T(8,128)(2,1)} %get-tuple-element., ...), custom_call_target="tpu_custom_call" | custom-call | tf_op jit(solution)/shard_map/attn_forward_1/pallas_call | solution.py:957
  218.0 42.4 %ffn_forward_1.1 = (bf16[1152,1024]{1,0:T(8,128)(2,1)}, bf16[1152,352]{1,0:T(8,128)(2,1)}, bf16[1152,352]{1,0:T(8,128)(2,1)}, bf16[1152,352]{1,0:T(8,128)(2,1)},...) custom-call(f32[3,48,1024]{2,1,0:T(8,128)} %get-tuple-element.95.refs_0_.refs_1_, ...), custom_call_target="tpu_custom_call" | custom-call | tf_op jit(solution)/shard_map/ffn_forward_1/pallas_call | solution.py:957
  260.5 39.7 %ffn_backward_1.1 = (f32[3,48,1024]{2,1,0:T(8,128)}, f32[1,1024]{1,0:T(1,128)}, bf16[3,1024,352]{2,1,0:T(8,128)(2,1)}, bf16[3,384,128]{2,1,0:T(8,128)(2,1)}, bf16[3,24,64,128]{3,2,1,0:T(8,128)(2,1)}) custom-call(bf16[3,48,1024]{2,1,0:T(8,128)(2,1)} %get-tuple-element.99.refs_0_, f32[3,48,1024]{2,1,0:T(8,128)} %get-tuple-element.95.refs_0_.refs_1_, ...), custom_call_target="tpu_custom_call" | custom-call | tf_op jit(solution)/shard_map/ffn_backward_1/pallas_call | solution.py:957
  300.2 48.9 %attn_backward_1.1 = (bf16[3,48,1024]{2,1,0:T(8,128)(2,1)}, f32[1,1024]{1,0:T(1,128)}, f32[2,16,128]{2,1,0:T(8,128)}, bf16[1,1024,512]{2,1,0:T(8,128)(2,1)}, bf1...) custom-call(f32[3,48,1024]{2,1,0:T(8,128)} %get-tuple-element.106.refs_0_, ...), custom_call_target="tpu_custom_call" | custom-call | tf_op jit(solution)/shard_map/attn_backward_1/pallas_call | solution.py:957
  349.1 53.6 %ffn_backward_0.1 = (f32[3,48,1024]{2,1,0:T(8,128)}, f32[1,1024]{1,0:T(1,128)}, bf16[3,1024,352]{2,1,0:T(8,128)(2,1)}, bf16[3,384,128]{2,1,0:T(8,128)(2,1)}, bf1...) custom-call(bf16[3,48,1024]{2,1,0:T(8,128)(2,1)} %get-tuple-element.113.refs_0_, ...), custom_call_target="tpu_custom_call" | custom-call | tf_op jit(solution)/shard_map/ffn_backward_0/pallas_call | solution.py:957
  402.8 54.7 %attn_backward_0.1 = (bf16[3,48,1024]{2,1,0:T(8,128)(2,1)}, f32[1,1024]{1,0:T(1,128)}, f32[2,16,128]{2,1,0:T(8,128)}, bf16[1,1024,512]{2,1,0:T(8,128)(2,1)}, bf1...) custom-call(f32[3,48,1024]{2,1,0:T(8,128)} %get-tuple-element.120.refs_0_, ...), custom_call_target="tpu_custom_call" | custom-call | tf_op jit(solution)/shard_map/attn_backward_0/pallas_call | solution.py:957
  457.4 0.7 constant_dynamic-update-slice_fusion.5
  458.1 0.8 select_reduce_fusion.refs_11_
  458.9 0.7 constant_dynamic-update-slice_fusion.1
  459.7 0.6 copy-done.8
  460.3 54.8 %restore.1 = (bf16[3,384,256]{2,1,0:T(8,128)(2,1)}, bf16[3,384,256]{2,1,0:T(8,128)(2,1)}, bf16[2,1,256,512]{3,2,1,0:T(8,128)(2,1)}, bf16[2,3,256,352]{3,2,1,0:T(...) custom-call(bf16[3,48,1024]{2,1,0:T(8,128)(2,1)} %get-tuple-element.128.refs_0_, ...), custom_call_target="tpu_custom_call" | custom-call | tf_op jit(solution)/shard_map/restore/pallas_call | solution.py:957
  515.1 0.7 dynamic-slice_bitcast_fusion
  515.8 0.4 collective-permute-start
  516.2 1.5 slice_bitcast_fusion.1
  517.7 0.1 slice_bitcast_fusion.7
  517.9 0.1 constant_dynamic-slice_fusion
  518.0 0.5 slice_bitcast_fusion.8
  518.5 0.1 maximum_convert_fusion.2
  518.6 0.1 maximum_convert_fusion.1
  518.8 0.1 maximum_convert_fusion
  518.9 0.7 maximum_convert_fusion.5
  519.7 0.7 maximum_convert_fusion.4
  520.4 0.7 maximum_convert_fusion.3
  521.1 1.1 copy.76
  522.2 1.1 copy.75
  523.3 1.1 copy.74
  524.4 0.8 copy.73
  525.3 0.7 bitcast_select_fusion
  526.0 0.6 pad_maximum_fusion.1
  526.6 0.8 copy.85
  527.4 0.8 copy.86
  (48 shorter events, 0.2 us)
Async XLA Ops:
  0.6 4.2 copy-start.3
  0.7 4.5 copy-start.4
  3.6 1.8 copy-start.5
  3.6 2.0 copy-start.6
  4.8 1.0 copy-start.7
  4.9 1.1 copy-start.11
  4.9 1.8 copy-start.12
  5.1 2.0 copy-start.13
  5.1 2.7 copy-start.17
  5.1 2.6 copy-start.18
  402.7 56.2 %copy-start.16 = (f32[1,1024]{1,0:T(1,128)S(1)}, f32[1,1024]{1,0:T(1,128)}, u32[]{:S(2)}) copy-start(f32[1,1024]{1,0:T(1,128)} %get-tuple-element.139) | copy-start | bytes 12292
  402.7 56.2 %copy-start.15 = (f32[1,1024]{1,0:T(1,128)S(1)}, f32[1,1024]{1,0:T(1,128)}, u32[]{:S(2)}) copy-start(f32[1,1024]{1,0:T(1,128)} %get-tuple-element.140) | copy-start | bytes 12292
  402.7 56.2 %copy-start.14 = (f32[1,1024]{1,0:T(1,128)S(1)}, f32[1,1024]{1,0:T(1,128)}, u32[]{:S(2)}) copy-start(f32[1,1024]{1,0:T(1,128)} %get-tuple-element.141) | copy-start | bytes 12292
  402.7 56.9 %copy-start.9 = (f32[2,16,128]{2,1,0:T(8,128)S(1)}, f32[2,16,128]{2,1,0:T(8,128)}, u32[]{:S(2)}) copy-start(f32[2,16,128]{2,1,0:T(8,128)} %get-tuple-element.143) | copy-start | bytes 49156
  459.7 0.6 copy-start.8
  515.8 9.4 %collective-permute-start = (f32[2,4,128]{2,1,0:T(4,128)S(1)}, f32[2,4,128]{2,1,0:T(4,128)S(1)}, u32[]{:S(2)}, u32[]{:S(2)}) collective-permute-start(f32[2,4,128]{2,1,0:T(4,128)S(1)} %dynamic-slice_bitcast_fusion), channel_id=1, source_target_pairs={{0,16},{16,0},{1,17},{17,1},{2,18},{18,2},{3,19},{19,3},{4,20},{20... | collective-permute-start | bytes 12296 | tf_op jit(solution)/shard_map/ppermute | solution.py:1676
  516.2 1.5 copy-start.2
  516.2 1.6 copy-start.10
  523.3 3.3 copy-start.1
  524.4 3.0 copy-start

commit v3 on v2

v3 whole, which is shorter than its diff:
```python
from types import SimpleNamespace

import jax
import jax.numpy as jnp
from jax import lax
from jax.experimental import pallas as pl
from jax.experimental.pallas import tpu as pltpu
from jax.sharding import PartitionSpec as P

BLOCK = 64
EPS = 1e-06
MESH = pl.DeviceIdType.MESH
F32 = jnp.float32
BF16 = jnp.bfloat16
VMEM_LIMIT = 60 << 20
N_AG, N_RS = 8, 7


def dot(a, b, ca=1, cb=0):
    return lax.dot_general(a, b, (((ca,), (cb,)), ((), ())), preferred_element_type=F32)


class Rows:
    def __init__(self, rows, own, width, send, recv):
        self.rows, self.own, self.width, self.half = rows, own, width, width // 2
        self.send, self.recv = send, recv
        self.s, self.r, self.c = (lax.axis_index(a) for a in ("section", "row", "col"))
        self.rx = self.r + 1 - 2 * lax.rem(self.r, 2)
        self.ry = lax.rem(self.r + 2, 4)
        self.rd = lax.rem(self.rx + 2, 4)
        self.x = (self.s, self.rx, self.c)
        self.y = (self.s, self.ry, self.c)
        self.sib = (1 - self.s, self.r, self.c)
        self.started = []

    def greet(self, others=()):
        barrier = pltpu.get_barrier_semaphore()
        peers = [self.x, self.y, self.sib] + list(others)
        for peer in peers:
            pl.semaphore_signal(barrier, inc=1, device_id=peer, device_id_type=MESH)
        pl.semaphore_wait(barrier, len(peers))

    def copy(self, src, dst, m, k, peer):
        return pltpu.make_async_remote_copy(
            src_ref=src,
            dst_ref=dst,
            send_sem=self.send.at[m, k],
            recv_sem=self.recv.at[m, k],
            device_id=peer,
            device_id_type=MESH,
        )

    def go(self, copy):
        copy.start()
        self.started.append(copy)

    def finish(self):
        for copy in self.started:
            copy.wait_send()
        self.started = []

    def span(self, m, s, r):
        return pl.ds(pl.multiple_of(m * self.rows + (s * 4 + r) * self.own, 16), self.own)

    def ag_copy(self, full, m, k):
        left, right = pl.ds(0, self.half), pl.ds(self.half, self.half)
        mine, atx, aty, atd = (
            self.span(m, self.s, r) for r in (self.r, self.rx, self.ry, self.rd)
        )
        if k == 0:
            return self.copy(full.at[mine, :], full.at[mine, :], m, 0, self.x)
        if k == 1:
            return self.copy(full.at[mine, :], full.at[mine, :], m, 1, self.y)
        if k == 2:
            return self.copy(full.at[mine, :], full.at[mine, :], m, 2, self.sib)
        if k == 3:
            return self.copy(full.at[atx, left], full.at[atx, left], m, 3, self.y)
        if k == 4:
            return self.copy(full.at[aty, right], full.at[aty, right], m, 4, self.x)
        if k == 5:
            return self.copy(full.at[atx, :], full.at[atx, :], m, 5, self.sib)
        if k == 6:
            return self.copy(full.at[aty, :], full.at[aty, :], m, 6, self.sib)
        return self.copy(full.at[atd, :], full.at[atd, :], m, 7, self.sib)

    def ag_start(self, full, m):
        for k in (0, 1, 2):
            self.go(self.ag_copy(full, m, k))

    def ag_pass(self, full, m):
        self.ag_copy(full, m, 0).wait_recv()
        self.go(self.ag_copy(full, m, 3))
        self.go(self.ag_copy(full, m, 5))
        self.ag_copy(full, m, 1).wait_recv()
        self.go(self.ag_copy(full, m, 4))
        self.go(self.ag_copy(full, m, 6))

    def ag_diag(self, full, m):
        self.ag_copy(full, m, 3).wait_recv()
        self.ag_copy(full, m, 4).wait_recv()
        self.go(self.ag_copy(full, m, 7))

    def ag_wait(self, full, m):
        for k in (2, 5, 6, 7):
            self.ag_copy(full, m, k).wait_recv()

    def rs_copy(self, m, k):
        part, pair, both, transit, final = self.buffers
        left, right = pl.ds(0, self.half), pl.ds(self.half, self.half)
        if k == 8:
            other = pl.ds(
                pl.multiple_of(m * self.rows + (1 - self.s) * 4 * self.own, 16), 4 * self.own
            )
            return self.copy(part.at[other, :], pair.at[m], m, 8, self.sib)
        if k == 9:
            return self.copy(both.at[m, self.rd, :, left], transit.at[m, 0], m, 9, self.x)
        if k == 10:
            return self.copy(both.at[m, self.rd, :, right], transit.at[m, 1], m, 10, self.y)
        if k == 11:
            return self.copy(both.at[m, self.rx, :, left], final.at[m, 0, :, left], m, 11, self.x)
        if k == 12:
            return self.copy(both.at[m, self.ry, :, right], final.at[m, 1, :, right], m, 12, self.y)
        if k == 13:
            return self.copy(both.at[m, self.ry, :, left], final.at[m, 1, :, left], m, 13, self.y)
        return self.copy(both.at[m, self.rx, :, right], final.at[m, 0, :, right], m, 14, self.x)

    def rs_start(self, m):
        self.go(self.rs_copy(m, 8))

    def rs_pair(self, m):
        part, pair, both, _, _ = self.buffers
        self.rs_copy(m, 8).wait_recv()
        for r in range(4):
            mine = part[self.span(m, self.s, r), :].astype(F32)
            theirs = pair[m, r * self.own : (r + 1) * self.own, :].astype(F32)
            both[m, r] = (mine + theirs).astype(BF16)
        for k in (9, 10, 11, 12):
            self.go(self.rs_copy(m, k))

    def rs_transit(self, m):
        _, _, both, transit, _ = self.buffers
        left, right = pl.ds(0, self.half), pl.ds(self.half, self.half)
        self.rs_copy(m, 9).wait_recv()
        total = both[m, self.ry, :, left].astype(F32) + transit[m, 0].astype(F32)
        both[m, self.ry, :, left] = total.astype(BF16)
        self.go(self.rs_copy(m, 13))
        self.rs_copy(m, 10).wait_recv()
        total = both[m, self.rx, :, right].astype(F32) + transit[m, 1].astype(F32)
        both[m, self.rx, :, right] = total.astype(BF16)
        self.go(self.rs_copy(m, 14))

    def rs_result(self, m):
        _, _, both, _, final = self.buffers
        for k in (11, 12, 13, 14):
            self.rs_copy(m, k).wait_recv()
        return both[m, self.r].astype(F32) + final[m, 0].astype(F32) + final[m, 1].astype(F32)


class Local:
    def __init__(self, sems):
        self.sems, self.used, self.open = sems, 0, []

    def start(self, src, dst):
        copy = pltpu.make_async_copy(src, dst, self.sems.at[self.used])
        self.used += 1
        copy.start()
        self.open.append(copy)
        return copy

    def wait(self, copy):
        copy.wait()
        self.open = [other for other in self.open if other is not copy]

    def finish(self):
        for copy in list(self.open):
            copy.wait()


def inv_rms(values):
    return lax.rsqrt(jnp.mean(values * values, axis=1, keepdims=True) + EPS)


def norm_to(full, gain, values, span):
    full[span, :] = (values * inv_rms(values) * gain).astype(BF16)


def norm_back(values, gain, grad):
    scale = inv_rms(values)
    weighted = grad * gain
    inner = jnp.mean(weighted * values, axis=1, keepdims=True)
    back = scale * weighted - values * (scale * scale * scale * inner)
    return back, jnp.sum(grad * values * scale, axis=0, keepdims=True)


def wait_both(copies):
    for condition, copy in copies:

        @pl.when(condition)
        def _(copy=copy):
            copy.wait_send()


class Side:
    def __init__(self, tag):
        self.tag = tag

    def ref(self, name):
        return getattr(self.ns, self.tag + name)

    def bind(self, ns, row, groups):
        self.ns, self.row, self.c, self.groups = ns, row, row.c, groups
        self.sent = []

    def when(self, condition, copy):
        @pl.when(condition)
        def _():
            copy.start()

        self.sent.append((condition, copy))

    def arrived(self, condition, copy):
        @pl.when(condition)
        def _():
            copy.wait_recv()

    def remote(self, src, dst, send, recv, to):
        return pltpu.make_async_remote_copy(
            src_ref=src,
            dst_ref=dst,
            send_sem=send,
            recv_sem=recv,
            device_id=(self.row.s, self.row.r, to),
            device_id_type=MESH,
        )


def part_of(ref, at, per, axis):
    where = pl.ds(pl.multiple_of(at * per, per), per)
    return ref.at[(slice(None),) * axis + (where,)]


class Gather(Side):
    def __init__(self, tag, array, dims, groups, axis, view=None, home=None):
        super().__init__(tag)
        self.array, self.axis, self.view, self.home = array, axis, view, home
        self.per = dims[axis]
        self.dims = dims[:axis] + (dims[axis] * groups,) + dims[axis + 1 :]

    def declare(self, ins, outs, scratch, groups):
        if self.array is not None:
            ins[self.tag + "src"] = (self.array, HB)
        if self.home is None:
            outs[self.tag + "dst"] = (self.dims, BF16, HB)
        else:
            scratch[self.tag + "dst"] = pltpu.VMEM(self.dims, BF16)
        scratch[self.tag + "send"] = pltpu.SemaphoreType.DMA((2, groups))
        scratch[self.tag + "recv"] = pltpu.SemaphoreType.DMA((groups,))
        scratch[self.tag + "own"] = pltpu.SemaphoreType.DMA((1,))

    def slot(self, j):
        return part_of(self.ref("dst"), jnp.clip(j, 0, self.groups - 1), self.per, self.axis)

    def source(self):
        return self.view(self.ns, self.row) if self.view else self.ref("src")

    def move(self, j, side, src=None):
        to = jnp.clip(self.c + (1 - 2 * side), 0, self.groups - 1)
        j = jnp.clip(j, 0, self.groups - 1)
        src = self.slot(j) if src is None else src
        return self.remote(
            src, self.slot(j), self.ref("send").at[side, j], self.ref("recv").at[j], to
        )

    def start(self):
        c, n = self.c, self.groups
        self.at, self.done = 1, False
        self.own = pltpu.make_async_copy(self.source(), self.slot(c), self.ref("own").at[0])
        self.own.start()
        self.when(c + 1 < n, self.move(c, 0, self.source()))
        self.when(c >= 1, self.move(c, 1, self.source()))

    def step(self):
        c, n, k = self.c, self.groups, self.at
        if k < n:
            self.arrived(c >= k, self.move(c - k, 0))
            self.arrived(c + k < n, self.move(c + k, 1))
            if k < n - 1:
                self.when((c >= k) & (c + 1 < n), self.move(c - k, 0))
                self.when((c + k < n) & (c >= 1), self.move(c + k, 1))
        self.at += 1

    def finish(self):
        if not self.done:
            while self.at < self.groups:
                self.step()
            self.own.wait()
            self.done = True

    def drain(self):
        wait_both(self.sent)


class Total(Side):
    def __init__(self, tag, parts, dims, groups, span, view=None, home=None):
        super().__init__(tag)
        self.parts, self.span, self.view, self.home = parts, span, view, home
        self.per = dims[1] // groups
        self.count = span[1]
        self.dims = (self.count, self.per, dims[2])

    def declare(self, ins, outs, scratch, groups):
        if self.home is None:
            outs[self.tag + "sum"] = (self.dims, BF16, VM)
        else:
            scratch[self.tag + "sum"] = pltpu.VMEM(self.dims, BF16)
        if self.view is None:
            ins[self.tag + "parts"] = (self.parts, HB)
            whole = (self.count, self.per * groups, self.dims[2])
            scratch[self.tag + "mine"] = pltpu.VMEM(whole, BF16)
        scratch[self.tag + "box"] = pltpu.VMEM((2, groups) + self.dims, BF16)
        scratch[self.tag + "send"] = pltpu.SemaphoreType.DMA((2, groups))
        scratch[self.tag + "recv"] = pltpu.SemaphoreType.DMA((2, groups))
        scratch[self.tag + "load"] = pltpu.SemaphoreType.DMA((1,))

    def clip(self, j):
        return jnp.clip(j, 0, self.groups - 1)

    def piece(self, ref, d, p=None):
        d = self.clip(d)
        where = pl.ds(pl.multiple_of(d * self.per, self.per), self.per)
        if p is None:
            return ref.at[:, where, :]
        return ref[p + (self.span[0] if self.view else 0), where, :]

    def source(self):
        parts = self.view(self.ns) if self.view else self.ref("parts")
        return parts.at[pl.ds(*self.span)]

    def mine(self):
        return self.view(self.ns) if self.view else self.ref("mine")

    def move(self, side, d, src):
        d = self.clip(d)
        to = self.clip(self.c + (1 - 2 * side))
        return self.remote(
            src,
            self.ref("box").at[side, d],
            self.ref("send").at[side, d],
            self.ref("recv").at[side, d],
            to,
        )

    def boxed(self, side, d):
        return self.ref("box").at[side, self.clip(d)]

    def start(self):
        c, n = self.c, self.groups
        self.at, self.done = 1, False
        if self.view is None:
            self.load = pltpu.make_async_copy(
                self.source(), self.ref("mine"), self.ref("load").at[0]
            )
            self.load.start()
        self.ends(0)

    def ends(self, t):
        c, n = self.c, self.groups
        self.when(c == 0, self.move(0, n - 1 - t, self.piece(self.source(), n - 1 - t)))
        self.when(c == n - 1, self.move(1, t, self.piece(self.source(), t)))

    def step(self):
        c, n, t = self.c, self.groups, self.at
        box, mine = self.ref("box"), self.mine()
        if t == 1 and self.view is None:
            self.load.wait()
        if t < n - 1:
            self.ends(t)
            for side, place, d in ((0, c, n - 1 - t + c), (1, n - 1 - c, t + c - (n - 1))):
                here = (place >= 1) & (place <= t)
                self.arrived(here, self.move(side, d, self.boxed(side, d)))

                @pl.when(here)
                def _(side=side, d=d):
                    for p in range(self.count):
                        total = self.piece(mine, d, p).astype(F32)
                        total = total + box[side, self.clip(d), p].astype(F32)
                        box[side, self.clip(d), p] = total.astype(BF16)

                self.when(here, self.move(side, d, self.boxed(side, d)))
        self.at += 1

    def finish(self):
        if self.done:
            return
        self.done = True
        c, n = self.c, self.groups
        while self.at < n - 1:
            self.step()
        box, mine = self.ref("box"), self.mine()
        above, below = c >= 1, c + 1 < n
        self.arrived(above, self.move(0, c, self.boxed(0, c)))
        self.arrived(below, self.move(1, c, self.boxed(1, c)))
        for p in range(self.count):
            first = jnp.where(c >= 1, 0, 1)
            total = self.piece(mine, c, p).astype(F32) + box[first, c, p].astype(F32)
            self.ref("sum")[p] = total.astype(BF16)

            @pl.when(above & below)
            def _(p=p, total=total):
                self.ref("sum")[p] = (total + box[1, c, p].astype(F32)).astype(BF16)

    def drain(self):
        wait_both(self.sent)


def others(row):
    for k in range(1, 8):
        ps = lax.rem(row.s + k // 4, 2)
        low = row.rx if k % 2 else row.r
        pr = lax.rem(low + 2 * ((k // 2) % 2), 4)
        yield k, ps, pr


class Swap:
    def __init__(self, tag):
        self.tag = tag

    def declare(self, scratch):
        scratch[self.tag + "send"] = pltpu.SemaphoreType.DMA((8,))
        scratch[self.tag + "recv"] = pltpu.SemaphoreType.DMA((8,))
        scratch[self.tag + "own"] = pltpu.SemaphoreType.DMA((1,))

    def start(self, ns, row, own, lanes, src, dst, to_tokens):
        send, recv, local = (getattr(ns, self.tag + a) for a in ("send", "recv", "own"))

        def tokens_of(s, r):
            return pl.ds(pl.multiple_of((s * 4 + r) * own, 16), own)

        def lanes_of(s, r):
            return pl.ds(pl.multiple_of((r * 2 + s) * lanes, 128), lanes)

        def ends(ps, pr):
            if to_tokens:
                return src.at[:, tokens_of(ps, pr), :], dst.at[:, :, lanes_of(row.s, row.r)]
            return src.at[:, :, lanes_of(ps, pr)], dst.at[:, tokens_of(row.s, row.r), :]

        a, b = ends(row.s, row.r)
        self.mine = pltpu.make_async_copy(a, b, local.at[0])
        self.mine.start()
        self.copies = []
        for k, ps, pr in others(row):
            a, b = ends(ps, pr)
            copy = pltpu.make_async_remote_copy(
                src_ref=a,
                dst_ref=b,
                send_sem=send.at[k],
                recv_sem=recv.at[k],
                device_id=(ps, pr, row.c),
                device_id_type=MESH,
            )
            copy.start()
            self.copies.append(copy)

    def wait(self):
        for copy in self.copies:
            copy.wait_recv()
        self.mine.wait()

    def drain(self):
        for copy in self.copies:
            copy.wait_send()


def plane_peers(row):
    return [
        (ps, pr, row.c) for k, ps, pr in others(row) if k not in (1, 2, 4)
    ]


def gather_first(row, full, micros):
    row.ag_pass(full, 0)
    if micros > 1:
        row.ag_pass(full, 1)
    row.ag_diag(full, 0)


def gather_more(row, full, micros, m):
    if m + 2 < micros:
        row.ag_pass(full, m + 2)
    if m + 1 < micros:
        row.ag_diag(full, m + 1)


def tail(row, micros, result, hook, between=()):
    more = list(between)

    def step():
        if more:
            more.pop(0)()

    step()
    row.rs_transit(micros - 2)
    row.rs_pair(micros - 1)
    for m in range(micros - 2):
        step()
        result(m)
    hook("tail")
    step()
    row.rs_transit(micros - 1)
    result(micros - 2)
    while more:
        step()
    hook("last")
    result(micros - 1)


def ffn_forward(p, row, loc, cfg, hook, deliver):
    micros, rows, full = cfg.micros, cfg.rows, p.full
    gather_first(row, full, micros)
    for m in range(micros):
        row.ag_wait(full, m)
        hook("gathered", m)
        if m >= 1:
            row.rs_pair(m - 1)
        if m >= 2:
            row.rs_transit(m - 2)
        here = pl.ds(m * rows, rows)
        loc.start(full.at[here, :], p.xin_o.at[here, :])
        gate = dot(full[here, :], p.gate_dst[0])
        lift = dot(full[here, :], p.up_dst[0])
        p.gp[here, :] = gate.astype(BF16)
        p.up[here, :] = lift.astype(BF16)
        p.act[here, :] = (gate * jax.nn.sigmoid(gate) * lift).astype(BF16)
        hook("acted", m)
        row.part[here, :] = dot(p.act[here, :], p.down_dst[0], 1, 1).astype(BF16)
        for a, b in ((p.gp, p.gp_o), (p.up, p.up_o), (p.act, p.act_o)):
            loc.start(a.at[here, :], b.at[here, :])
        row.rs_start(m)
        gather_more(row, full, micros, m)
        hook("computed", m)
    tail(row, micros, lambda m: deliver(m, row.rs_result(m)), hook)


def ffn_backward(p, row, loc, cfg, hook, loads, late, deliver):
    micros, rows, width, full = cfg.micros, cfg.rows, cfg.width, p.full
    gather_first(row, full, micros)
    for copy in loads:
        loc.wait(copy)
    for m in range(micros):
        row.ag_wait(full, m)
        hook("gathered", m)
        if m >= 1:
            row.rs_pair(m - 1)
        if m >= 2:
            row.rs_transit(m - 2)
        here = pl.ds(m * rows, rows)
        d_act = dot(full[here, :], p.w[2])
        gate = p.gp[here, :].astype(F32)
        lift = p.up[here, :].astype(F32)
        sig = jax.nn.sigmoid(gate)
        silu = gate * sig
        p.dg[here, :] = (d_act * lift * (sig + silu * (1.0 - sig))).astype(BF16)
        p.du[here, :] = (d_act * silu).astype(BF16)
        total = dot(p.dg[here, :], p.w[0], 1, 1) + dot(p.du[here, :], p.w[1], 1, 1)
        row.part[here, :] = total.astype(BF16)
        row.rs_start(m)
        gather_more(row, full, micros, m)
        hook("computed", m)

    def grad(i, left, right):
        def body():
            if i == 2:
                for copy in late:
                    loc.wait(copy)

            @pl.loop(0, width // 256)
            def _(t):
                at = pl.ds(pl.multiple_of(t * 256, 256), 256)
                p.grad[i, at, :] = dot(left[:, at], right[...], 0, 0).astype(BF16)

            hook("grad", i)

        return body

    grads = [grad(2, full, p.act), grad(0, p.xin, p.dg), grad(1, p.xin, p.du)]
    tail(row, micros, lambda m: deliver(m, row.rs_result(m)), hook, grads)


def pair_masks(size):
    rows_at = lax.broadcasted_iota(jnp.int32, (size, size), 0)
    cols_at = lax.broadcasted_iota(jnp.int32, (size, size), 1)
    return (rows_at >= cols_at) & (rows_at // BLOCK == cols_at // BLOCK)


def gate_columns(gates, columns):
    count, size = gates.shape
    rows_at = lax.broadcasted_iota(jnp.int32, (size, size), 0)
    cols_at = lax.broadcasted_iota(jnp.int32, (size, size), 1)
    for i in range(count):
        spread = jnp.where(rows_at == cols_at, gates[i : i + 1, :], 0.0)
        columns[i * size : (i + 1) * size, :] = jnp.sum(spread, axis=1, keepdims=True)


def gain_row(k, cfg, layer, kind):
    rows_each = cfg.width // 4 // 128
    pieces = [
        k.gains[layer, r, kind * rows_each + h : kind * rows_each + h + 1, :]
        for r in range(4)
        for h in range(rows_each)
    ]
    return jnp.concatenate(pieces, axis=1)


class Heads:
    def __init__(self, k, row, cfg, layer):
        self.k, self.row, self.cfg, self.layer = k, row, cfg, layer

    def persist(self):
        k, cfg = self.k, self.cfg
        out = []
        for kind in range(2):
            start = pl.multiple_of(8 + (2 * kind + self.row.s) * 8, 8)
            for j in range(cfg.groups):
                block = k.line[self.layer, j, pl.ds(start, 8), :]
                k.persist[j * cfg.per : (j + 1) * cfg.per, :] = block[: cfg.per, :]
            out.append(k.persist[...].astype(BF16))
        return out

    def keeps(self, j):
        decays = self.k.line[self.layer, j, 40:48, :] * self.k.starts[j]
        return jnp.where(self.row.s == 0, decays[0:1, :], decays[1:2, :])

    def own(self):
        keeps = self.keeps(self.row.c)
        blocks = self.cfg.blocks

        def of(m, b):
            return keeps[:, m * blocks + b : m * blocks + b + 1]

        return of

    def through(self, m, j):
        keeps = self.keeps(j)
        product = None
        for b in range(self.cfg.blocks):
            at = m * self.cfg.blocks + b
            one = keeps[:, at : at + 1]
            product = one if product is None else product * one
        return product


def pair_probs(q, k, pk, mask, scale):
    inner = jnp.where(mask, dot(q, k, 1, 1) * scale, -1e30)
    outer = dot(q, pk, 1, 1) * scale
    top = jnp.maximum(
        jnp.max(inner, axis=1, keepdims=True), jnp.max(outer, axis=1, keepdims=True)
    )
    inner = jnp.exp(inner - top)
    outer = jnp.exp(outer - top)
    norm = 1.0 / (jnp.sum(inner, axis=1, keepdims=True) + jnp.sum(outer, axis=1, keepdims=True))
    return inner * norm, outer * norm


class States:
    def __init__(self, row, groups, k, backward):
        self.backward, self.sent = backward, []
        self.row, self.groups, self.mine, self.box = row, groups, k.leaving, k.box
        self.send, self.recv, self.entering = k.ssend, k.srecv, k.entering

    def copy(self, m, k):
        n = self.groups
        to = self.row.c + (-k if self.backward else k)
        return pltpu.make_async_remote_copy(
            src_ref=self.mine.at[m],
            dst_ref=self.box.at[m, k],
            send_sem=self.send.at[m, k],
            recv_sem=self.recv.at[m, k],
            device_id=(self.row.s, self.row.r, jnp.clip(to, 0, n - 1)),
            device_id_type=MESH,
        )

    def after(self, k):
        c, n = self.row.c, self.groups
        return (c >= k) if self.backward else (c + k < n)

    def before(self, k):
        c, n = self.row.c, self.groups
        return (c + k < n) if self.backward else (c >= k)

    def start(self, m):
        for k in range(1, self.groups):

            @pl.when(self.after(k))
            def _(k=k):
                self.copy(m, k).start()

            self.sent.append((self.after(k), self.copy(m, k)))

    def wait(self, m):
        for k in range(1, self.groups):

            @pl.when(self.before(k))
            def _(k=k):
                self.copy(m, k).wait_recv()

    def drain(self):
        wait_both(self.sent)

    def fold(self, m, through):
        entering = self.entering
        entering[...] = jnp.zeros_like(entering)
        for k in range(self.groups - 1, 0, -1):

            @pl.when(self.before(k))
            def _(k=k):
                source = self.row.c + (k if self.backward else -k)
                factor = through(m, jnp.clip(source, 0, self.groups - 1))
                entering[...] = factor * entering[...] + self.box[m, k].astype(F32)


def attn_forward(p, row, loc, cfg, hook, layer, loads, deliver):
    micros, rows, size, full = cfg.micros, cfg.rows, cfg.size, p.full
    blocks = rows // BLOCK
    factor = size ** (-0.5)
    states = States(row, cfg.groups, p, False)
    qs, ks, vs = (pl.ds(i * size, size) for i in range(3))
    mask = pair_masks(2 * BLOCK)
    gather_first(row, full, micros)
    gate_columns(p.gates[layer, 0 : micros * rows // 128, :], p.gate)
    heads = Heads(p, row, cfg, layer)
    pk, pv = heads.persist()
    keep = heads.own()
    for copy in loads:
        loc.wait(copy)
    for m in range(micros):
        row.ag_wait(full, m)
        hook("gathered", m)
        here = pl.ds(m * rows, rows)
        loc.start(full.at[here, :], p.xin_o.at[here, :])
        p.qkv[here, :] = dot(full[here, :], p.wq[0]).astype(BF16)
        loc.start(p.qkv.at[here, :], p.qkv_o.at[here, :])
        total = jnp.zeros((size, size), F32)
        for b in range(blocks):
            at = pl.ds(m * rows + b * BLOCK, BLOCK)
            keys = (p.qkv[at, ks].astype(F32) * p.gate[at, :]).astype(BF16)
            fresh = dot(keys, p.qkv[at, vs], 0, 0)
            p.update[m * blocks + b] = fresh
            total = keep(m, b) * total + fresh
        p.leaving[m] = total.astype(BF16)
        states.start(m)
        gather_more(row, full, micros, m)
        hook("states", m)
    for m in range(micros):
        here = pl.ds(m * rows, rows)
        states.wait(m)
        states.fold(m, heads.through)
        memory = p.entering[...]
        for b in range(0, blocks, 2):
            at = pl.ds(m * rows + b * BLOCK, 2 * BLOCK)
            q, ky, v = p.qkv[at, qs], p.qkv[at, ks], p.qkv[at, vs]
            inner, outer = pair_probs(q, ky, pk, mask, factor)
            value = dot(inner.astype(BF16), v) + dot(outer.astype(BF16), pv)
            reads = []
            for i in range(2):
                now = keep(m, b + i) * memory
                low = now.astype(BF16)
                p.state[m * blocks + b + i] = low
                reads.append(dot(q[i * BLOCK : (i + 1) * BLOCK, :], low) * factor)
                memory = now + p.update[m * blocks + b + i]
            p.mixed[at, :] = (value + jnp.concatenate(reads, axis=0)).astype(BF16)
        hook("mixed", m)
        row.part[here, :] = dot(p.mixed[here, :], p.wo_dst[0], 1, 1).astype(BF16)
        loc.start(p.mixed.at[here, :], p.mixed_o.at[here, :])
        row.rs_start(m)
        if m >= 1:
            row.rs_pair(m - 1)
        if m >= 2:
            row.rs_transit(m - 2)
        hook("computed", m)
    loc.start(p.state, p.state_o)
    tail(row, micros, lambda m: deliver(m, row.rs_result(m)), hook)
    states.drain()


def attn_backward(p, row, loc, cfg, hook, layer, loads, late, deliver):
    micros, rows, size, width, full = cfg.micros, cfg.rows, cfg.size, cfg.width, p.full
    blocks = rows // BLOCK
    factor = size ** (-0.5)
    states = States(row, cfg.groups, p, True)
    qs, ks, vs = (pl.ds(i * size, size) for i in range(3))
    in_cols, out_cols = pl.ds(0, 3 * size), pl.ds(3 * size, size)
    mask = pair_masks(2 * BLOCK)
    p.dpersist[...] = jnp.zeros_like(p.dpersist)
    gate_columns(p.gates[layer, 0 : micros * rows // 128, :], p.gate)
    heads = Heads(p, row, cfg, layer)
    pk, pv = heads.persist()
    keep = heads.own()
    gather_first(row, full, micros)
    for copy in loads:
        loc.wait(copy)
    for m in range(micros):
        row.ag_wait(full, m)
        hook("gathered", m)
        here = pl.ds(m * rows, rows)
        p.dmix[here, :] = dot(full[here, :], p.wo[0]).astype(BF16)
        total = jnp.zeros((size, size), F32)
        for b in reversed(range(blocks)):
            at = pl.ds(m * rows + b * BLOCK, BLOCK)
            fresh = dot(p.qkv[at, qs], p.dmix[at, :], 0, 0) * factor
            p.update[m * blocks + b] = fresh
            total = keep(m, b) * (fresh + total)
        p.leaving[m] = total.astype(BF16)
        states.start(m)
        gather_more(row, full, micros, m)
        hook("states", m)
    for m in range(micros):
        here = pl.ds(m * rows, rows)
        states.wait(m)
        states.fold(m, heads.through)
        memory = p.entering[...]
        for b in reversed(range(0, blocks, 2)):
            at = pl.ds(m * rows + b * BLOCK, 2 * BLOCK)
            q, ky, v, d = p.qkv[at, qs], p.qkv[at, ks], p.qkv[at, vs], p.dmix[at, :]
            inner, outer = pair_probs(q, ky, pk, mask, factor)
            d_inner = dot(d, v, 1, 1)
            d_outer = dot(d, pv, 1, 1)
            centre = jnp.sum(inner * d_inner, axis=1, keepdims=True) + jnp.sum(
                outer * d_outer, axis=1, keepdims=True
            )
            d_inner = (inner * (d_inner - centre)).astype(BF16)
            d_outer = (outer * (d_outer - centre)).astype(BF16)
            inner, outer = inner.astype(BF16), outer.astype(BF16)
            p.dpersist[0] += dot(d_outer, q, 0, 0) * factor
            p.dpersist[1] += dot(outer, d, 0, 0)
            dq = dot(d_inner, ky) + dot(d_outer, pk)
            dk = dot(d_inner, q, 0, 0) * factor
            dv = dot(inner, d, 0, 0)
            keys = (ky.astype(F32) * p.gate[at, :]).astype(BF16)
            parts = [None, None]
            for i in (1, 0):
                sub = slice(i * BLOCK, (i + 1) * BLOCK)
                low = memory.astype(BF16)
                parts[i] = (
                    dot(d[sub, :], p.state[m * blocks + b + i], 1, 1),
                    dot(v[sub, :], low, 1, 1),
                    dot(keys[sub, :], low),
                )
                memory = keep(m, b + i) * (p.update[m * blocks + b + i] + memory)
            more_q, more_k, more_v = (jnp.concatenate(pieces, axis=0) for pieces in zip(*parts))
            p.dqkv[at, qs] = ((dq + more_q) * factor).astype(BF16)
            p.dqkv[at, ks] = (dk + p.gate[at, :] * more_k).astype(BF16)
            p.dqkv[at, vs] = (dv + more_v).astype(BF16)
        row.part[here, :] = dot(p.dqkv[here, :], p.wq[0], 1, 1).astype(BF16)
        row.rs_start(m)
        if m >= 1:
            row.rs_pair(m - 1)
        if m >= 2:
            row.rs_transit(m - 2)
        hook("computed", m)

    def out_grad():
        for copy in late:
            loc.wait(copy)

        @pl.loop(0, width // 256)
        def _(t):
            at = pl.ds(pl.multiple_of(t * 256, 256), 256)
            p.grad[0, at, out_cols] = dot(full[:, at], p.mixed[...], 0, 0).astype(BF16)

    def qkv_grad():
        @pl.loop(0, width // 256)
        def _(t):
            at = pl.ds(pl.multiple_of(t * 256, 256), 256)
            p.grad[0, at, in_cols] = dot(p.xin[:, at], p.dqkv[...], 0, 0).astype(BF16)

        hook("grads")

    tail(row, micros, lambda m: deliver(m, row.rs_result(m)), hook, [out_grad, qkv_grad])
    states.drain()


VM = pl.BlockSpec(memory_space=pltpu.VMEM)
SM = pl.BlockSpec(memory_space=pltpu.SMEM)
HB = pl.BlockSpec(memory_space=pl.ANY)


def vm(dims, dtype=BF16):
    return pltpu.VMEM(dims, dtype)


def launch(name, collective, body, ins, outs, scratch):
    names = list(ins) + list(outs) + list(scratch)

    def kernel(*refs):
        body(SimpleNamespace(**dict(zip(names, refs))))

    results = pl.pallas_call(
        kernel,
        out_shape=tuple(jax.ShapeDtypeStruct(d, t) for d, t, _ in outs.values()),
        in_specs=[spec for _, spec in ins.values()],
        out_specs=tuple(spec for _, _, spec in outs.values()),
        scratch_shapes=list(scratch.values()),
        compiler_params=pltpu.CompilerParams(
            collective_id=collective, has_side_effects=True, vmem_limit_bytes=VMEM_LIMIT
        ),
        name=name,
    )(*[a for a, _ in ins.values()])
    return SimpleNamespace(**dict(zip(outs, results)))


def local(
    tokens, cotangent, block_order, lengths, decay, write_gate, gain_attn, w_query, w_key, w_value,
    persist_key, persist_value, w_output, gain_ffn, w_gate, w_up, w_down,
):
    sec, row_id, col = (lax.axis_index(a) for a in ("section", "row", "col"))
    groups = lax.axis_size("col")
    micros, rows, features = tokens.shape
    width = features * 4
    own, blocks, all_rows, size = rows // 8, rows // BLOCK, micros * rows, features // 2
    ffh = w_gate.shape[2] // 2
    per = persist_key.shape[1]
    persist = per * groups
    cfg = SimpleNamespace(
        micros=micros, rows=rows, own=own, size=size, width=width, groups=groups, blocks=blocks, per=per
    )
    total_blocks = block_order.shape[1]
    positions = jnp.arange(total_blocks, dtype=jnp.int32)
    my_blocks = col * blocks + jnp.arange(blocks, dtype=jnp.int32)
    deal_picks = lax.dynamic_slice_in_dim(block_order, col * blocks, blocks, 1)
    matches = (block_order[:, :, None] == my_blocks[None, None, :]).astype(jnp.int32)
    back_picks = jnp.sum(matches * positions[None, :, None], axis=1)

    def lanes(a):
        return jnp.pad(a, ((0, 0),) * (a.ndim - 1) + ((0, 128 - a.shape[-1]),))

    def eights(a):
        return jnp.pad(a, ((0, 0),) * (a.ndim - 2) + ((0, -a.shape[-2] % 8), (0, 0)))

    share = gain_attn.shape[1]
    own_gains = jnp.concatenate([gain_attn, gain_ffn], axis=0).astype(F32)
    placed = lax.dynamic_update_slice(
        jnp.zeros((2, features), F32), own_gains, (jnp.zeros_like(col), col * share)
    )
    packed = jnp.concatenate(
        [eights(placed.reshape(-1, 128))]
        + [
            eights(a[0].reshape(per, 2, size).transpose(1, 0, 2)).reshape(16, size).astype(F32)
            for a in (persist_key, persist_value)
        ]
        + [eights(lanes(decay[0].transpose(2, 0, 1).reshape(2, -1)))],
        axis=0,
    )
    gate_rows = eights(write_gate[0].transpose(2, 0, 1).reshape(2, -1, 128)) / BLOCK
    ends = jnp.cumsum(lengths, axis=1)
    is_start = jnp.any(positions[None, :, None] == (ends - lengths)[:, None, :], axis=2)
    starts = jnp.where(is_start, 0.0, 1.0).reshape(micros, groups, blocks).transpose(1, 0, 2)
    starts = jnp.broadcast_to(lanes(starts.reshape(groups, -1))[:, None], (groups, 8, 128))

    def cols_split(w):
        return w.reshape(w.shape[0], 2, -1).transpose(1, 0, 2)

    def rows_split(w):
        return w.reshape(2, -1, w.shape[1]).transpose(0, 2, 1)

    blocks_a = jnp.concatenate(
        [cols_split(w[0]) for w in (w_query, w_key, w_value)] + [rows_split(w_output[0])], axis=2
    )[:, None]
    blocks_b = jnp.stack(
        [cols_split(w_gate[0]), cols_split(w_up[0]), rows_split(w_down[0])], axis=1
    )

    a_dims, b_dims = blocks_a.shape[1:], blocks_b.shape[1:]
    q_dims, o_dims, one_dims = (1, a_dims[1], 3 * size), (1, a_dims[1], size), (1,) + b_dims[1:]
    grad_a_dims, grad_b_dims = (1, width, 4 * size), (3, width, ffh)
    stage_dims = (micros, rows, size)
    by_block = (micros, blocks, BLOCK, size)
    gain_rows = 4 * width // 128
    half_gains = width // 128
    hbm = lambda dims, dtype=BF16: (dims, dtype, HB)

    def row_scratch(prefix):
        return {
            "part": vm((all_rows, width)),
            "pair": vm((micros, 4 * own, width)),
            "both": vm((micros, 4, own, width)),
            "transit": vm((micros, 2, own, width // 2)),
            "final": vm((micros, 2, own, width)),
            prefix + "send": pltpu.SemaphoreType.DMA((micros, N_AG + N_RS)),
            prefix + "recv": pltpu.SemaphoreType.DMA((micros, N_AG + N_RS)),
            prefix + "full": vm((all_rows, width)),
        }

    def attn_scratch(prefix):
        names = dict(
            update=vm((micros * blocks, size, size), F32),
            entering=vm((size, size), F32),
            leaving=vm((micros, size, size)),
            box=vm((micros, groups, size, size)),
            ssend=pltpu.SemaphoreType.DMA((micros, groups)),
            srecv=pltpu.SemaphoreType.DMA((micros, groups)),
            gate=vm((all_rows, 1), F32),
            persist=vm((persist, size), F32),
            qkv=vm((all_rows, 3 * size)),
            state=vm((micros * blocks, size, size)),
            mixed=vm((all_rows, size)),
        )
        return {**row_scratch(prefix), **{prefix + a: b for a, b in names.items()}}

    def ffn_scratch(prefix):
        names = {a: vm((all_rows, ffh)) for a in ("gp", "up", "act")}
        return {**row_scratch(prefix), **{prefix + a: b for a, b in names.items()}}

    def view_of(k, prefix, **more):
        names = {a[len(prefix) :]: b for a, b in vars(k).items() if a.startswith(prefix)}
        return SimpleNamespace(**{**names, **more})

    def rows_of(k, prefix):
        p = view_of(k, prefix)
        row = Rows(rows, own, width, p.send, p.recv)
        row.buffers = (k.part, k.pair, k.both, k.transit, k.final)
        row.part = k.part
        return row

    def greet_all(row):
        row.greet(
            plane_peers(row)
            + [(row.s, row.r, lax.rem(row.c + i, groups)) for i in range(1, groups)]
        )

    def hooks(plan, prefix):
        def hook(point, at=""):
            for action in plan.get(prefix + point + str(at), ()):
                action()

        return hook

    def pusher(send, recv):
        def push(src, dst, i, to):
            copy = pltpu.make_async_remote_copy(
                src_ref=src,
                dst_ref=dst,
                send_sem=send.at[i],
                recv_sem=recv.at[i],
                device_id=to,
                device_id_type=MESH,
            )
            copy.start()
            return copy

        return push

    def blocks_from(buf, picks, stage, m, lead=()):
        for b in range(blocks):
            stage[lead + (m, pl.ds(b * BLOCK, BLOCK))] = buf[lead + (m, picks[m, b])]

    def forward_names(l):
        outs = dict(
            a_xin_o=hbm((all_rows, width)),
            a_qkv_o=hbm((all_rows, 3 * size)),
            a_state_o=hbm((micros * blocks, size, size)),
            a_mixed_o=hbm((all_rows, size)),
            f_xin_o=hbm((all_rows, width)),
            f_gp_o=hbm((all_rows, ffh)),
            f_up_o=hbm((all_rows, ffh)),
            f_act_o=hbm((all_rows, ffh)),
            wo_o=hbm((1, width, size)),
            w_o=hbm((3, width, ffh)),
            mid=((micros, own, width), F32, VM),
            y=((micros, own, width), BF16, VM),
        )
        return outs, {**attn_scratch("a_"), **ffn_scratch("f_")}

    def forward_layer(k, l, x, wq, loc, loads, plan, row_a, small):
        row_f = rows_of(k, "f_")
        gain_f = gain_row(small, cfg, l, 1)

        def middle(m, summed):
            k.mid[m] = x[m].astype(F32) + summed
            norm_to(k.f_full, gain_f, k.mid[m], row_f.span(m, row_f.s, row_f.r))
            row_f.ag_start(k.f_full, m)

        def leave(m, summed):
            k.y[m] = (k.mid[m] + summed).astype(BF16)

        p = view_of(k, "a_", wq=wq, wo_dst=k.wo_dst, **vars(small))
        attn_forward(p, row_a, loc, cfg, hooks(plan, "a_"), l, loads, middle)
        row_a.finish()
        loc.start(k.wo_dst, k.wo_o)
        p = view_of(k, "f_", gate_dst=k.gate_dst, up_dst=k.up_dst, down_dst=k.down_dst)
        ffn_forward(p, row_f, loc, cfg, hooks(plan, "f_"), leave)
        for i, w in enumerate((k.gate_dst, k.up_dst, k.down_dst)):
            loc.start(w, k.w_o.at[pl.ds(i, 1)])
        return row_f

    def one_b(tag, layer, which, array):
        view = None
        if array is None:
            view = lambda k, row: k.shards_b.at[layer, pl.ds(which, 1)]
        else:
            view = lambda k, row: getattr(k, tag + "src").at[layer, pl.ds(which, 1)]
        return Gather(tag, array, one_dims, groups, 1, view, "scratch")

    def q_of(ref, layer):
        return ref.at[layer, :, :, pl.ds(0, 3 * size)]

    def o_of(ref, layer):
        return ref.at[layer, :, :, pl.ds(3 * size, size)]

    def lanes_of_core(name):
        def view(k, row):
            mine = pl.ds(pl.multiple_of(row.s * size, 128), size)
            return getattr(k, name).at[:, :, :, mine]

        return view

    tokens_b = tokens.reshape(micros, blocks, BLOCK, features)
    cotangent_b = cotangent.reshape(micros, blocks, BLOCK, features)
    deal = Gather("deal_", tokens_b, by_block, groups, 1, lanes_of_core("deal_src"), "scratch")
    q0 = Gather("q0_", None, q_dims, groups, 1, lambda k, row: q_of(k.shards_a, 0), "scratch")
    wo0 = Gather("wo_", None, o_dims, groups, 1, lambda k, row: o_of(k.shards_a, 0), "scratch")
    gate0, up0, down0 = (one_b(t, 0, i, None) for i, t in enumerate(("gate_", "up_", "down_")))
    q1 = Gather("q1_", None, q_dims, groups, 1, lambda k, row: q_of(k.shards_a, 1))
    sides1 = [deal, q0, wo0, gate0, up0, down0, q1]
    swap1 = Swap("swap_")

    def first_body(k):
        row = rows_of(k, "a_")
        loc = Local(k.sems)
        greet_all(row)
        for side in sides1:
            side.bind(k, row, groups)
        push = pusher(k.psend, k.precv)
        crossing, keeps_here = [], []
        for i, (src, dst) in enumerate(((k.blocks_a, k.shards_a), (k.blocks_b, k.shards_b))):
            keeps_here.append(loc.start(src.at[row.s], dst.at[row.s]))
            crossing.append(push(src.at[1 - row.s], dst.at[row.s], groups + 9 + i, row.sib))
        deal.start()
        k.line[row.s, row.c] = k.packed[...]
        k.gates[row.s] = k.gate_rows[row.s]
        small = [
            push(
                k.packed,
                k.line.at[row.s, row.c],
                i,
                (row.s, row.r, lax.rem(row.c + i, groups)),
            )
            for i in range(1, groups)
        ]
        late = [push(k.gate_rows.at[1 - row.s], k.gates.at[row.s], 0, row.sib)]
        crossing[0].wait_recv()
        loc.wait(keeps_here[0])
        q0.start()
        deal.step()
        for copy in small:
            copy.wait_recv()
        total = k.line[row.s, 0, 0:8, :]
        for j in range(1, groups):
            total = total + k.line[row.s, j, 0:8, :]
        k.gains[row.s, row.r] = total
        for i, ps, pr in others(row):
            mine = k.gains.at[row.s, row.r]
            late.append(push(mine, mine, groups + i, (ps, pr, row.c)))
        late.append(push(k.line.at[row.s], k.line.at[row.s], groups + 8, row.sib))
        crossing[1].wait_recv()
        loc.wait(keeps_here[1])
        q0.step()
        wo0.start()
        deal.step()
        q0.step()
        gate0.start()
        up0.start()
        wo0.step()
        deal.finish()
        for m in range(micros):
            blocks_from(k.deal_dst, k.picks, k.stage, m)
        swap1.start(k, row, own, size, k.stage, k.x, True)
        q0.finish()
        wo0.step()
        for copy in late:
            copy.wait_recv()
        gain = gain_row(k, cfg, 0, 0)
        swap1.wait()
        for m in range(micros):
            norm_to(k.a_full, gain, k.x[m].astype(F32), row.span(m, row.s, row.r))
            row.ag_start(k.a_full, m)
        loc.start(k.q0_dst, k.q0_o)
        plan = dict(
            a_gathered0=[gate0.step, up0.step, down0.start],
            a_states2=[gate0.step, up0.step],
            a_mixed0=[wo0.finish],
            a_computed1=[down0.step],
            a_tail=[down0.step],
            f_gathered0=[gate0.finish, up0.finish],
            f_acted0=[down0.finish, q1.start],
            f_computed1=[q1.step],
            f_tail=[q1.step],
        )
        small_refs = SimpleNamespace(line=k.line, gains=k.gains, gates=k.gates, starts=k.starts)
        row_f = forward_layer(k, 0, k.x, k.q0_dst, loc, [], plan, row, small_refs)
        for side in sides1:
            side.finish()
        for copy in crossing + small + late:
            copy.wait_send()
        row.finish()
        row_f.finish()
        for side in sides1:
            side.drain()
        swap1.drain()
        loc.finish()

    outs, scratch = forward_names(0)
    ins = dict(
        picks=(deal_picks, SM),
        blocks_a=(blocks_a, HB),
        blocks_b=(blocks_b, HB),
        packed=(packed, VM),
        gate_rows=(gate_rows, VM),
        starts=(starts, VM),
    )
    outs.update(
        x=((micros, own, width), BF16, VM),
        shards_a=hbm(blocks_a.shape),
        shards_b=hbm(blocks_b.shape),
        line=((2, groups) + packed.shape, F32, VM),
        gains=((2, 4, 8, 128), F32, VM),
        gates=((2,) + gate_rows.shape[1:], F32, VM),
        q0_o=hbm((1, width, 3 * size)),
    )
    scratch.update(
        stage=vm(stage_dims),
        psend=pltpu.SemaphoreType.DMA((groups + 11,)),
        precv=pltpu.SemaphoreType.DMA((groups + 11,)),
        sems=pltpu.SemaphoreType.DMA((48,)),
    )
    for side in sides1:
        side.declare(ins, outs, scratch, groups)
    swap1.declare(scratch)
    f0 = launch("forward_0", 0, first_body, ins, outs, scratch)

    smalls = dict(
        line=(f0.line, VM), gains=(f0.gains, VM), gates=(f0.gates, VM),
        starts=(starts, VM),
    )

    def small_of(k):
        return SimpleNamespace(line=k.line, gains=k.gains, gates=k.gates, starts=k.starts)

    wo1 = Gather("wo_", f0.shards_a, o_dims, groups, 1, lambda k, row: o_of(k.wo_src, 1), "scratch")
    gate1, up1, down1 = (one_b(t, 1, i, f0.shards_b) for i, t in enumerate(("gate_", "up_", "down_")))
    cot = Gather("cot_", cotangent_b, by_block, groups, 1, lanes_of_core("cot_src"), "scratch")
    sides2 = [wo1, gate1, up1, down1, cot]
    swap_y, swap_c = Swap("swapy_"), Swap("swapc_")

    def second_body(k):
        row = rows_of(k, "a_")
        loc = Local(k.sems)
        loads = [loc.start(k.q_h, k.wq)]
        gain = gain_row(k, cfg, 1, 0)
        for m in range(micros):
            norm_to(k.a_full, gain, k.x[m].astype(F32), row.span(m, row.s, row.r))
        greet_all(row)
        for side in sides2:
            side.bind(k, row, groups)
        for m in range(micros):
            row.ag_start(k.a_full, m)
        for side in (wo1, gate1, up1):
            side.start()
        swap_y.start(k, row, own, size, k.x, k.stage_o, False)

        def deal_cot():
            cot.finish()
            for m in range(micros):
                blocks_from(k.cot_dst, k.picks, k.stage, m)
            swap_c.start(k, row, own, size, k.stage, k.dy, True)

        plan = dict(
            a_states0=[wo1.step, gate1.step],
            a_states1=[wo1.step],
            a_states2=[up1.step, down1.start],
            a_mixed0=[wo1.finish],
            a_computed0=[gate1.step],
            a_computed1=[up1.step, down1.step],
            a_tail=[down1.step, cot.start],
            f_gathered0=[gate1.finish, up1.finish],
            f_acted0=[down1.finish],
            f_computed0=[cot.step],
            f_computed2=[cot.step],
            f_last=[deal_cot],
        )
        row_f = forward_layer(k, 1, k.x, k.wq, loc, loads, plan, row, small_of(k))
        for side in sides2:
            side.finish()
        swap_y.wait()
        swap_c.wait()
        row.finish()
        row_f.finish()
        for side in sides2 + [swap_y, swap_c]:
            side.drain()
        loc.finish()

    outs, scratch = forward_names(1)
    ins = dict(x=(f0.y, VM), q_h=(f0.q1_dst, HB), picks=(deal_picks, SM), **smalls)
    outs.update(dy=((micros, own, width), BF16, VM), stage_o=hbm(stage_dims))
    scratch.update(
        stage=vm(stage_dims), wq=vm((1, width, 3 * size)), sems=pltpu.SemaphoreType.DMA((48,))
    )
    for side in sides2:
        side.declare(ins, outs, scratch, groups)
    swap_y.declare(scratch)
    swap_c.declare(scratch)
    f1 = launch("forward_1", 1, second_body, ins, outs, scratch)

    def backward_names(kept, dy, x, wq):
        ins = dict(
            dy=(dy, VM), mid=(kept.mid, VM), x=(x, VM), w_h=(kept.w_o, HB),
            wo_h=(kept.wo_o, HB), wq_h=(wq, HB), ax_h=(kept.a_xin_o, HB),
            qkv_h=(kept.a_qkv_o, HB), state_h=(kept.a_state_o, HB),
            mixed_h=(kept.a_mixed_o, HB), fx_h=(kept.f_xin_o, HB), gp_h=(kept.f_gp_o, HB),
            up_h=(kept.f_up_o, HB), act_h=(kept.f_act_o, HB), **smalls,
        )
        scratch = {**attn_scratch("a_"), **ffn_scratch("f_")}
        scratch.update(
            f_w=vm((3, width, ffh)), xin=vm((all_rows, width)),
            f_dg=vm((all_rows, ffh)), f_du=vm((all_rows, ffh)), f_grad=vm(grad_b_dims),
            a_wo=vm((1, width, size)), a_wq=vm((1, width, 3 * size)),
            a_dmix=vm((all_rows, size)),
            a_dqkv=vm((all_rows, 3 * size)), a_grad=vm(grad_a_dims),
            dmid=vm((micros, own, width), F32), sems=pltpu.SemaphoreType.DMA((48,)),
        )
        return ins, scratch

    def backward_layer(k, l, loc, sides, swaps_begin, plan, dx_done):
        row_f, row_a = rows_of(k, "f_"), rows_of(k, "a_")
        first = [
            loc.start(a, b) for a, b in ((k.w_h, k.f_w), (k.gp_h, k.f_gp), (k.up_h, k.f_up))
        ]
        late_f = [loc.start(a, b) for a, b in ((k.act_h, k.f_act), (k.fx_h, k.xin))]
        loads_a = [
            loc.start(a, b)
            for a, b in (
                (k.wo_h, k.a_wo), (k.qkv_h, k.a_qkv), (k.wq_h, k.a_wq), (k.state_h, k.a_state)
            )
        ]
        late_a = [loc.start(k.mixed_h, k.a_mixed)]
        for m in range(micros):
            k.f_full[row_f.span(m, row_f.s, row_f.r), :] = k.dy[m]
        greet_all(row_f)
        for side in sides:
            side.bind(k, row_f, groups)
        for m in range(micros):
            row_f.ag_start(k.f_full, m)
        swaps_begin(row_f)
        gain_a, gain_f = gain_row(k, cfg, l, 0), gain_row(k, cfg, l, 1)
        k.dgain[...] = jnp.zeros_like(k.dgain)

        def middle(m, summed):
            back, gains = norm_back(k.mid[m], gain_f, summed)
            k.dmid[m] = k.dy[m].astype(F32) + back
            k.dgain[1:2, :] += gains
            k.a_full[row_a.span(m, row_a.s, row_a.r), :] = k.dmid[m].astype(BF16)
            row_a.ag_start(k.a_full, m)

        def leave(m, summed):
            back, gains = norm_back(k.x[m].astype(F32), gain_a, summed)
            k.dx[m] = (k.dmid[m] + back).astype(BF16)
            k.dgain[0:1, :] += gains
            dx_done(m)

        ffn_backward(view_of(k, "f_", xin=k.xin), row_f, loc, cfg, hooks(plan, "f_"), first, late_f, middle)
        row_f.finish()
        late_a.append(loc.start(k.ax_h, k.xin))
        p = view_of(k, "a_", dpersist=k.dpersist, xin=k.xin, **vars(small_of(k)))
        attn_backward(p, row_a, loc, cfg, hooks(plan, "a_"), l, loads_a, late_a, leave)
        return row_f, row_a

    def staged(tag, array, home=None):
        return Gather(tag, array.reshape(by_block), by_block, groups, 1, None, home)

    def grad_of(k):
        return k.f_grad

    y0 = staged("y0_", f1.stage_o)
    y1 = Gather("y1_", None, stage_dims, groups, 1, lambda k, row: k.stage)
    td1, tg1 = (Total(t, None, grad_b_dims, groups, (i, 1), grad_of) for t, i in (("td_", 2), ("tg_", 0)))
    sides3 = [y0, y1, td1, tg1]
    swap_y1 = Swap("swap_")

    def third_body(k):
        loc = Local(k.sems)

        def begin(row):
            y0.start()
            swap_y1.start(k, row, own, size, k.y, k.stage, False)

        plan = dict(
            f_computed0=[y0.step],
            f_computed2=[y0.step, swap_y1.wait, y1.start],
            f_grad1=[td1.start],
            a_states2=[y1.step, td1.step, tg1.start],
            a_computed1=[td1.step, y1.step, tg1.step],
            a_tail=[tg1.step],
        )
        row_f, row_a = backward_layer(k, 1, loc, sides3, begin, plan, lambda m: None)
        for i in range(3):
            loc.start(k.f_grad.at[i], k.grad_b_o.at[i])
        loc.start(k.a_grad, k.grad_a_o)
        for side in sides3:
            side.finish()
        row_f.finish()
        row_a.finish()
        for side in sides3 + [swap_y1]:
            side.drain()
        loc.finish()

    ins, scratch = backward_names(f1, f1.dy, f0.y, f0.q1_dst)
    ins["y"] = (f1.y, VM)
    small_outs = dict(
        dgain=((2, width), F32, VM),
        dpersist=((2, persist, size), F32, VM),
        dx=((micros, own, width), BF16, VM),
    )
    outs = dict(grad_a_o=hbm(grad_a_dims), grad_b_o=hbm(grad_b_dims), **small_outs)
    scratch["stage"] = vm(stage_dims)
    for side in sides3:
        side.declare(ins, outs, scratch, groups)
    swap_y1.declare(scratch)
    b1 = launch("backward_1", 2, third_body, ins, outs, scratch)

    small_rows = gain_rows + 4 * persist
    tu1 = Total("tu1_", b1.grad_b_o, grad_b_dims, groups, (1, 1), None, "scratch")
    ta1 = Total("ta1_", b1.grad_a_o, grad_a_dims, groups, (0, 1), None, "scratch")
    td0, tg0, tu0 = (
        Total(t, None, grad_b_dims, groups, (i, 1), grad_of, "scratch")
        for t, i in (("td_", 2), ("tg_", 0), ("tu_", 1))
    )
    ta0 = Total("ta0_", None, grad_a_dims, groups, (0, 1), lambda k: k.a_grad, "scratch")
    g1 = Gather("g1_", None, by_block, groups, 1, lambda k, row: k.staged1)
    g0 = [
        Gather(f"g0{m}_", None, by_block[1:], groups, 0, lambda k, row, m=m: k.staged0.at[m], "scratch")
        for m in range(micros)
    ]

    def blocked(stage, staged, m):
        for b in range(blocks):
            staged[m, b] = stage[m, b * BLOCK : (b + 1) * BLOCK, :]
    sides4 = [tu1, ta1, td0, tg0, tu0, ta0, g1, *g0]
    swap_g1, swaps0 = Swap("swap_"), [Swap(f"swap{m}_") for m in range(micros)]

    def last_body(k):
        loc = Local(k.sems)
        push = pusher(k.psend, k.precv)
        load_y = loc.start(k.y0_buf, k.whole)
        loads = [
            loc.start(a, b)
            for a, b in (
                (k.bg1, k.res_b.at[1, pl.ds(0, 1)]), (k.bd1, k.res_b.at[1, pl.ds(2, 1)]),
            )
        ]

        def begin(row):
            tu1.start()
            ta1.start()
            swap_g1.start(k, row, own, size, k.dy, k.stage, False)

        def start_g1():
            swap_g1.wait()
            for m in range(micros):
                blocked(k.stage, k.staged1, m)
            g1.start()

        def dx_done(m):
            row = ta0.row
            swaps0[m].start(
                k, row, own, size, k.dx.at[pl.ds(m, 1)], k.stage0.at[pl.ds(m, 1)], False
            )

        plan = dict(
            f_gathered0=[tu1.step, ta1.step],
            f_computed0=[start_g1],
            f_computed1=[tu1.step, ta1.step],
            f_computed2=[g1.step],
            f_grad1=[td0.start],
            a_states2=[g1.step, td0.step, tg0.start, tu0.start],
            a_computed1=[td0.step, tg0.step, tu0.step],
            a_computed2=[tg0.step, tu0.step],
            a_grads=[ta0.start],
        )
        row_f, row = backward_layer(k, 0, loc, sides4, begin, plan, dx_done)
        for m in range(micros - 1):
            swaps0[m].wait()
            blocked(k.stage0, k.staged0, m)
            g0[m].start()
        for i in range(half_gains):
            lanes_here = slice(i * 128, (i + 1) * 128)
            for j, ref in enumerate((k.dgain, k.dgain1)):
                for kind in range(2):
                    at = (j * 2 + kind) * half_gains + i
                    k.smalls[at : at + 1, :] = ref[kind : kind + 1, lanes_here]
        for j, ref in enumerate((k.dpersist, k.dpersist1)):
            for kind in range(2):
                at = gain_rows + (j * 2 + kind) * persist
                k.smalls[at : at + persist, :] = ref[kind]
        swaps0[-1].wait()
        blocked(k.stage0, k.staged0, micros - 1)
        g0[-1].start()
        pushes = []
        for i in range(1, groups):
            to = (row.s, row.r, lax.rem(row.c + i, groups))
            pushes.append(push(k.smalls, k.small_box.at[i], i, to))
        for copy in loads:
            loc.wait(copy)

        def all_restored(slot):
            for m in range(micros):
                for b in range(blocks):
                    where = pl.ds(b * BLOCK, BLOCK)
                    k.halves[slot, m, where, :] = k.whole[m, k.back[m, b]]

        loc.wait(load_y)
        all_restored(0)
        loc.wait(loc.start(k.y1_buf, k.whole))
        all_restored(1)
        moved, kept_here = [], []
        mine_lanes = pl.ds(pl.multiple_of(row.s * size, 128), size)

        def give(i, pair, out):
            moved.append(push(pair.at[1 - row.s], out, groups + 8 + i, row.sib))
            kept_here.append(loc.start(pair.at[row.s], out))

        give(0, k.halves.at[pl.ds(0, 2)], k.acts_o.at[:, :, mine_lanes])

        for g in g0:
            g.step()
        ta0.step()
        g1.finish()
        loc.wait(loc.start(k.g1_dst, k.whole))
        all_restored(3)
        for g in g0:
            g.step()
        ta0.step()
        for total in (td0, tg0, tu0, tu1, ta1):
            total.finish()
        k.res_b[0, pl.ds(2, 1)] = k.td_sum[...]
        k.res_b[0, pl.ds(0, 1)] = k.tg_sum[...]
        k.res_b[0, pl.ds(1, 1)] = k.tu_sum[...]
        k.res_b[1, pl.ds(1, 1)] = k.tu1_sum[...]
        k.res_a[1] = k.ta1_sum[...]
        give(1, k.res_b, k.grad_b.at[row.s])
        for copy in pushes:
            copy.wait_recv()
        total = k.smalls[...]
        for i in range(1, groups):
            total = total + k.small_box[i]
        k.small_sum[...] = total
        gains = []
        for i, ps, pr in others(row):
            src = k.small_sum.at[pl.ds(0, gain_rows), :]
            gains.append(push(src, k.gain_box.at[i], groups + i, (ps, pr, row.c)))
        ta0.finish()
        k.res_a[0] = k.ta0_sum[...]
        give(2, k.res_a, k.grad_a.at[row.s])
        for m, g in enumerate(g0):
            g.finish()
            buf = getattr(k, f"g0{m}_dst")
            for b in range(blocks):
                k.halves[2, m, pl.ds(b * BLOCK, BLOCK), :] = buf[k.back[m, b]]
        give(3, k.halves.at[pl.ds(2, 2)], k.grads_o.at[:, :, mine_lanes])
        for copy in gains:
            copy.wait_recv()
        total = k.small_sum[0:gain_rows, :]
        for i in range(1, 8):
            total = total + k.gain_box[i]
        k.gain_o[...] = total
        k.persist_o[...] = k.small_sum[gain_rows:, :]
        for copy in moved:
            copy.wait()
        for copy in pushes + gains:
            copy.wait_send()
        for side in sides4:
            side.finish()
        row_f.finish()
        row.finish()
        for side in sides4 + [swap_g1] + swaps0:
            side.drain()
        loc.finish()

    ins, scratch = backward_names(f0, b1.dx, f0.x, f0.q0_o)
    ins.update(
        y0_buf=(b1.y0_dst, HB),
        y1_buf=(b1.y1_dst.reshape(b1.y0_dst.shape), HB),
        bg1=(b1.tg_sum, HB),
        bd1=(b1.td_sum, HB),
        dgain1=(b1.dgain, VM),
        dpersist1=(b1.dpersist, VM),
        back=(back_picks, SM),
    )
    outs = dict(
        acts_o=((micros, rows, features), BF16, VM),
        grads_o=((micros, rows, features), BF16, VM),
        grad_a=((2,) + ta0.dims, BF16, VM),
        grad_b=((2, 3) + tu0.dims[1:], BF16, VM),
        gain_o=((gain_rows, 128), F32, VM),
        persist_o=((4 * persist, 128), F32, VM),
    )
    scratch.update(
        stage=vm(stage_dims),
        stage0=vm(stage_dims),
        whole=vm((micros, total_blocks, BLOCK, size)),
        staged0=vm(by_block),
        staged1=vm(by_block),
        halves=vm((4,) + stage_dims),
        res_a=vm((2,) + ta0.dims),
        res_b=vm((2, 3) + tu0.dims[1:]),
        smalls=vm((small_rows, 128), F32),
        small_box=vm((groups, small_rows, 128), F32),
        small_sum=vm((small_rows, 128), F32),
        gain_box=vm((8, gain_rows, 128), F32),
        dgain=vm((2, width), F32),
        dpersist=vm((2, persist, size), F32),
        dx=vm((micros, own, width)),
        psend=pltpu.SemaphoreType.DMA((groups + 12,)),
        precv=pltpu.SemaphoreType.DMA((groups + 12,)),
    )
    for side in sides4:
        side.declare(ins, outs, scratch, groups)
    for swap in [swap_g1] + swaps0:
        swap.declare(scratch)
    closed = launch("backward_0", 3, last_body, ins, outs, scratch)

    def cols_join(pair):
        return jnp.concatenate([pair[0], pair[1]], axis=1).astype(F32)[None]

    def rows_join(pair):
        return jnp.concatenate([pair[0].T, pair[1].T], axis=0).astype(F32)[None]

    grad_a, grad_b = closed.grad_a[:, 0], closed.grad_b
    heads = [cols_join(grad_a[:, :, i * size : (i + 1) * size]) for i in range(3)]
    grad_out = rows_join(grad_a[:, :, 3 * size :])
    grad_gate, grad_up = cols_join(grad_b[:, 0]), cols_join(grad_b[:, 1])
    grad_down = rows_join(grad_b[:, 2])
    gain_sum = closed.gain_o.reshape(2, 2, width)
    my_gain = lax.dynamic_slice_in_dim(
        lax.dynamic_index_in_dim(gain_sum, sec, 0, False), (row_id * groups + col) * share, share, 1
    )
    persist_sum = closed.persist_o.reshape(2, 2, persist, size)
    persist_sum = lax.dynamic_slice_in_dim(persist_sum, col * per, per, 2)
    mine_p = lax.dynamic_index_in_dim(persist_sum, sec, 0, False)
    got_p = lax.ppermute(
        lax.dynamic_index_in_dim(persist_sum, 1 - sec, 0, False), "section", [(0, 1), (1, 0)]
    )
    grad_persist = jnp.concatenate(
        [jnp.where(sec == 0, mine_p, got_p), jnp.where(sec == 0, got_p, mine_p)], axis=2
    )
    return (
        closed.acts_o[None],
        closed.grads_o[None],
        my_gain[0][None],
        heads[0],
        heads[1],
        heads[2],
        grad_persist[0][None],
        grad_persist[1][None],
        grad_out,
        my_gain[1][None],
        grad_gate,
        grad_up,
        grad_down,
    )


def solution(mesh):
    weight = P("section", "col", "row")
    across = P("section", "row", "col")
    gain = P("section", ("row", "col"))
    rows = P("section", None, "col", "row")
    return jax.shard_map(
        local,
        mesh=mesh,
        in_specs=(
            P(None, "col", "row"), P(None, "col", "row"), P(), P(), rows, rows, gain, weight, weight,
            weight, weight, weight, across, gain, weight, weight, across,
        ),
        out_specs=(
            rows, rows, gain, weight, weight, weight, weight, weight, across, gain, weight, weight,
            across,
        ),
        check_vma=False,
    )
```

time: 535 us -> 465 us (0.87)
  Pallas kernels: 501 us -> 432 us
    pallas_call x10 -> x4, Pallas kernels: 501 us -> 432 us  [launch(): pl.pallas_call(kernel, out_shape=tuple((jax.ShapeDtypeStruct(d, t) for d,...]
where the time goes in v3:
time: 465 us; the launch traced here: 459 us
  Pallas kernels  432 us (93%)
  local copies, waits for them, and re-layouts  14.6 us (3%)
  other arithmetic  10.5 us (2%)
    pallas_call x4, Pallas kernels, launch(): pl.pallas_call(kernel, out_shape=tuple((jax.ShapeDtypeStruct(d, t) for d,...  432 us
  transfers between devices with their start and end apart: 1, of which 0 were waited for; matrix products, arithmetic and copies ran while one was open for 2% of the time, Pallas kernels for 0%

profile of v3, /device:TPU:0, one launch (start us, length us, event | category | flops | bytes accessed | tf_op | source)
XLA Modules:
  0.0 458.9 jit_solution(6349495412652168063)
XLA Ops:
  0.6 0.0 copy-start.3
  0.7 0.0 copy-start.4
  0.7 0.7 maximum_convert_fusion.7
  1.4 0.2 dynamic_update_slice.3
  1.6 0.7 copy.70
  2.3 0.1 reshape.285
  2.4 0.9 reduce_window_sum.11
  3.2 0.7 sub.6
  3.9 0.1 fusion.1
  4.0 0.1 select_n.52
  4.1 0.1 reshape.287
  4.2 1.2 copy.65
  5.4 0.0 copy-start.5
  5.4 0.0 copy-start.6
  5.4 1.2 copy.66
  6.7 0.0 copy-start.7
  6.7 0.0 copy-done.3
  6.7 0.0 copy-start.9
  6.7 0.0 copy-start.10
  6.7 0.0 copy-start.11
  6.7 0.0 copy-start.12
  6.7 0.2 copy.67
  7.0 0.0 copy-done.4
  7.0 0.1 copy.58
  7.1 0.1 copy.59
  7.2 0.1 copy.60
  7.3 0.1 copy.61
  7.5 0.1 copy.62
  7.6 0.1 copy.63
  7.7 0.0 copy-done.7
  7.7 0.1 copy.64
  7.8 0.0 copy-done.9
  7.9 0.6 pad_multiply_fusion.refs_4_
  8.5 0.6 constant_dynamic-slice_fusion.1.refs_0_.refs_2_
  9.1 0.8 select_reduce_fusion.refs_24_
  9.9 1.4 pad_maximum_fusion.refs_2_
  11.3 0.6 select_maximum_fusion.refs_3_
  11.9 0.9 maximum_bitcast_fusion.refs_1_
  12.8 0.6 broadcast_in_dim.22.refs_5_.refs_6_.refs_17_
  13.4 129.3 %forward_0.1 = (bf16[1152,1024]{1,0:T(8,128)(2,1)}, bf16[1152,384]{1,0:T(8,128)(2,1)}, bf16[18,128,128]{2,1,0:T(8,128)(2,1)}, bf16[1152,128]{1,0:T(8,128)(2,1)},...) custom-call(s32[3,6]{1,0:T(4,128)} %constant_dynamic-slice_fusion.1., ...), custom_call_target="tpu_custom_call" | custom-call | tf_op jit(solution)/shard_map/forward_0/pallas_call | solution.py:897
  142.6 87.7 %forward_1.1 = (bf16[1152,1024]{1,0:T(8,128)(2,1)}, bf16[1152,384]{1,0:T(8,128)(2,1)}, bf16[18,128,128]{2,1,0:T(8,128)(2,1)}, bf16[1152,128]{1,0:T(8,128)(2,1)},...) custom-call(bf16[3,48,1024]{2,1,0:T(8,128)(2,1)} %get-tuple-element., ...), custom_call_target="tpu_custom_call" | custom-call | tf_op jit(solution)/shard_map/forward_1/pallas_call | solution.py:897
  230.3 86.0 %backward_1.1 = (bf16[1,1024,512]{2,1,0:T(8,128)(2,1)}, bf16[3,1024,352]{2,1,0:T(8,128)(2,1)}, f32[2,1024]{1,0:T(2,128)}, f32[2,16,128]{2,1,0:T(8,128)}, bf16[3,...) custom-call(bf16[3,48,1024]{2,1,0:T(8,128)(2,1)} %get-tuple-element., ...), custom_call_target="tpu_custom_call" | custom-call | tf_op jit(solution)/shard_map/backward_1/pallas_call | solution.py:897
  316.3 129.0 %backward_0.1 = (bf16[3,384,256]{2,1,0:T(8,128)(2,1)}, bf16[3,384,256]{2,1,0:T(8,128)(2,1)}, bf16[2,1,256,512]{3,2,1,0:T(8,128)(2,1)}, bf16[2,3,256,352]{3,2,1,0...) custom-call(bf16[3,48,1024]{2,1,0:T(8,128)(2,1)} %get-tuple-element.83.refs_0_, ...), custom_call_target="tpu_custom_call" | custom-call | tf_op jit(solution)/shard_map/backward_0/pallas_call | solution.py:897
  445.3 0.7 dynamic-slice_bitcast_fusion
  446.1 0.4 collective-permute-start
  446.4 1.5 slice_bitcast_fusion.1
  447.9 0.1 slice_bitcast_fusion.7
  448.1 0.1 constant_dynamic-slice_fusion
  448.2 0.5 slice_bitcast_fusion.8
  448.7 0.1 maximum_convert_fusion.2
  448.8 0.1 maximum_convert_fusion.1
  449.0 0.1 maximum_convert_fusion
  449.2 0.7 maximum_convert_fusion.5
  449.9 0.7 maximum_convert_fusion.4
  450.6 0.7 maximum_convert_fusion.3
  451.3 1.1 copy.76
  452.4 1.1 copy.75
  453.6 1.1 copy.74
  454.7 0.8 copy.73
  455.5 0.0 collective-permute-done
  455.5 0.7 bitcast_select_fusion
  456.2 0.6 pad_maximum_fusion.1
  456.8 0.8 copy.80
  457.7 0.8 copy.81
  (24 shorter events, 0.1 us)
Async XLA Ops:
  0.6 6.0 %copy-start.3 = (bf16[1,704,256]{2,1,0:T(8,128)(2,1)S(1)}, bf16[1,704,256]{2,1,0:T(8,128)(2,1)}, u32[]{:S(2)}) copy-start(bf16[1,704,256]{2,1,0:T(8,128)(2,1)} %param.33) | copy-start | bytes 1081348
  0.7 6.3 %copy-start.4 = (bf16[1,256,256]{2,1,0:T(8,128)(2,1)S(1)}, bf16[1,256,256]{2,1,0:T(8,128)(2,1)}, u32[]{:S(2)}) copy-start(bf16[1,256,256]{2,1,0:T(8,128)(2,1)} %param.24) | copy-start | bytes 393220
  5.4 1.8 copy-start.5
  5.4 2.0 copy-start.6
  6.7 1.0 copy-start.7
  6.7 1.1 copy-start.9
  6.7 1.8 copy-start.10
  6.7 3.2 copy-start.11
  6.7 3.2 copy-start.12
  446.1 9.4 %collective-permute-start = (f32[2,4,128]{2,1,0:T(4,128)S(1)}, f32[2,4,128]{2,1,0:T(4,128)S(1)}, u32[]{:S(2)}, u32[]{:S(2)}) collective-permute-start(f32[2,4,128]{2,1,0:T(4,128)S(1)} %dynamic-slice_bitcast_fusion), channel_id=1, source_target_pairs={{0,16},{16,0},{1,17},{17,1},{2,18},{18,2},{3,19},{19,3},{4,20},{20... | collective-permute-start | bytes 12296 | tf_op jit(solution)/shard_map/ppermute | solution.py:1648
  446.4 1.5 copy-start.2
  446.4 1.6 copy-start.8
  453.6 3.3 copy-start.1
  454.7 3.0 copy-start

commit v4 on v3

--- a/solution.py
+++ b/solution.py
@@ -14,6 +14,32 @@
 BF16 = jnp.bfloat16
 VMEM_LIMIT = 60 << 20
 N_AG, N_RS = 8, 7
+
+A, F = 0, 100
+PLACES = dict(
+    first=[
+        A, A + 10, A + 30, A + 21, A + 12, A + 32, A + 41, A + 41, F + 31, F + 32,
+    ],
+    second=[
+        A, A + 21, A + 2, A, A + 12, A + 41, A + 30, A + 32, A + 40, A + 41,
+        F + 11, F + 32, F + 41,
+    ],
+    third=[
+        F + 30, F + 32, F + 30, F + 52, F + 52, F + 50, A + 2, A + 32, A + 12, A + 31,
+        A + 32,
+    ],
+    last=[
+        F + 40, F, F, A + 31, F + 31, F + 40, F + 50, A + 10, A + 30, F + 50,
+        F + 51, A + 31, A + 1, A + 2, A + 40, A + 30, A + 60,
+    ],
+)
+
+
+def place(points, actions, fixed=()):
+    plan = {}
+    for point, action in list(zip(points, actions, strict=True)) + list(fixed):
+        plan.setdefault(point, []).append(action)
+    return plan
 
 
 def dot(a, b, ca=1, cb=0):
@@ -477,11 +503,20 @@
     ]
 
 
-def gather_first(row, full, micros):
-    row.ag_pass(full, 0)
-    if micros > 1:
-        row.ag_pass(full, 1)
+def gather_first(row, full, micros, fresh, fill=()):
+    if fresh:
+        row.ag_pass(full, 0)
+        for m in range(2, micros):
+            row.ag_start(full, m)
+    for work in fill:
+        work()
+    row.ag_pass(full, 1)
     row.ag_diag(full, 0)
+
+
+def ag_begin(row, full):
+    row.ag_start(full, 0)
+    row.ag_start(full, 1)
 
 
 def gather_more(row, full, micros, m):
@@ -491,35 +526,38 @@
         row.ag_diag(full, m + 1)
 
 
-def tail(row, micros, result, hook, between=()):
+def tail(row, micros, result, hook, between=(), relay=None):
     more = list(between)
 
     def step():
         if more:
             more.pop(0)()
 
+    row.rs_transit(micros - 2)
+    for m in range(micros - 2):
+        result(m)
+    row.rs_pair(micros - 1)
+    hook(40)
     step()
-    row.rs_transit(micros - 2)
-    row.rs_pair(micros - 1)
-    for m in range(micros - 2):
-        step()
-        result(m)
-    hook("tail")
+    result(micros - 2)
+    row.rs_transit(micros - 1)
+    if relay:
+        relay()
     step()
-    row.rs_transit(micros - 1)
-    result(micros - 2)
-    while more:
-        step()
-    hook("last")
+    if relay is None:
+        while more:
+            step()
+    hook(41)
     result(micros - 1)
-
-
-def ffn_forward(p, row, loc, cfg, hook, deliver):
+    return more
+
+
+def ffn_forward(p, row, loc, cfg, hook, deliver, relay=None):
     micros, rows, full = cfg.micros, cfg.rows, p.full
-    gather_first(row, full, micros)
+    gather_first(row, full, micros, False)
     for m in range(micros):
         row.ag_wait(full, m)
-        hook("gathered", m)
+        hook(m)
         if m >= 1:
             row.rs_pair(m - 1)
         if m >= 2:
@@ -531,24 +569,24 @@
         p.gp[here, :] = gate.astype(BF16)
         p.up[here, :] = lift.astype(BF16)
         p.act[here, :] = (gate * jax.nn.sigmoid(gate) * lift).astype(BF16)
-        hook("acted", m)
+        hook(10 + m)
         row.part[here, :] = dot(p.act[here, :], p.down_dst[0], 1, 1).astype(BF16)
         for a, b in ((p.gp, p.gp_o), (p.up, p.up_o), (p.act, p.act_o)):
             loc.start(a.at[here, :], b.at[here, :])
         row.rs_start(m)
         gather_more(row, full, micros, m)
-        hook("computed", m)
-    tail(row, micros, lambda m: deliver(m, row.rs_result(m)), hook)
-
-
-def ffn_backward(p, row, loc, cfg, hook, loads, late, deliver):
+        hook(30 + m)
+    tail(row, micros, lambda m: deliver(m, row.rs_result(m)), hook, (), relay)
+
+
+def ffn_backward(p, row, loc, cfg, hook, loads, late, deliver, relay=None):
     micros, rows, width, full = cfg.micros, cfg.rows, cfg.width, p.full
-    gather_first(row, full, micros)
+    gather_first(row, full, micros, True)
     for copy in loads:
         loc.wait(copy)
     for m in range(micros):
         row.ag_wait(full, m)
-        hook("gathered", m)
+        hook(m)
         if m >= 1:
             row.rs_pair(m - 1)
         if m >= 2:
@@ -565,7 +603,7 @@
         row.part[here, :] = total.astype(BF16)
         row.rs_start(m)
         gather_more(row, full, micros, m)
-        hook("computed", m)
+        hook(30 + m)
 
     def grad(i, left, right):
         def body():
@@ -578,12 +616,12 @@
                 at = pl.ds(pl.multiple_of(t * 256, 256), 256)
                 p.grad[i, at, :] = dot(left[:, at], right[...], 0, 0).astype(BF16)
 
-            hook("grad", i)
+            hook(50 + i)
 
         return body
 
     grads = [grad(2, full, p.act), grad(0, p.xin, p.dg), grad(1, p.xin, p.du)]
-    tail(row, micros, lambda m: deliver(m, row.rs_result(m)), hook, grads)
+    return tail(row, micros, lambda m: deliver(m, row.rs_result(m)), hook, grads, relay)
 
 
 def pair_masks(size):
@@ -718,14 +756,14 @@
                 entering[...] = factor * entering[...] + self.box[m, k].astype(F32)
 
 
-def attn_forward(p, row, loc, cfg, hook, layer, loads, deliver):
+def attn_forward(p, row, loc, cfg, hook, layer, loads, deliver, relay=None):
     micros, rows, size, full = cfg.micros, cfg.rows, cfg.size, p.full
     blocks = rows // BLOCK
     factor = size ** (-0.5)
     states = States(row, cfg.groups, p, False)
     qs, ks, vs = (pl.ds(i * size, size) for i in range(3))
     mask = pair_masks(2 * BLOCK)
-    gather_first(row, full, micros)
+    gather_first(row, full, micros, True)
     gate_columns(p.gates[layer, 0 : micros * rows // 128, :], p.gate)
     heads = Heads(p, row, cfg, layer)
     pk, pv = heads.persist()
@@ -734,7 +772,7 @@
         loc.wait(copy)
     for m in range(micros):
         row.ag_wait(full, m)
-        hook("gathered", m)
+        hook(m)
         here = pl.ds(m * rows, rows)
         loc.start(full.at[here, :], p.xin_o.at[here, :])
         p.qkv[here, :] = dot(full[here, :], p.wq[0]).astype(BF16)
@@ -749,7 +787,7 @@
         p.leaving[m] = total.astype(BF16)
         states.start(m)
         gather_more(row, full, micros, m)
-        hook("states", m)
+        hook(10 + m)
     for m in range(micros):
         here = pl.ds(m * rows, rows)
         states.wait(m)
@@ -768,7 +806,7 @@
                 reads.append(dot(q[i * BLOCK : (i + 1) * BLOCK, :], low) * factor)
                 memory = now + p.update[m * blocks + b + i]
             p.mixed[at, :] = (value + jnp.concatenate(reads, axis=0)).astype(BF16)
-        hook("mixed", m)
+        hook(20 + m)
         row.part[here, :] = dot(p.mixed[here, :], p.wo_dst[0], 1, 1).astype(BF16)
         loc.start(p.mixed.at[here, :], p.mixed_o.at[here, :])
         row.rs_start(m)
@@ -776,13 +814,13 @@
             row.rs_pair(m - 1)
         if m >= 2:
             row.rs_transit(m - 2)
-        hook("computed", m)
+        hook(30 + m)
     loc.start(p.state, p.state_o)
-    tail(row, micros, lambda m: deliver(m, row.rs_result(m)), hook)
+    tail(row, micros, lambda m: deliver(m, row.rs_result(m)), hook, (), relay)
     states.drain()
 
 
-def attn_backward(p, row, loc, cfg, hook, layer, loads, late, deliver):
+def attn_backward(p, row, loc, cfg, hook, layer, loads, late, deliver, fill, relay=None):
     micros, rows, size, width, full = cfg.micros, cfg.rows, cfg.size, cfg.width, p.full
     blocks = rows // BLOCK
     factor = size ** (-0.5)
@@ -795,12 +833,12 @@
     heads = Heads(p, row, cfg, layer)
     pk, pv = heads.persist()
     keep = heads.own()
-    gather_first(row, full, micros)
+    gather_first(row, full, micros, False, fill)
     for copy in loads:
         loc.wait(copy)
     for m in range(micros):
         row.ag_wait(full, m)
-        hook("gathered", m)
+        hook(m)
         here = pl.ds(m * rows, rows)
         p.dmix[here, :] = dot(full[here, :], p.wo[0]).astype(BF16)
         total = jnp.zeros((size, size), F32)
@@ -812,7 +850,7 @@
         p.leaving[m] = total.astype(BF16)
         states.start(m)
         gather_more(row, full, micros, m)
-        hook("states", m)
+        hook(10 + m)
     for m in range(micros):
         here = pl.ds(m * rows, rows)
         states.wait(m)
@@ -856,7 +894,7 @@
             row.rs_pair(m - 1)
         if m >= 2:
             row.rs_transit(m - 2)
-        hook("computed", m)
+        hook(30 + m)
 
     def out_grad():
         for copy in late:
@@ -873,9 +911,9 @@
             at = pl.ds(pl.multiple_of(t * 256, 256), 256)
             p.grad[0, at, in_cols] = dot(p.xin[:, at], p.dqkv[...], 0, 0).astype(BF16)
 
-        hook("grads")
-
-    tail(row, micros, lambda m: deliver(m, row.rs_result(m)), hook, [out_grad, qkv_grad])
+        hook(60)
+
+    tail(row, micros, lambda m: deliver(m, row.rs_result(m)), hook, [out_grad, qkv_grad], relay)
     states.drain()
 
 
@@ -1028,8 +1066,8 @@
         )
 
     def hooks(plan, prefix):
-        def hook(point, at=""):
-            for action in plan.get(prefix + point + str(at), ()):
+        def hook(point):
+            for action in plan.get(prefix + point, ()):
                 action()
 
         return hook
@@ -1083,11 +1121,14 @@
             k.y[m] = (k.mid[m] + summed).astype(BF16)
 
         p = view_of(k, "a_", wq=wq, wo_dst=k.wo_dst, **vars(small))
-        attn_forward(p, row_a, loc, cfg, hooks(plan, "a_"), l, loads, middle)
+        attn_forward(
+            p, row_a, loc, cfg, hooks(plan, A), l, loads, middle,
+            lambda: row_f.ag_pass(k.f_full, 0),
+        )
         row_a.finish()
         loc.start(k.wo_dst, k.wo_o)
         p = view_of(k, "f_", gate_dst=k.gate_dst, up_dst=k.up_dst, down_dst=k.down_dst)
-        ffn_forward(p, row_f, loc, cfg, hooks(plan, "f_"), leave)
+        ffn_forward(p, row_f, loc, cfg, hooks(plan, F), leave)
         for i, w in enumerate((k.gate_dst, k.up_dst, k.down_dst)):
             loc.start(w, k.w_o.at[pl.ds(i, 1)])
         return row_f
@@ -1182,18 +1223,17 @@
         swap1.wait()
         for m in range(micros):
             norm_to(k.a_full, gain, k.x[m].astype(F32), row.span(m, row.s, row.r))
-            row.ag_start(k.a_full, m)
+        ag_begin(row, k.a_full)
         loc.start(k.q0_dst, k.q0_o)
-        plan = dict(
-            a_gathered0=[gate0.step, up0.step, down0.start],
-            a_states2=[gate0.step, up0.step],
-            a_mixed0=[wo0.finish],
-            a_computed1=[down0.step],
-            a_tail=[down0.step],
-            f_gathered0=[gate0.finish, up0.finish],
-            f_acted0=[down0.finish, q1.start],
-            f_computed1=[q1.step],
-            f_tail=[q1.step],
+        plan = place(
+            PLACES["first"],
+            [
+                gate0.step, up0.step, down0.start, gate0.step, up0.step, down0.step, down0.step,
+                q1.start, q1.step, q1.step,
+            ],
+            [
+                (A + 20, wo0.finish), (F, gate0.finish), (F, up0.finish), (F + 10, down0.finish),
+            ],
         )
         small_refs = SimpleNamespace(line=k.line, gains=k.gains, gates=k.gates, starts=k.starts)
         row_f = forward_layer(k, 0, k.x, k.q0_dst, loc, [], plan, row, small_refs)
@@ -1261,8 +1301,7 @@
         greet_all(row)
         for side in sides2:
             side.bind(k, row, groups)
-        for m in range(micros):
-            row.ag_start(k.a_full, m)
+        ag_begin(row, k.a_full)
         for side in (wo1, gate1, up1):
             side.start()
         swap_y.start(k, row, own, size, k.x, k.stage_o, False)
@@ -1273,19 +1312,15 @@
                 blocks_from(k.cot_dst, k.picks, k.stage, m)
             swap_c.start(k, row, own, size, k.stage, k.dy, True)
 
-        plan = dict(
-            a_states0=[wo1.step, gate1.step],
-            a_states1=[wo1.step],
-            a_states2=[up1.step, down1.start],
-            a_mixed0=[wo1.finish],
-            a_computed0=[gate1.step],
-            a_computed1=[up1.step, down1.step],
-            a_tail=[down1.step, cot.start],
-            f_gathered0=[gate1.finish, up1.finish],
-            f_acted0=[down1.finish],
-            f_computed0=[cot.step],
-            f_computed2=[cot.step],
-            f_last=[deal_cot],
+        plan = place(
+            PLACES["second"],
+            [
+                wo1.step, gate1.step, wo1.step, up1.step, down1.start, gate1.step, up1.step, down1.step,
+                down1.step, cot.start, cot.step, cot.step, deal_cot,
+            ],
+            [
+                (A + 20, wo1.finish), (F, gate1.finish), (F, up1.finish), (F + 10, down1.finish),
+            ],
         )
         row_f = forward_layer(k, 1, k.x, k.wq, loc, loads, plan, row, small_of(k))
         for side in sides2:
@@ -1347,8 +1382,7 @@
         greet_all(row_f)
         for side in sides:
             side.bind(k, row_f, groups)
-        for m in range(micros):
-            row_f.ag_start(k.f_full, m)
+        ag_begin(row_f, k.f_full)
         swaps_begin(row_f)
         gain_a, gain_f = gain_row(k, cfg, l, 0), gain_row(k, cfg, l, 1)
         k.dgain[...] = jnp.zeros_like(k.dgain)
@@ -1366,11 +1400,18 @@
             k.dgain[0:1, :] += gains
             dx_done(m)
 
-        ffn_backward(view_of(k, "f_", xin=k.xin), row_f, loc, cfg, hooks(plan, "f_"), first, late_f, middle)
+        left = ffn_backward(
+            view_of(k, "f_", xin=k.xin), row_f, loc, cfg, hooks(plan, F), first, late_f, middle,
+            lambda: row_a.ag_pass(k.a_full, 0),
+        )
         row_f.finish()
-        late_a.append(loc.start(k.ax_h, k.xin))
+
+        def load_xin():
+            late_a.append(loc.start(k.ax_h, k.xin))
+
+        left = list(left) + [load_xin]
         p = view_of(k, "a_", dpersist=k.dpersist, xin=k.xin, **vars(small_of(k)))
-        attn_backward(p, row_a, loc, cfg, hooks(plan, "a_"), l, loads_a, late_a, leave)
+        attn_backward(p, row_a, loc, cfg, hooks(plan, A), l, loads_a, late_a, leave, left)
         return row_f, row_a
 
     def staged(tag, array, home=None):
@@ -1392,13 +1433,16 @@
             y0.start()
             swap_y1.start(k, row, own, size, k.y, k.stage, False)
 
-        plan = dict(
-            f_computed0=[y0.step],
-            f_computed2=[y0.step, swap_y1.wait, y1.start],
-            f_grad1=[td1.start],
-            a_states2=[y1.step, td1.step, tg1.start],
-            a_computed1=[td1.step, y1.step, tg1.step],
-            a_tail=[tg1.step],
+        def start_y1():
+            swap_y1.wait()
+            y1.start()
+
+        plan = place(
+            PLACES["third"],
+            [
+                y0.step, y0.step, start_y1, td1.start, y1.step, td1.step, tg1.start, td1.step, y1.step,
+                tg1.step, tg1.step,
+            ],
         )
         row_f, row_a = backward_layer(k, 1, loc, sides3, begin, plan, lambda m: None)
         for i in range(3):
@@ -1468,28 +1512,26 @@
                 blocked(k.stage, k.staged1, m)
             g1.start()
 
-        def dx_done(m):
-            row = ta0.row
-            swaps0[m].start(
-                k, row, own, size, k.dx.at[pl.ds(m, 1)], k.stage0.at[pl.ds(m, 1)], False
-            )
-
-        plan = dict(
-            f_gathered0=[tu1.step, ta1.step],
-            f_computed0=[start_g1],
-            f_computed1=[tu1.step, ta1.step],
-            f_computed2=[g1.step],
-            f_grad1=[td0.start],
-            a_states2=[g1.step, td0.step, tg0.start, tu0.start],
-            a_computed1=[td0.step, tg0.step, tu0.step],
-            a_computed2=[tg0.step, tu0.step],
-            a_grads=[ta0.start],
-        )
-        row_f, row = backward_layer(k, 0, loc, sides4, begin, plan, dx_done)
-        for m in range(micros - 1):
+        def gather_g0(m):
             swaps0[m].wait()
             blocked(k.stage0, k.staged0, m)
             g0[m].start()
+
+        def dx_done(m):
+            swaps0[m].start(
+                k, ta0.row, own, size, k.dx.at[pl.ds(m, 1)], k.stage0.at[pl.ds(m, 1)], False
+            )
+            if m >= 1:
+                gather_g0(m - 1)
+
+        plan = place(
+            PLACES["last"],
+            [
+                tu1.step, ta1.step, start_g1, tu1.step, ta1.step, g1.step, td0.start, g1.step, td0.step,
+                tg0.start, tu0.start, td0.step, tg0.step, tu0.step, tg0.step, tu0.step, ta0.start,
+            ],
+        )
+        row_f, row = backward_layer(k, 0, loc, sides4, begin, plan, dx_done)
         for i in range(half_gains):
             lanes_here = slice(i * 128, (i + 1) * 128)
             for j, ref in enumerate((k.dgain, k.dgain1)):
@@ -1500,9 +1542,7 @@
             for kind in range(2):
                 at = gain_rows + (j * 2 + kind) * persist
                 k.smalls[at : at + persist, :] = ref[kind]
-        swaps0[-1].wait()
-        blocked(k.stage0, k.staged0, micros - 1)
-        g0[-1].start()
+        gather_g0(micros - 1)
         pushes = []
         for i in range(1, groups):
             to = (row.s, row.r, lax.rem(row.c + i, groups))

time: 465 us -> 442 us (0.951)
  Pallas kernels: 432 us -> 409 us
    pallas_call x4, Pallas kernels: 432 us -> 409 us  [launch(): pl.pallas_call(kernel, out_shape=tuple((jax.ShapeDtypeStruct(d, t) for d,...]
where the time goes in v4:
time: 442 us; the launch traced here: 436 us
  Pallas kernels  409 us (93%)
  local copies, waits for them, and re-layouts  14.6 us (3%)
  other arithmetic  10.5 us (2%)
    pallas_call x4, Pallas kernels, launch(): pl.pallas_call(kernel, out_shape=tuple((jax.ShapeDtypeStruct(d, t) for d,...  409 us
  transfers between devices with their start and end apart: 1, of which 0 were waited for; matrix products, arithmetic and copies ran while one was open for 2% of the time, Pallas kernels for 0%

profile of v4, /device:TPU:0, one launch (start us, length us, event | category | flops | bytes accessed | tf_op | source)
XLA Modules:
  0.0 436.4 jit_solution(9878226407160725435)
XLA Ops:
  0.6 0.0 copy-start.3
  0.7 0.0 copy-start.4
  0.7 0.7 maximum_convert_fusion.7
  1.4 0.2 dynamic_update_slice.3
  1.6 0.7 copy.70
  2.3 0.1 reshape.285
  2.4 0.9 reduce_window_sum.11
  3.2 0.7 sub.6
  3.9 0.1 fusion.1
  4.0 0.1 select_n.52
  4.1 0.1 reshape.287
  4.2 1.2 copy.65
  5.4 0.0 copy-start.5
  5.4 0.0 copy-start.6
  5.4 1.2 copy.66
  6.7 0.0 copy-start.7
  6.7 0.0 copy-done.3
  6.7 0.0 copy-start.9
  6.7 0.0 copy-start.10
  6.7 0.0 copy-start.11
  6.7 0.0 copy-start.12
  6.7 0.2 copy.67
  7.0 0.1 copy.58
  7.1 0.1 copy.59
  7.2 0.1 copy.60
  7.3 0.1 copy.61
  7.5 0.1 copy.62
  7.6 0.1 copy.63
  7.7 0.1 copy.64
  7.9 0.6 pad_multiply_fusion.refs_4_
  8.5 0.0 copy-done.10
  8.5 0.6 constant_dynamic-slice_fusion.1.refs_0_.refs_2_
  9.1 0.8 select_reduce_fusion.refs_24_
  9.9 0.0 copy-done.11
  9.9 1.4 pad_maximum_fusion.refs_2_
  11.3 0.6 select_maximum_fusion.refs_3_
  11.9 0.9 maximum_bitcast_fusion.refs_1_
  12.8 0.6 broadcast_in_dim.22.refs_5_.refs_6_.refs_17_
  13.4 123.0 %forward_0.1 = (bf16[1152,1024]{1,0:T(8,128)(2,1)}, bf16[1152,384]{1,0:T(8,128)(2,1)}, bf16[18,128,128]{2,1,0:T(8,128)(2,1)}, bf16[1152,128]{1,0:T(8,128)(2,1)},...) custom-call(s32[3,6]{1,0:T(4,128)} %constant_dynamic-slice_fusion.1., ...), custom_call_target="tpu_custom_call" | custom-call | tf_op jit(solution)/shard_map/forward_0/pallas_call | solution.py:935
  136.3 82.6 %forward_1.1 = (bf16[1152,1024]{1,0:T(8,128)(2,1)}, bf16[1152,384]{1,0:T(8,128)(2,1)}, bf16[18,128,128]{2,1,0:T(8,128)(2,1)}, bf16[1152,128]{1,0:T(8,128)(2,1)},...) custom-call(bf16[3,48,1024]{2,1,0:T(8,128)(2,1)} %get-tuple-element., ...), custom_call_target="tpu_custom_call" | custom-call | tf_op jit(solution)/shard_map/forward_1/pallas_call | solution.py:935
  218.9 78.7 %backward_1.1 = (bf16[1,1024,512]{2,1,0:T(8,128)(2,1)}, bf16[3,1024,352]{2,1,0:T(8,128)(2,1)}, f32[2,1024]{1,0:T(2,128)}, f32[2,16,128]{2,1,0:T(8,128)}, bf16[3,...) custom-call(bf16[3,48,1024]{2,1,0:T(8,128)(2,1)} %get-tuple-element., ...), custom_call_target="tpu_custom_call" | custom-call | tf_op jit(solution)/shard_map/backward_1/pallas_call | solution.py:935
  297.6 125.2 %backward_0.1 = (bf16[3,384,256]{2,1,0:T(8,128)(2,1)}, bf16[3,384,256]{2,1,0:T(8,128)(2,1)}, bf16[2,1,256,512]{3,2,1,0:T(8,128)(2,1)}, bf16[2,3,256,352]{3,2,1,0...) custom-call(bf16[3,48,1024]{2,1,0:T(8,128)(2,1)} %get-tuple-element.83.refs_0_, ...), custom_call_target="tpu_custom_call" | custom-call | tf_op jit(solution)/shard_map/backward_0/pallas_call | solution.py:935
  422.8 0.7 dynamic-slice_bitcast_fusion
  423.6 0.4 collective-permute-start
  423.9 1.5 slice_bitcast_fusion.1
  425.5 0.1 slice_bitcast_fusion.7
  425.6 0.0 copy-done.8
  425.6 0.1 constant_dynamic-slice_fusion
  425.7 0.5 slice_bitcast_fusion.8
  426.2 0.1 maximum_convert_fusion.2
  426.4 0.1 maximum_convert_fusion.1
  426.5 0.1 maximum_convert_fusion
  426.7 0.7 maximum_convert_fusion.5
  427.4 0.7 maximum_convert_fusion.4
  428.1 0.7 maximum_convert_fusion.3
  428.8 1.1 copy.76
  430.0 1.1 copy.75
  431.1 1.1 copy.74
  432.2 0.8 copy.73
  433.0 0.0 collective-permute-done
  433.0 0.7 bitcast_select_fusion
  433.7 0.6 pad_maximum_fusion.1
  434.3 0.8 copy.80
  435.2 0.8 copy.81
  (24 shorter events, 0.1 us)
Async XLA Ops:
  0.6 6.0 %copy-start.3 = (bf16[1,704,256]{2,1,0:T(8,128)(2,1)S(1)}, bf16[1,704,256]{2,1,0:T(8,128)(2,1)}, u32[]{:S(2)}) copy-start(bf16[1,704,256]{2,1,0:T(8,128)(2,1)} %param.33) | copy-start | bytes 1081348
  0.7 6.3 %copy-start.4 = (bf16[1,256,256]{2,1,0:T(8,128)(2,1)S(1)}, bf16[1,256,256]{2,1,0:T(8,128)(2,1)}, u32[]{:S(2)}) copy-start(bf16[1,256,256]{2,1,0:T(8,128)(2,1)} %param.24) | copy-start | bytes 393220
  5.4 1.8 copy-start.5
  5.4 2.0 copy-start.6
  6.7 1.0 copy-start.7
  6.7 1.1 copy-start.9
  6.7 1.8 copy-start.10
  6.7 3.2 copy-start.11
  6.7 3.2 copy-start.12
  423.6 9.4 %collective-permute-start = (f32[2,4,128]{2,1,0:T(4,128)S(1)}, f32[2,4,128]{2,1,0:T(4,128)S(1)}, u32[]{:S(2)}, u32[]{:S(2)}) collective-permute-start(f32[2,4,128]{2,1,0:T(4,128)S(1)} %dynamic-slice_bitcast_fusion), channel_id=1, source_target_pairs={{0,16},{16,0},{1,17},{17,1},{2,18},{18,2},{3,19},{19,3},{4,20},{20... | collective-permute-start | bytes 12296 | tf_op jit(solution)/shard_map/ppermute | solution.py:1688
  423.9 1.5 copy-start.2
  423.9 1.6 copy-start.8
  431.1 3.3 copy-start.1
  432.2 3.0 copy-start

commit v5 on v4

--- a/solution.py
+++ b/solution.py
@@ -15,14 +15,13 @@
 VMEM_LIMIT = 60 << 20
 N_AG, N_RS = 8, 7
 
-A, F = 0, 100
+A, F, NEXT = 0, 100, 200
 PLACES = dict(
     first=[
         A, A + 10, A + 30, A + 21, A + 12, A + 32, A + 41, A + 41, F + 31, F + 32,
-    ],
-    second=[
-        A, A + 21, A + 2, A, A + 12, A + 41, A + 30, A + 32, A + 40, A + 41,
-        F + 11, F + 32, F + 41,
+        F + 40, NEXT, NEXT, F + 40, F + 41,
+        NEXT + 12, NEXT + 2, NEXT + 12, NEXT + 41, NEXT + 30, NEXT + 32, NEXT + 40,
+        NEXT + 41, NEXT + F + 11, NEXT + F + 32, NEXT + F + 41,
     ],
     third=[
         F + 30, F + 32, F + 30, F + 52, F + 52, F + 50, A + 2, A + 32, A + 12, A + 31,
@@ -756,20 +755,18 @@
                 entering[...] = factor * entering[...] + self.box[m, k].astype(F32)
 
 
-def attn_forward(p, row, loc, cfg, hook, layer, loads, deliver, relay=None):
+def attn_forward(p, row, loc, cfg, hook, layer, fresh, deliver, relay=None):
     micros, rows, size, full = cfg.micros, cfg.rows, cfg.size, p.full
     blocks = rows // BLOCK
     factor = size ** (-0.5)
     states = States(row, cfg.groups, p, False)
     qs, ks, vs = (pl.ds(i * size, size) for i in range(3))
     mask = pair_masks(2 * BLOCK)
-    gather_first(row, full, micros, True)
+    gather_first(row, full, micros, fresh)
     gate_columns(p.gates[layer, 0 : micros * rows // 128, :], p.gate)
     heads = Heads(p, row, cfg, layer)
     pk, pv = heads.persist()
     keep = heads.own()
-    for copy in loads:
-        loc.wait(copy)
     for m in range(micros):
         row.ag_wait(full, m)
         hook(m)
@@ -1028,6 +1025,8 @@
             prefix + "full": vm((all_rows, width)),
         }
 
+    shared_rows = ("part", "pair", "both", "transit", "final")
+
     def attn_scratch(prefix):
         names = dict(
             update=vm((micros * blocks, size, size), F32),
@@ -1108,7 +1107,7 @@
         )
         return outs, {**attn_scratch("a_"), **ffn_scratch("f_")}
 
-    def forward_layer(k, l, x, wq, loc, loads, plan, row_a, small):
+    def forward_layer(k, l, x, wq, loc, plan, base, row_a, small, fresh, leave, relay):
         row_f = rows_of(k, "f_")
         gain_f = gain_row(small, cfg, l, 1)
 
@@ -1117,29 +1116,26 @@
             norm_to(k.f_full, gain_f, k.mid[m], row_f.span(m, row_f.s, row_f.r))
             row_f.ag_start(k.f_full, m)
 
-        def leave(m, summed):
+        def leave_y(m, summed):
             k.y[m] = (k.mid[m] + summed).astype(BF16)
+            leave(m)
 
         p = view_of(k, "a_", wq=wq, wo_dst=k.wo_dst, **vars(small))
         attn_forward(
-            p, row_a, loc, cfg, hooks(plan, A), l, loads, middle,
+            p, row_a, loc, cfg, hooks(plan, base), l, fresh, middle,
             lambda: row_f.ag_pass(k.f_full, 0),
         )
         row_a.finish()
         loc.start(k.wo_dst, k.wo_o)
         p = view_of(k, "f_", gate_dst=k.gate_dst, up_dst=k.up_dst, down_dst=k.down_dst)
-        ffn_forward(p, row_f, loc, cfg, hooks(plan, F), leave)
+        ffn_forward(p, row_f, loc, cfg, hooks(plan, base + F), leave_y, relay)
+        row_f.finish()
         for i, w in enumerate((k.gate_dst, k.up_dst, k.down_dst)):
             loc.start(w, k.w_o.at[pl.ds(i, 1)])
-        return row_f
-
-    def one_b(tag, layer, which, array):
-        view = None
-        if array is None:
-            view = lambda k, row: k.shards_b.at[layer, pl.ds(which, 1)]
-        else:
-            view = lambda k, row: getattr(k, tag + "src").at[layer, pl.ds(which, 1)]
-        return Gather(tag, array, one_dims, groups, 1, view, "scratch")
+
+    def one_b(tag, layer, which):
+        view = lambda k, row: k.shards_b.at[layer, pl.ds(which, 1)]
+        return Gather(tag, None, one_dims, groups, 1, view, "scratch")
 
     def q_of(ref, layer):
         return ref.at[layer, :, :, pl.ds(0, 3 * size)]
@@ -1159,10 +1155,15 @@
     deal = Gather("deal_", tokens_b, by_block, groups, 1, lanes_of_core("deal_src"), "scratch")
     q0 = Gather("q0_", None, q_dims, groups, 1, lambda k, row: q_of(k.shards_a, 0), "scratch")
     wo0 = Gather("wo_", None, o_dims, groups, 1, lambda k, row: o_of(k.shards_a, 0), "scratch")
-    gate0, up0, down0 = (one_b(t, 0, i, None) for i, t in enumerate(("gate_", "up_", "down_")))
-    q1 = Gather("q1_", None, q_dims, groups, 1, lambda k, row: q_of(k.shards_a, 1))
-    sides1 = [deal, q0, wo0, gate0, up0, down0, q1]
-    swap1 = Swap("swap_")
+    gate0, up0, down0 = (one_b(t, 0, i) for i, t in enumerate(("gate_", "up_", "down_")))
+    q1 = Gather("q1_", None, q_dims, groups, 1, lambda k, row: q_of(k.shards_a, 1), "scratch")
+    wo1 = Gather("L1_wo_", None, o_dims, groups, 1, lambda k, row: o_of(k.shards_a, 1), "scratch")
+    gate1, up1, down1 = (
+        one_b(t, 1, i) for i, t in enumerate(("L1_gate_", "L1_up_", "L1_down_"))
+    )
+    cot = Gather("cot_", cotangent_b, by_block, groups, 1, lanes_of_core("cot_src"), "scratch")
+    sides1 = [deal, q0, wo0, gate0, up0, down0, q1, wo1, gate1, up1, down1, cot]
+    swap1, swap_y, swap_c = Swap("swap_"), Swap("swapy_"), Swap("swapc_")
 
     def first_body(k):
         row = rows_of(k, "a_")
@@ -1225,30 +1226,59 @@
             norm_to(k.a_full, gain, k.x[m].astype(F32), row.span(m, row.s, row.r))
         ag_begin(row, k.a_full)
         loc.start(k.q0_dst, k.q0_o)
+        def deal_cot():
+            cot.finish()
+            for m in range(micros):
+                blocks_from(k.cot_dst, k.picks, k.stage_c, m)
+            swap_c.start(k, row, own, size, k.stage_c, k.dy, True)
+
         plan = place(
             PLACES["first"],
             [
                 gate0.step, up0.step, down0.start, gate0.step, up0.step, down0.step, down0.step,
-                q1.start, q1.step, q1.step,
+                q1.start, q1.step, q1.step, wo1.start, wo1.step, wo1.step, gate1.start, up1.start,
+                down1.start, gate1.step, up1.step, down1.step, gate1.step, up1.step, down1.step,
+                cot.start, cot.step, cot.step, deal_cot,
             ],
             [
                 (A + 20, wo0.finish), (F, gate0.finish), (F, up0.finish), (F + 10, down0.finish),
+                (NEXT, q1.finish), (NEXT + 20, wo1.finish), (NEXT + F, gate1.finish),
+                (NEXT + F, up1.finish), (NEXT + F + 10, down1.finish),
             ],
         )
         small_refs = SimpleNamespace(line=k.line, gains=k.gains, gates=k.gates, starts=k.starts)
-        row_f = forward_layer(k, 0, k.x, k.q0_dst, loc, [], plan, row, small_refs)
+        second = SimpleNamespace(**{**vars(k), **vars(view_of(k, "L1_"))})
+        row_next = rows_of(second, "a_")
+        gain_next = gain_row(small_refs, cfg, 1, 0)
+
+        def begin_next(m):
+            rows_here = row_next.span(m, row_next.s, row_next.r)
+            norm_to(second.a_full, gain_next, k.y[m].astype(F32), rows_here)
+            row_next.ag_start(second.a_full, m)
+
+        forward_layer(
+            k, 0, k.x, k.q0_dst, loc, plan, A, row, small_refs, True, begin_next,
+            lambda: row_next.ag_pass(second.a_full, 0),
+        )
+        swap_y.start(k, row, own, size, k.y, k.stage_o, False)
+        forward_layer(
+            second, 1, k.y, k.q1_dst, loc, plan, NEXT, row_next, small_refs, False, lambda m: None,
+            None,
+        )
+        loc.start(k.q1_dst, k.q1_o)
         for side in sides1:
             side.finish()
+        swap_y.wait()
+        swap_c.wait()
         for copy in crossing + small + late:
             copy.wait_send()
-        row.finish()
-        row_f.finish()
-        for side in sides1:
+        for side in sides1 + [swap1, swap_y, swap_c]:
             side.drain()
-        swap1.drain()
         loc.finish()
 
     outs, scratch = forward_names(0)
+    for names, into in zip(forward_names(1), (outs, scratch)):
+        into.update({"L1_" + a: b for a, b in names.items() if a not in shared_rows})
     ins = dict(
         picks=(deal_picks, SM),
         blocks_a=(blocks_a, HB),
@@ -1265,17 +1295,23 @@
         gains=((2, 4, 8, 128), F32, VM),
         gates=((2,) + gate_rows.shape[1:], F32, VM),
         q0_o=hbm((1, width, 3 * size)),
+        q1_o=hbm((1, width, 3 * size)),
+        dy=((micros, own, width), BF16, VM),
+        stage_o=hbm(stage_dims),
     )
     scratch.update(
         stage=vm(stage_dims),
+        stage_c=vm(stage_dims),
         psend=pltpu.SemaphoreType.DMA((groups + 11,)),
         precv=pltpu.SemaphoreType.DMA((groups + 11,)),
-        sems=pltpu.SemaphoreType.DMA((48,)),
+        sems=pltpu.SemaphoreType.DMA((80,)),
     )
     for side in sides1:
         side.declare(ins, outs, scratch, groups)
-    swap1.declare(scratch)
-    f0 = launch("forward_0", 0, first_body, ins, outs, scratch)
+    for swap in (swap1, swap_y, swap_c):
+        swap.declare(scratch)
+    f0 = launch("forward", 0, first_body, ins, outs, scratch)
+    f1 = SimpleNamespace(**{**vars(f0), **vars(view_of(f0, "L1_"))})
 
     smalls = dict(
         line=(f0.line, VM), gains=(f0.gains, VM), gates=(f0.gates, VM),
@@ -1284,66 +1320,6 @@
 
     def small_of(k):
         return SimpleNamespace(line=k.line, gains=k.gains, gates=k.gates, starts=k.starts)
-
-    wo1 = Gather("wo_", f0.shards_a, o_dims, groups, 1, lambda k, row: o_of(k.wo_src, 1), "scratch")
-    gate1, up1, down1 = (one_b(t, 1, i, f0.shards_b) for i, t in enumerate(("gate_", "up_", "down_")))
-    cot = Gather("cot_", cotangent_b, by_block, groups, 1, lanes_of_core("cot_src"), "scratch")
-    sides2 = [wo1, gate1, up1, down1, cot]
-    swap_y, swap_c = Swap("swapy_"), Swap("swapc_")
-
-    def second_body(k):
-        row = rows_of(k, "a_")
-        loc = Local(k.sems)
-        loads = [loc.start(k.q_h, k.wq)]
-        gain = gain_row(k, cfg, 1, 0)
-        for m in range(micros):
-            norm_to(k.a_full, gain, k.x[m].astype(F32), row.span(m, row.s, row.r))
-        greet_all(row)
-        for side in sides2:
-            side.bind(k, row, groups)
-        ag_begin(row, k.a_full)
-        for side in (wo1, gate1, up1):
-            side.start()
-        swap_y.start(k, row, own, size, k.x, k.stage_o, False)
-
-        def deal_cot():
-            cot.finish()
-            for m in range(micros):
-                blocks_from(k.cot_dst, k.picks, k.stage, m)
-            swap_c.start(k, row, own, size, k.stage, k.dy, True)
-
-        plan = place(
-            PLACES["second"],
-            [
-                wo1.step, gate1.step, wo1.step, up1.step, down1.start, gate1.step, up1.step, down1.step,
-                down1.step, cot.start, cot.step, cot.step, deal_cot,
-            ],
-            [
-                (A + 20, wo1.finish), (F, gate1.finish), (F, up1.finish), (F + 10, down1.finish),
-            ],
-        )
-        row_f = forward_layer(k, 1, k.x, k.wq, loc, loads, plan, row, small_of(k))
-        for side in sides2:
-            side.finish()
-        swap_y.wait()
-        swap_c.wait()
-        row.finish()
-        row_f.finish()
-        for side in sides2 + [swap_y, swap_c]:
-            side.drain()
-        loc.finish()
-
-    outs, scratch = forward_names(1)
-    ins = dict(x=(f0.y, VM), q_h=(f0.q1_dst, HB), picks=(deal_picks, SM), **smalls)
-    outs.update(dy=((micros, own, width), BF16, VM), stage_o=hbm(stage_dims))
-    scratch.update(
-        stage=vm(stage_dims), wq=vm((1, width, 3 * size)), sems=pltpu.SemaphoreType.DMA((48,))
-    )
-    for side in sides2:
-        side.declare(ins, outs, scratch, groups)
-    swap_y.declare(scratch)
-    swap_c.declare(scratch)
-    f1 = launch("forward_1", 1, second_body, ins, outs, scratch)
 
     def backward_names(kept, dy, x, wq):
         ins = dict(
@@ -1456,7 +1432,7 @@
             side.drain()
         loc.finish()
 
-    ins, scratch = backward_names(f1, f1.dy, f0.y, f0.q1_dst)
+    ins, scratch = backward_names(f1, f1.dy, f0.y, f0.q1_o)
     ins["y"] = (f1.y, VM)
     small_outs = dict(
         dgain=((2, width), F32, VM),

time: 442 us -> 432 us (0.977)
  Pallas kernels: 409 us -> 400 us
    pallas_call x4 -> x3, Pallas kernels: 409 us -> 400 us  [launch(): pl.pallas_call(kernel, out_shape=tuple((jax.ShapeDtypeStruct(d, t) for d,...]
where the time goes in v5:
time: 432 us; the launch traced here: 427 us
  Pallas kernels  400 us (93%)
  local copies, waits for them, and re-layouts  14.6 us (3%)
  other arithmetic  10.5 us (2%)
    pallas_call x3, Pallas kernels, launch(): pl.pallas_call(kernel, out_shape=tuple((jax.ShapeDtypeStruct(d, t) for d,...  400 us
  transfers between devices with their start and end apart: 1, of which 0 were waited for; matrix products, arithmetic and copies ran while one was open for 2% of the time, Pallas kernels for 0%

profile of v5, /device:TPU:0, one launch (start us, length us, event | category | flops | bytes accessed | tf_op | source)
XLA Modules:
  0.0 426.8 jit_solution(18038514913180625704)
XLA Ops:
  0.6 0.0 copy-start.3
  0.7 0.0 copy-start.4
  0.7 0.7 maximum_convert_fusion.7
  1.4 0.2 dynamic_update_slice.3
  1.6 0.7 copy.70
  2.3 0.1 reshape.285
  2.4 0.9 reduce_window_sum.11
  3.2 0.7 sub.6
  3.9 0.1 fusion.1
  4.0 0.1 select_n.52
  4.1 0.1 reshape.287
  4.2 1.2 copy.65
  5.4 0.0 copy-start.5
  5.4 0.0 copy-start.6
  5.4 1.2 copy.66
  6.7 0.0 copy-start.7
  6.7 0.0 copy-done.3
  6.7 0.0 copy-start.9
  6.7 0.0 copy-start.10
  6.7 0.0 copy-start.11
  6.7 0.0 copy-start.12
  6.7 0.2 copy.67
  7.0 0.1 copy.58
  7.1 0.1 copy.59
  7.2 0.1 copy.60
  7.3 0.1 copy.61
  7.4 0.0 copy-done.6
  7.5 0.1 copy.62
  7.6 0.1 copy.63
  7.7 0.1 copy.64
  7.9 0.6 pad_multiply_fusion.refs_4_
  8.5 0.0 copy-done.10
  8.5 0.6 constant_dynamic-slice_fusion.1.refs_0_
  9.1 0.8 select_reduce_fusion.refs_24_
  9.9 1.3 pad_maximum_fusion.refs_2_
  11.2 0.6 select_maximum_fusion.refs_3_
  11.9 0.9 maximum_bitcast_fusion.refs_1_
  12.7 0.6 broadcast_in_dim.22.refs_5_.refs_17_
  13.3 196.4 %forward.1 = (bf16[1152,1024]{1,0:T(8,128)(2,1)}, bf16[1152,384]{1,0:T(8,128)(2,1)}, bf16[18,128,128]{2,1,0:T(8,128)(2,1)}, bf16[1152,128]{1,0:T(8,128)(2,1)}, b...) custom-call(s32[3,6]{1,0:T(4,128)} %constant_dynamic-slice_fusion.1., ...), custom_call_target="tpu_custom_call" | custom-call | tf_op jit(solution)/shard_map/forward/pallas_call | solution.py:932
  209.7 78.2 %backward_1.1 = (bf16[1,1024,512]{2,1,0:T(8,128)(2,1)}, bf16[3,1024,352]{2,1,0:T(8,128)(2,1)}, f32[2,1024]{1,0:T(2,128)}, f32[2,16,128]{2,1,0:T(8,128)}, bf16[3,...) custom-call(bf16[3,48,1024]{2,1,0:T(8,128)(2,1)} %get-tuple-element., ...), custom_call_target="tpu_custom_call" | custom-call | tf_op jit(solution)/shard_map/backward_1/pallas_call | solution.py:932
  287.9 125.3 %backward_0.1 = (bf16[3,384,256]{2,1,0:T(8,128)(2,1)}, bf16[3,384,256]{2,1,0:T(8,128)(2,1)}, bf16[2,1,256,512]{3,2,1,0:T(8,128)(2,1)}, bf16[2,3,256,352]{3,2,1,0...) custom-call(bf16[3,48,1024]{2,1,0:T(8,128)(2,1)} %get-tuple-element.79.refs_0_, ...), custom_call_target="tpu_custom_call" | custom-call | tf_op jit(solution)/shard_map/backward_0/pallas_call | solution.py:932
  413.2 0.7 dynamic-slice_bitcast_fusion
  413.9 0.4 collective-permute-start
  414.3 1.5 slice_bitcast_fusion.1
  415.8 0.0 copy-done.2
  415.8 0.1 slice_bitcast_fusion.7
  415.9 0.1 constant_dynamic-slice_fusion
  416.0 0.5 slice_bitcast_fusion.8
  416.5 0.1 maximum_convert_fusion.2
  416.7 0.1 maximum_convert_fusion.1
  416.8 0.1 maximum_convert_fusion
  417.0 0.7 maximum_convert_fusion.5
  417.7 0.7 maximum_convert_fusion.4
  418.5 0.7 maximum_convert_fusion.3
  419.2 1.1 copy.76
  420.3 1.1 copy.75
  421.4 1.1 copy.74
  422.5 0.8 copy.73
  423.3 0.0 collective-permute-done
  423.4 0.7 bitcast_select_fusion
  424.1 0.6 pad_maximum_fusion.1
  424.7 0.8 copy.80
  425.5 0.0 copy-done
  425.5 0.8 copy.81
  (23 shorter events, 0.1 us)
Async XLA Ops:
  0.6 6.0 %copy-start.3 = (bf16[1,704,256]{2,1,0:T(8,128)(2,1)S(1)}, bf16[1,704,256]{2,1,0:T(8,128)(2,1)}, u32[]{:S(2)}) copy-start(bf16[1,704,256]{2,1,0:T(8,128)(2,1)} %param.33) | copy-start | bytes 1081348
  0.7 6.3 %copy-start.4 = (bf16[1,256,256]{2,1,0:T(8,128)(2,1)S(1)}, bf16[1,256,256]{2,1,0:T(8,128)(2,1)}, u32[]{:S(2)}) copy-start(bf16[1,256,256]{2,1,0:T(8,128)(2,1)} %param.24) | copy-start | bytes 393220
  5.4 1.8 copy-start.5
  5.4 2.0 copy-start.6
  6.7 1.0 copy-start.7
  6.7 1.1 copy-start.9
  6.7 1.8 copy-start.10
  6.7 3.2 copy-start.11
  6.7 3.2 copy-start.12
  413.9 9.4 %collective-permute-start = (f32[2,4,128]{2,1,0:T(4,128)S(1)}, f32[2,4,128]{2,1,0:T(4,128)S(1)}, u32[]{:S(2)}, u32[]{:S(2)}) collective-permute-start(f32[2,4,128]{2,1,0:T(4,128)S(1)} %dynamic-slice_bitcast_fusion), channel_id=1, source_target_pairs={{0,16},{16,0},{1,17},{17,1},{2,18},{18,2},{3,19},{19,3},{4,20},{20... | collective-permute-start | bytes 12296 | tf_op jit(solution)/shard_map/ppermute | solution.py:1664
  414.3 1.5 copy-start.2
  414.3 1.6 copy-start.8
  421.4 3.3 copy-start.1
  422.5 3.0 copy-start

commit v6 on v5

--- a/solution.py
+++ b/solution.py
@@ -961,7 +961,6 @@
     total_blocks = block_order.shape[1]
     positions = jnp.arange(total_blocks, dtype=jnp.int32)
     my_blocks = col * blocks + jnp.arange(blocks, dtype=jnp.int32)
-    deal_picks = lax.dynamic_slice_in_dim(block_order, col * blocks, blocks, 1)
     matches = (block_order[:, :, None] == my_blocks[None, None, :]).astype(jnp.int32)
     back_picks = jnp.sum(matches * positions[None, :, None], axis=1)
 
@@ -986,8 +985,10 @@
         axis=0,
     )
     gate_rows = eights(write_gate[0].transpose(2, 0, 1).reshape(2, -1, 128)) / BLOCK
-    ends = jnp.cumsum(lengths, axis=1)
-    is_start = jnp.any(positions[None, :, None] == (ends - lengths)[:, None, :], axis=2)
+    sequences = jnp.arange(lengths.shape[1])
+    earlier = sequences[None, :] < sequences[:, None]
+    firsts = jnp.sum(jnp.where(earlier[None], lengths[:, None, :], 0), axis=2)
+    is_start = jnp.any(positions[None, :, None] == firsts[:, None, :], axis=2)
     starts = jnp.where(is_start, 0.0, 1.0).reshape(micros, groups, blocks).transpose(1, 0, 2)
     starts = jnp.broadcast_to(lanes(starts.reshape(groups, -1))[:, None], (groups, 8, 128))
 
@@ -1086,9 +1087,9 @@
 
         return push
 
-    def blocks_from(buf, picks, stage, m, lead=()):
+    def blocks_from(buf, picks, stage, m, group):
         for b in range(blocks):
-            stage[lead + (m, pl.ds(b * BLOCK, BLOCK))] = buf[lead + (m, picks[m, b])]
+            stage[m, pl.ds(b * BLOCK, BLOCK), :] = buf[m, picks[m, group * blocks + b]]
 
     def forward_names(l):
         outs = dict(
@@ -1214,7 +1215,7 @@
         wo0.step()
         deal.finish()
         for m in range(micros):
-            blocks_from(k.deal_dst, k.picks, k.stage, m)
+            blocks_from(k.deal_dst, k.picks, k.stage, m, row.c)
         swap1.start(k, row, own, size, k.stage, k.x, True)
         q0.finish()
         wo0.step()
@@ -1229,7 +1230,7 @@
         def deal_cot():
             cot.finish()
             for m in range(micros):
-                blocks_from(k.cot_dst, k.picks, k.stage_c, m)
+                blocks_from(k.cot_dst, k.picks, k.stage_c, m, row.c)
             swap_c.start(k, row, own, size, k.stage_c, k.dy, True)
 
         plan = place(
@@ -1280,7 +1281,7 @@
     for names, into in zip(forward_names(1), (outs, scratch)):
         into.update({"L1_" + a: b for a, b in names.items() if a not in shared_rows})
     ins = dict(
-        picks=(deal_picks, SM),
+        picks=(block_order, SM),
         blocks_a=(blocks_a, HB),
         blocks_b=(blocks_b, HB),
         packed=(packed, VM),
@@ -1568,6 +1569,14 @@
         for i in range(1, groups):
             total = total + k.small_box[i]
         k.small_sum[...] = total
+
+        def persist_rows(layer):
+            at = pl.multiple_of(gain_rows + layer * 2 * persist, 8)
+            return k.small_sum.at[pl.ds(at, 2 * persist), :]
+
+        out = k.persist_o.at[row.s]
+        moved.append(push(persist_rows(1 - row.s), out, groups + 12, row.sib))
+        kept_here.append(loc.start(persist_rows(row.s), out))
         gains = []
         for i, ps, pr in others(row):
             src = k.small_sum.at[pl.ds(0, gain_rows), :]
@@ -1587,7 +1596,6 @@
         for i in range(1, 8):
             total = total + k.gain_box[i]
         k.gain_o[...] = total
-        k.persist_o[...] = k.small_sum[gain_rows:, :]
         for copy in moved:
             copy.wait()
         for copy in pushes + gains:
@@ -1616,7 +1624,7 @@
         grad_a=((2,) + ta0.dims, BF16, VM),
         grad_b=((2, 3) + tu0.dims[1:], BF16, VM),
         gain_o=((gain_rows, 128), F32, VM),
-        persist_o=((4 * persist, 128), F32, VM),
+        persist_o=((2, 2 * persist, 128), F32, VM),
     )
     scratch.update(
         stage=vm(stage_dims),
@@ -1634,8 +1642,8 @@
         dgain=vm((2, width), F32),
         dpersist=vm((2, persist, size), F32),
         dx=vm((micros, own, width)),
-        psend=pltpu.SemaphoreType.DMA((groups + 12,)),
-        precv=pltpu.SemaphoreType.DMA((groups + 12,)),
+        psend=pltpu.SemaphoreType.DMA((groups + 13,)),
+        precv=pltpu.SemaphoreType.DMA((groups + 13,)),
     )
     for side in sides4:
         side.declare(ins, outs, scratch, groups)
@@ -1660,13 +1668,7 @@
     )
     persist_sum = closed.persist_o.reshape(2, 2, persist, size)
     persist_sum = lax.dynamic_slice_in_dim(persist_sum, col * per, per, 2)
-    mine_p = lax.dynamic_index_in_dim(persist_sum, sec, 0, False)
-    got_p = lax.ppermute(
-        lax.dynamic_index_in_dim(persist_sum, 1 - sec, 0, False), "section", [(0, 1), (1, 0)]
-    )
-    grad_persist = jnp.concatenate(
-        [jnp.where(sec == 0, mine_p, got_p), jnp.where(sec == 0, got_p, mine_p)], axis=2
-    )
+    grad_persist = jnp.concatenate([persist_sum[0], persist_sum[1]], axis=2)
     return (
         closed.acts_o[None],
         closed.grads_o[None],

time: 432 us -> 430 us (level)
  transfers between devices with their start and end apart: 1 -> 0, of which waited for: 0 -> 0; matrix products, arithmetic and copies ran while one was open for 2% -> 0% of each run, Pallas kernels for 0% -> 0%
where the time goes in v6:
time: 430 us; the launch traced here: 424 us
  Pallas kernels  400 us (93%)
  local copies, waits for them, and re-layouts  13.1 us (3%)
  other arithmetic  9.75 us (2%)
    pallas_call x3, Pallas kernels, launch(): pl.pallas_call(kernel, out_shape=tuple((jax.ShapeDtypeStruct(d, t) for d,...  400 us

profile of v6, /device:TPU:0, one launch (start us, length us, event | category | flops | bytes accessed | tf_op | source)
XLA Modules:
  0.0 423.9 jit_solution(14406664457143567394)
XLA Ops:
  0.6 0.0 copy-start.3
  0.7 0.0 copy-start.4
  0.7 0.7 maximum_convert_fusion.7
  1.4 0.2 dynamic_update_slice.3
  1.6 0.7 bitcast_convert_fusion
  2.3 0.7 copy.70
  3.0 0.1 reshape.298
  3.1 0.6 select_maximum_fusion.refs_3_
  3.7 0.8 select_reduce_fusion.1
  4.5 0.1 fusion.1
  4.6 0.1 select_n.32
  4.7 0.1 reshape.300
  4.8 0.6 broadcast_in_dim.69.refs_5_.refs_17_
  5.4 1.2 copy.65
  6.6 0.0 copy-done.3
  6.6 0.2 copy.66
  6.9 0.0 copy-done.4
  6.9 0.2 copy.67
  7.1 0.0 copy-start.5
  7.1 0.0 copy-start.6
  7.1 0.0 copy-start.7
  7.1 1.3 pad_maximum_fusion.refs_2_
  8.4 0.0 copy-done.5
  8.4 0.1 copy.58
  8.5 0.1 copy.59
  8.6 0.0 copy-done.6
  8.7 0.0 copy-start.10
  8.7 0.1 copy.60
  8.8 0.1 copy.61
  8.9 0.0 copy-done.7
  8.9 0.1 copy.62
  9.0 0.1 copy.63
  9.1 0.2 copy-done.8
  9.3 0.1 copy.64
  9.4 0.9 maximum_bitcast_fusion.refs_1_
  10.3 0.0 copy-done.10
  10.3 0.6 pad_multiply_fusion.refs_4_
  10.9 196.3 %forward.1 = (bf16[1152,1024]{1,0:T(8,128)(2,1)}, bf16[1152,384]{1,0:T(8,128)(2,1)}, bf16[18,128,128]{2,1,0:T(8,128)(2,1)}, bf16[1152,128]{1,0:T(8,128)(2,1)}, b...) custom-call(s32[3,24]{1,0:T(4,128)} %refs_0_.1, ...), custom_call_target="tpu_custom_call" | custom-call | tf_op jit(solution)/shard_map/forward/pallas_call | solution.py:932
  207.2 0.0 copy-start.11
  207.2 78.0 %backward_1.1 = (bf16[1,1024,512]{2,1,0:T(8,128)(2,1)}, bf16[3,1024,352]{2,1,0:T(8,128)(2,1)}, f32[2,1024]{1,0:T(2,128)}, f32[2,16,128]{2,1,0:T(8,128)}, bf16[3,...) custom-call(bf16[3,48,1024]{2,1,0:T(8,128)(2,1)} %get-tuple-element., ...), custom_call_target="tpu_custom_call" | custom-call | tf_op jit(solution)/shard_map/backward_1/pallas_call | solution.py:932
  285.3 0.0 copy-done.11
  285.3 0.8 select_reduce_fusion.refs_24_
  286.1 125.4 %backward_0.1 = (bf16[3,384,256]{2,1,0:T(8,128)(2,1)}, bf16[3,384,256]{2,1,0:T(8,128)(2,1)}, bf16[2,1,256,512]{3,2,1,0:T(8,128)(2,1)}, bf16[2,3,256,352]{3,2,1,0...) custom-call(bf16[3,48,1024]{2,1,0:T(8,128)(2,1)} %get-tuple-element.79.refs_0_, ...), custom_call_target="tpu_custom_call" | custom-call | tf_op jit(solution)/shard_map/backward_0/pallas_call | solution.py:932
  411.5 1.5 slice_bitcast_fusion.1
  412.9 0.1 maximum_convert_fusion.2
  413.1 1.1 copy.76
  414.2 0.1 maximum_convert_fusion.1
  414.3 1.1 copy.75
  415.5 0.1 maximum_convert_fusion
  415.6 1.1 copy.74
  416.7 0.0 copy-done.2
  416.7 0.1 slice_bitcast_fusion.7
  416.8 0.0 copy-start.9
  416.9 0.8 copy.73
  417.7 0.7 dynamic-slice_bitcast_fusion
  418.4 0.6 pad_maximum_fusion.1
  419.0 0.7 maximum_convert_fusion.5
  419.7 0.7 maximum_convert_fusion.4
  420.5 0.7 maximum_convert_fusion.3
  421.2 0.1 constant_dynamic-slice_fusion
  421.3 0.5 slice_bitcast_fusion.8
  421.8 0.8 copy.80
  422.6 0.0 copy-done
  422.6 0.8 copy.81
  (17 shorter events, 0.1 us)
Async XLA Ops:
  0.6 6.0 %copy-start.3 = (bf16[1,256,704]{1,2,0:T(8,128)(2,1)S(1)}, bf16[1,256,704]{1,2,0:T(8,128)(2,1)}, u32[]{:S(2)}) copy-start(bf16[1,256,704]{1,2,0:T(8,128)(2,1)} %param.32) | copy-start | bytes 1081348
  0.7 6.2 %copy-start.4 = (bf16[1,704,256]{2,1,0:T(8,128)(2,1)S(1)}, bf16[1,704,256]{2,1,0:T(8,128)(2,1)}, u32[]{:S(2)}) copy-start(bf16[1,704,256]{2,1,0:T(8,128)(2,1)} %param.33) | copy-start | bytes 1081348
  7.1 1.3 copy-start.5
  7.1 1.5 copy-start.6
  7.1 1.8 copy-start.7
  8.4 0.9 copy-start.8
  8.7 1.6 copy-start.10
  207.2 78.0 %copy-start.11 = (s32[3,24]{1,0:T(4,128)S(1)}, s32[3,24]{1,0:T(4,128)}, u32[]{:S(2)}) copy-start(s32[3,24]{1,0:T(4,128)} %refs_0_.1) | copy-start | bytes 868
  415.5 1.3 copy-start.2
  416.8 4.4 %copy-start.9 = (f32[32,128]{1,0:T(8,128)S(1)}, f32[32,128]{1,0:T(8,128)}, u32[]{:S(2)}) copy-start(f32[32,128]{1,0:T(8,128)} %get-tuple-element.103) | copy-start | bytes 49156
  416.8 5.0 %copy-start.1 = (bf16[3,384,256]{2,1,0:T(8,128)(2,1)S(1)}, bf16[3,384,256]{2,1,0:T(8,128)(2,1)}, u32[]{:S(2)}) copy-start(bf16[3,384,256]{2,1,0:T(8,128)(2,1)} %get-tuple-element.101) | copy-start | bytes 1769476
  419.0 3.6 copy-start

commit v7 on v6

--- a/solution.py
+++ b/solution.py
@@ -1153,7 +1153,20 @@
 
     tokens_b = tokens.reshape(micros, blocks, BLOCK, features)
     cotangent_b = cotangent.reshape(micros, blocks, BLOCK, features)
-    deal = Gather("deal_", tokens_b, by_block, groups, 1, lanes_of_core("deal_src"), "scratch")
+
+    def tokens_of(m):
+        def view(k, row):
+            mine = pl.ds(pl.multiple_of(row.s * size, 128), size)
+            return k.deal0_src.at[m, :, :, mine]
+
+        return view
+
+    deals = [
+        Gather(
+            f"deal{m}_", tokens_b if m == 0 else None, by_block[1:], groups, 0, tokens_of(m), "scratch"
+        )
+        for m in range(micros)
+    ]
     q0 = Gather("q0_", None, q_dims, groups, 1, lambda k, row: q_of(k.shards_a, 0), "scratch")
     wo0 = Gather("wo_", None, o_dims, groups, 1, lambda k, row: o_of(k.shards_a, 0), "scratch")
     gate0, up0, down0 = (one_b(t, 0, i) for i, t in enumerate(("gate_", "up_", "down_")))
@@ -1163,8 +1176,9 @@
         one_b(t, 1, i) for i, t in enumerate(("L1_gate_", "L1_up_", "L1_down_"))
     )
     cot = Gather("cot_", cotangent_b, by_block, groups, 1, lanes_of_core("cot_src"), "scratch")
-    sides1 = [deal, q0, wo0, gate0, up0, down0, q1, wo1, gate1, up1, down1, cot]
-    swap1, swap_y, swap_c = Swap("swap_"), Swap("swapy_"), Swap("swapc_")
+    sides1 = [*deals, q0, wo0, gate0, up0, down0, q1, wo1, gate1, up1, down1, cot]
+    swaps1 = [Swap(f"swap{m}_") for m in range(micros)]
+    swap_y, swap_c = Swap("swapy_"), Swap("swapc_")
 
     def first_body(k):
         row = rows_of(k, "a_")
@@ -1177,7 +1191,8 @@
         for i, (src, dst) in enumerate(((k.blocks_a, k.shards_a), (k.blocks_b, k.shards_b))):
             keeps_here.append(loc.start(src.at[row.s], dst.at[row.s]))
             crossing.append(push(src.at[1 - row.s], dst.at[row.s], groups + 9 + i, row.sib))
-        deal.start()
+        for side in deals[:2]:
+            side.start()
         k.line[row.s, row.c] = k.packed[...]
         k.gates[row.s] = k.gate_rows[row.s]
         small = [
@@ -1193,7 +1208,10 @@
         crossing[0].wait_recv()
         loc.wait(keeps_here[0])
         q0.start()
-        deal.step()
+        for side in deals[2:]:
+            side.start()
+        for side in deals[:2]:
+            side.step()
         for copy in small:
             copy.wait_recv()
         total = k.line[row.s, 0, 0:8, :]
@@ -1207,25 +1225,33 @@
         crossing[1].wait_recv()
         loc.wait(keeps_here[1])
         q0.step()
+        for side in deals[2:] + deals[:2]:
+            side.step()
+        q0.step()
+        for side in deals[2:]:
+            side.step()
         wo0.start()
-        deal.step()
-        q0.step()
         gate0.start()
         up0.start()
-        wo0.step()
-        deal.finish()
         for m in range(micros):
-            blocks_from(k.deal_dst, k.picks, k.stage, m, row.c)
-        swap1.start(k, row, own, size, k.stage, k.x, True)
-        q0.finish()
-        wo0.step()
+            deals[m].finish()
+            buf = getattr(k, f"deal{m}_dst")
+            for b in range(blocks):
+                where = pl.ds(b * BLOCK, BLOCK)
+                k.stage[m, where, :] = buf[k.picks[m, row.c * blocks + b]]
+            one = pl.ds(m, 1)
+            swaps1[m].start(k, row, own, size, k.stage.at[one], k.x.at[one], True)
         for copy in late:
             copy.wait_recv()
         gain = gain_row(k, cfg, 0, 0)
-        swap1.wait()
         for m in range(micros):
+            swaps1[m].wait()
             norm_to(k.a_full, gain, k.x[m].astype(F32), row.span(m, row.s, row.r))
-        ag_begin(row, k.a_full)
+            if m < 2:
+                row.ag_start(k.a_full, m)
+        wo0.step()
+        wo0.step()
+        q0.finish()
         loc.start(k.q0_dst, k.q0_o)
         def deal_cot():
             cot.finish()
@@ -1273,7 +1299,7 @@
         swap_c.wait()
         for copy in crossing + small + late:
             copy.wait_send()
-        for side in sides1 + [swap1, swap_y, swap_c]:
+        for side in sides1 + swaps1 + [swap_y, swap_c]:
             side.drain()
         loc.finish()
 
@@ -1309,7 +1335,7 @@
     )
     for side in sides1:
         side.declare(ins, outs, scratch, groups)
-    for swap in (swap1, swap_y, swap_c):
+    for swap in (*swaps1, swap_y, swap_c):
         swap.declare(scratch)
     f0 = launch("forward", 0, first_body, ins, outs, scratch)
     f1 = SimpleNamespace(**{**vars(f0), **vars(view_of(f0, "L1_"))})

time: 430 us -> 428 us (level)
  no operation moved by 1% of the time
where the time goes in v7:
time: 428 us; the launch traced here: 422 us
  Pallas kernels  398 us (93%)
  local copies, waits for them, and re-layouts  13.1 us (3%)
  other arithmetic  9.75 us (2%)
    pallas_call x3, Pallas kernels, launch(): pl.pallas_call(kernel, out_shape=tuple((jax.ShapeDtypeStruct(d, t) for d,...  398 us

profile of v7, /device:TPU:0, one launch (start us, length us, event | category | flops | bytes accessed | tf_op | source)
XLA Modules:
  0.0 422.5 jit_solution(15582043767162327359)
XLA Ops:
  0.6 0.0 copy-start.3
  0.7 0.0 copy-start.4
  0.7 0.7 maximum_convert_fusion.7
  1.4 0.2 dynamic_update_slice.3
  1.6 0.7 bitcast_convert_fusion
  2.3 0.7 copy.70
  3.0 0.1 reshape.298
  3.1 0.6 select_maximum_fusion.refs_3_
  3.7 0.8 select_reduce_fusion.1
  4.5 0.1 fusion.1
  4.6 0.1 select_n.32
  4.7 0.1 reshape.300
  4.8 0.6 broadcast_in_dim.69.refs_5_.refs_17_
  5.4 1.2 copy.65
  6.6 0.0 copy-done.3
  6.6 0.2 copy.66
  6.9 0.0 copy-done.4
  6.9 0.2 copy.67
  7.1 0.0 copy-start.5
  7.1 0.0 copy-start.6
  7.1 0.0 copy-start.7
  7.1 1.3 pad_maximum_fusion.refs_2_
  8.4 0.0 copy-done.5
  8.4 0.1 copy.58
  8.5 0.1 copy.59
  8.6 0.0 copy-done.6
  8.7 0.0 copy-start.10
  8.7 0.1 copy.60
  8.8 0.1 copy.61
  8.9 0.0 copy-done.7
  8.9 0.1 copy.62
  9.0 0.1 copy.63
  9.1 0.2 copy-done.8
  9.3 0.1 copy.64
  9.4 0.9 maximum_bitcast_fusion.refs_1_
  10.3 0.0 copy-done.10
  10.3 0.6 pad_multiply_fusion.refs_4_
  10.9 194.2 %forward.1 = (bf16[1152,1024]{1,0:T(8,128)(2,1)}, bf16[1152,384]{1,0:T(8,128)(2,1)}, bf16[18,128,128]{2,1,0:T(8,128)(2,1)}, bf16[1152,128]{1,0:T(8,128)(2,1)}, b...) custom-call(s32[3,24]{1,0:T(4,128)} %refs_0_.1, ...), custom_call_target="tpu_custom_call" | custom-call | tf_op jit(solution)/shard_map/forward/pallas_call | solution.py:932
  205.2 0.0 copy-start.11
  205.2 78.9 %backward_1.1 = (bf16[1,1024,512]{2,1,0:T(8,128)(2,1)}, bf16[3,1024,352]{2,1,0:T(8,128)(2,1)}, f32[2,1024]{1,0:T(2,128)}, f32[2,16,128]{2,1,0:T(8,128)}, bf16[3,...) custom-call(bf16[3,48,1024]{2,1,0:T(8,128)(2,1)} %get-tuple-element., ...), custom_call_target="tpu_custom_call" | custom-call | tf_op jit(solution)/shard_map/backward_1/pallas_call | solution.py:932
  284.1 0.0 copy-done.11
  284.1 0.8 select_reduce_fusion.refs_24_
  284.9 125.1 %backward_0.1 = (bf16[3,384,256]{2,1,0:T(8,128)(2,1)}, bf16[3,384,256]{2,1,0:T(8,128)(2,1)}, bf16[2,1,256,512]{3,2,1,0:T(8,128)(2,1)}, bf16[2,3,256,352]{3,2,1,0...) custom-call(bf16[3,48,1024]{2,1,0:T(8,128)(2,1)} %get-tuple-element.79.refs_0_, ...), custom_call_target="tpu_custom_call" | custom-call | tf_op jit(solution)/shard_map/backward_0/pallas_call | solution.py:932
  410.1 1.5 slice_bitcast_fusion.1
  411.5 0.1 maximum_convert_fusion.2
  411.7 1.1 copy.76
  412.8 0.1 maximum_convert_fusion.1
  412.9 1.1 copy.75
  414.0 0.1 maximum_convert_fusion
  414.2 1.1 copy.74
  415.3 0.0 copy-done.2
  415.3 0.1 slice_bitcast_fusion.7
  415.4 0.0 copy-start.9
  415.4 0.0 copy-start.1
  415.4 0.8 copy.73
  416.3 0.7 dynamic-slice_bitcast_fusion
  417.0 0.6 pad_maximum_fusion.1
  417.6 0.7 maximum_convert_fusion.5
  418.3 0.7 maximum_convert_fusion.4
  419.1 0.7 maximum_convert_fusion.3
  419.8 0.1 constant_dynamic-slice_fusion
  419.9 0.5 slice_bitcast_fusion.8
  420.4 0.8 copy.80
  421.2 0.8 copy.81
  (17 shorter events, 0.1 us)
Async XLA Ops:
  0.6 6.0 %copy-start.3 = (bf16[1,256,704]{1,2,0:T(8,128)(2,1)S(1)}, bf16[1,256,704]{1,2,0:T(8,128)(2,1)}, u32[]{:S(2)}) copy-start(bf16[1,256,704]{1,2,0:T(8,128)(2,1)} %param.32) | copy-start | bytes 1081348
  0.7 6.2 %copy-start.4 = (bf16[1,704,256]{2,1,0:T(8,128)(2,1)S(1)}, bf16[1,704,256]{2,1,0:T(8,128)(2,1)}, u32[]{:S(2)}) copy-start(bf16[1,704,256]{2,1,0:T(8,128)(2,1)} %param.33) | copy-start | bytes 1081348
  7.1 1.3 copy-start.5
  7.1 1.5 copy-start.6
  7.1 1.8 copy-start.7
  8.4 0.9 copy-start.8
  8.7 1.6 copy-start.10
  205.2 78.9 %copy-start.11 = (s32[3,24]{1,0:T(4,128)S(1)}, s32[3,24]{1,0:T(4,128)}, u32[]{:S(2)}) copy-start(s32[3,24]{1,0:T(4,128)} %refs_0_.1) | copy-start | bytes 868
  414.0 1.3 copy-start.2
  415.4 4.4 %copy-start.9 = (f32[32,128]{1,0:T(8,128)S(1)}, f32[32,128]{1,0:T(8,128)}, u32[]{:S(2)}) copy-start(f32[32,128]{1,0:T(8,128)} %get-tuple-element.103) | copy-start | bytes 49156
  415.4 5.0 %copy-start.1 = (bf16[3,384,256]{2,1,0:T(8,128)(2,1)S(1)}, bf16[3,384,256]{2,1,0:T(8,128)(2,1)}, u32[]{:S(2)}) copy-start(bf16[3,384,256]{2,1,0:T(8,128)(2,1)} %get-tuple-element.101) | copy-start | bytes 1769476
  417.6 3.6 copy-start
